TPU v7x, 128 devices: a whole 4x4x4 slice. The times are simulated.
128 devices in a mesh: boot: 4 (over x_hi, core), slab: 32 (over y, x_lo, z).
Axes of the slice: x: 4 (x_hi: 2, x_lo: 2; x = x_hi * 2 + x_lo), y: 4, z: 4, core: 2. Of those that a mesh axis runs over, the one named last changes fastest.
Arguments:
- params: bfloat16 [2, 200, 262144], P(None, None, 'slab'), may hold values from -6 to 6
- predicted: bfloat16 [200, 4096], P(None, 'slab'), may hold values from -6 to 6
- perturbation: bfloat16 [200, 4096], P(None, 'slab'), may hold values from -6 to 6
- observed: bfloat16 [4096], P('slab'), may hold values from -6 to 6
- obs_sd: bfloat16 [4096], P('slab'), may hold values from 0.5 to 2
- members: int32 [16, 200], P('boot'), may hold values from 0 to 199
- block_map: int32 [2048, 64], P('slab'), may hold values from 0 to 4095
Outputs:
- posterior: float32 [2, 200, 262144], P(None, None, 'slab')
Inputs may be any that keep to these rules, and one draw needn't show every extreme that they name: Row r lists the 200 members, with repetition, of resample r. `block_map`: row k lists the 64 data whose gains are kept for cells k * 128 to k * 128 + 127.
All inputs are finite; a program needn't handle non-finite values.
Results may differ from a plain program's by a relative error of at most 0.00065.
Values may be sent and summed in bfloat16 or wider, within the bound.
No kernel may reach another device: no remote copies, remote signals or barrier semaphores. Data moves between devices by JAX's collectives and lax.ppermute only.
A program may use at most 256 MiB of HBM per device.

v0:
```python
from functools import partial
import math

import jax
import jax.numpy as jnp
from jax import lax
from jax.sharding import PartitionSpec as P

NB = 16


screen_floor = 1e-05
highest = lax.Precision.HIGHEST


def centering(members_count):
    return (jnp.eye(members_count, dtype=jnp.float32) - 1.0 / members_count) / math.sqrt(
        members_count - 1
    )


def projector(chosen, center):
    members_count = center.shape[0]
    onehot = (jnp.arange(members_count, dtype=jnp.int32)[:, None] == chosen[None, :]).astype(
        jnp.float32
    )
    return jnp.dot(onehot, center, precision=highest)


def member_map(gram_matrix, proj_matrix):
    members_count = gram_matrix.shape[0]
    inner = jnp.dot(gram_matrix, proj_matrix, precision=highest)
    system = jnp.eye(members_count, dtype=jnp.float32) + jnp.dot(
        proj_matrix.T, inner, precision=highest
    )
    factor = jnp.linalg.cholesky(system)
    solved = jax.scipy.linalg.cho_solve((factor, True), proj_matrix.T)
    return jnp.dot(proj_matrix, solved, precision=highest)


def resample_map(gram_matrix, center, chosen):
    return member_map(gram_matrix, projector(chosen, center))


def all_maps(gram_matrix, center, members):
    boot_maps = jax.vmap(partial(resample_map, gram_matrix, center))(members)
    return jnp.concatenate([member_map(gram_matrix, center)[None], boot_maps], axis=0)


def prepare(predicted, perturbation, observed, obs_sd):
    noise = obs_sd.astype(jnp.float32)
    ensemble = predicted.astype(jnp.float32)
    scaled = ensemble / noise
    weighted = scaled / noise
    innovation = (
        observed.astype(jnp.float32) + noise * perturbation.astype(jnp.float32) - ensemble
    ).astype(jnp.bfloat16)
    return (scaled, weighted, innovation)


def gain_terms(params_part, columns, map_part):
    members_count = params_part.shape[1]
    block_count = map_part.shape[0]
    blocks = params_part.reshape(2, members_count, block_count, params_part.shape[2] // block_count)
    selected = jnp.take(columns, map_part, axis=2)
    gains = jnp.einsum("pmkc,bmkj->bpjkc", blocks, selected, preferred_element_type=jnp.float32)
    full_gain = gains[0]
    local_spread = jnp.sum(jnp.square(gains[1:] - full_gain[None]), axis=0)
    return (full_gain, local_spread)


def screen_gain(full_gain, spread):
    squared = full_gain * full_gain
    return (squared / (squared + spread + screen_floor) * full_gain).astype(jnp.bfloat16)


def on_device(params, predicted, perturbation, observed, obs_sd, members, block_map):
    members_count = params.shape[1]
    cells_dev = params.shape[2]
    center = centering(members_count)
    whole = (
        lax.all_gather(predicted, "slab", axis=1, tiled=True),
        lax.all_gather(perturbation, "slab", axis=1, tiled=True),
        lax.all_gather(observed, "slab", axis=0, tiled=True),
        lax.all_gather(obs_sd, "slab", axis=0, tiled=True),
    )
    scaled, weighted, innovation = prepare(whole[0], whole[1], whole[2], whole[3])
    gram_matrix = jnp.dot(scaled, scaled.T, precision=highest)
    maps = all_maps(gram_matrix, center, members)
    columns = jnp.einsum("bmn,nd->bmd", maps, weighted, precision=highest).astype(jnp.bfloat16)
    full_gain, local_spread = gain_terms(params, columns, block_map)
    spread = lax.psum(local_spread.astype(jnp.bfloat16), "boot").astype(jnp.float32) / NB
    screened = screen_gain(full_gain, spread)
    chosen_innov = jnp.take(innovation, block_map, axis=1)
    change = jnp.einsum(
        "pjkc,mkj->pmkc", screened, chosen_innov, preferred_element_type=jnp.float32
    )
    return params.astype(jnp.float32) + change.reshape(2, members_count, cells_dev)


def solution(mesh):
    return jax.shard_map(
        on_device,
        mesh=mesh,
        in_specs=(
            P(None, None, "slab"),
            P(None, "slab"),
            P(None, "slab"),
            P("slab"),
            P("slab"),
            P("boot", None),
            P("slab", None),
        ),
        out_specs=P(None, None, "slab"),
        check_vma=False,
    )
```

profile of v0, /device:TPU:0, one launch (start us, length us, event | category | flops | bytes accessed | tf_op | source)
XLA Modules:
  0.0 685.0 jit_solution(17077585996862716999)
XLA Ops:
  6.5 1.5 copy.76
  8.1 1.5 copy.75
  12.4 0.8 compare_select_fusion
  13.1 0.8 compare_and_fusion
  13.9 82.5 %all-gather.1 = bf16[32,1,128]{2,1,0:T(2,128)(2,1)S(1)} all-gather(bf16[1,1,128]{2,1,0:T(2,128)(2,1)} %bitcast.134), channel_id=1, replica_groups=mesh['boot'=4,'slab'=32] {'slab'}, dimensions={0}, use_global_device_ids=true | all-gather | bytes 8448 | tf_op jit(solution)/shard_map/all_gather | solution.py:85
  96.5 1.2 fusion.29
  99.3 4.8 copy.113
  104.1 4.3 bitcast_bitcast_fusion
  108.4 56.2 %all-gather.7.cloned.1.call-done = bf16[200,4096]{0,1:T(8,128)(2,1)} async-done(((bf16[200,128]{0,1:T(8,128)(2,1)}), bf16[200,4096]{0,1:T(8,128)(2,1)}) %all-gather.7.cloned.1.call-update) | async-done | bytes 1638416 | tf_op jit(solution)/shard_map/all_gather | solution.py:82
  164.6 10.1 %fusion.9 = f32[200,200]{1,0:T(8,128)S(1)} fusion(bf16[200,4096]{0,1:T(8,128)(2,1)} %all-gather.7.cloned.1.call-done, f32[4096]{0:T(1024)S(1)} %bitcast.131), kind=kOutput, calls=%fused_computation.18 | convolution fusion | flops 1967718400 | bytes 1814784 | tf_op jit(solution)/shard_map/dot_general | solution.py:88
  175.8 11.9 %cholesky.95 = f32[128,128]{1,0:T(8,128)S(1)} custom-call(f32[128,128]{1,0:T(8,128)S(1)} %cholesky.244), custom_call_target="Cholesky" | custom-call | tf_op jit(solution)/shard_map/jit(cholesky)/cholesky | solution.py:36
  187.8 9.8 %custom-call.38 = f32[1,128,128]{1,2,0:T(8,128)S(1)} custom-call(f32[1,128,128]{2,1,0:T(8,128)S(1)} %get-tuple-element.50), custom_call_target="InvertDiagBlocksLowerTriangular" | custom-call | tf_op jit(solution)/shard_map/jit(cholesky)/cholesky | solution.py:36
  198.1 6.6 cholesky.200
  207.4 20.1 %custom-call.39 = f32[2,128,128]{1,2,0:T(8,128)S(1)} custom-call(f32[2,128,128]{2,1,0:T(8,128)S(1)} %pad_maximum_fusion.1), custom_call_target="InvertDiagBlocksLowerTriangular" | custom-call | tf_op jit(solution)/shard_map/jit(_cho_solve)/triangular_solve | solution.py:37
  228.8 1.0 convolution_subtract_fusion.3
  229.8 0.7 copy.78
  230.5 0.8 fusion.40
  231.4 1.7 fusion.87
  233.4 1.1 fusion.28
  234.5 0.9 copy-done
  235.4 46.9 %custom-call.40 = f32[4,128,128]{2,1,0:T(8,128)S(1)} custom-call(f32[4,128,128]{2,1,0:T(8,128)S(1)} %cholesky.247), custom_call_target="Cholesky" | custom-call | tf_op jit(solution)/shard_map/vmap(jit(cholesky))/cholesky | solution.py:36
  282.3 0.8 select_reduce_fusion
  283.1 39.5 %custom-call.41 = f32[4,1,128,128]{2,3,1,0:T(8,128)S(1)} custom-call(f32[4,1,128,128]{3,2,1,0:T(8,128)S(1)} %get-tuple-element.46), custom_call_target="InvertDiagBlocksLowerTriangular" | custom-call | tf_op jit(solution)/shard_map/vmap(jit(cholesky))/cholesky | solution.py:36
  322.6 1.3 constant_dynamic-update-slice_fusion.1
  323.9 1.3 convolution_subtract_fusion.2
  325.2 26.4 %custom-call.42 = f32[4,72,72]{2,1,0:T(8,128)S(1)} custom-call(f32[4,72,72]{2,1,0:T(8,128)S(1)} %convolution_subtract_fusion.2), custom_call_target="Cholesky" | custom-call | tf_op jit(solution)/shard_map/vmap(jit(cholesky))/cholesky | solution.py:36
  351.7 0.7 select_reduce_fusion.1
  352.7 1.0 select_select_fusion
  353.9 0.8 pad_maximum_fusion
  354.7 79.4 %custom-call.43 = f32[4,2,128,128]{2,3,1,0:T(8,128)S(1)} custom-call(f32[4,2,128,128]{3,2,1,0:T(8,128)} %pad_maximum_fusion), custom_call_target="InvertDiagBlocksLowerTriangular" | custom-call | tf_op jit(solution)/shard_map/vmap(jit(_cho_solve))/triangular_solve | solution.py:37
  434.1 1.1 fusion.30
  435.3 0.9 convolution_subtract_fusion.1
  437.1 0.9 convolution_subtract_fusion
  438.1 1.3 fusion.67
  439.4 1.8 fusion.36
  441.5 0.9 fusion.23
  442.5 17.5 %convolution_convert_fusion = bf16[5,200,4096]{2,1,0:T(8,128)(2,1)} fusion(bf16[200,4096]{0,1:T(8,128)(2,1)} %all-gather.7.cloned.1.call-done, f32[4096]{0:T(1024)S(1)} %copy-done.7, f32[4,200,200]{2,1,0:T(8,128)S(1)} %fusion.23, f32[1,200,200]{2,1,0:T(8,128)S(1)} %convolution_bitcast_fusion.1), kind=kOutput, calls=%fused_computation.11 | convolution fusion | flops 9836334080 | bytes 10646784 | tf_op jit(solution)/shard_map/bmn,nd->bmd/dot_general | solution.py:90
  460.0 19.8 %copy.91 = bf16[5,200,4096]{1,0,2:T(8,128)(2,1)} copy(bf16[5,200,4096]{2,1,0:T(8,128)(2,1)} %convolution_convert_fusion) | data formatting | bytes 16384000 | tf_op jit(solution)/shard_map/convert_element_type | solution.py:90
  479.8 36.9 %gather_fusion.1 = bf16[4096,5,200]{2,1,0:T(8,128)(2,1)} fusion(bf16[5,200,4096]{1,0,2:T(8,128)(2,1)} %copy.91, s32[4096]{0:T(1024)S(1)} %copy-done.3), kind=kCustom, calls=%fused_computation.1 | custom fusion | bytes 16400384 | tf_op jit(solution)/shard_map/jit(_take)/gather | solution.py:65
  516.8 12.5 %copy.92 = bf16[4096,5,200]{2,0,1:T(8,128)(2,1)} copy(bf16[4096,5,200]{2,1,0:T(8,128)(2,1)} %gather_fusion.1) | data formatting | bytes 16384000 | tf_op jit(solution)/shard_map/jit(_take)/gather | solution.py:65
  529.3 23.3 %fusion.4 = f32[5,2,64,64,128]{4,2,1,0,3:T(8,128)} fusion(bf16[2,200,64,128,1]{3,2,1,0,4:T(8,128)(2,1)} %bitcast_bitcast_fusion, bf16[64,64,5,200]{3,1,0,2:T(8,128)(2,1)} %bitcast.125, pred[64,64]{1,0:T(8,128)(4,1)S(1)} %compare_and_fusion), kind=kOutput, calls=%fused_computation.10 | convolution fusion | flops 2101248000 | bytes 35721216 | tf_op jit(solution)/shard_map/pmkc,bmkj->bpjkc/dot_general | solution.py:66
  552.6 2.7 slice_bitcast_fusion
  555.3 9.2 %fusion.1 = bf16[2,64,64,128]{3,1,0,2:T(8,128)(2,1)} fusion(f32[5,2,64,64,128]{4,2,1,0,3:T(8,128)} %fusion.4, f32[2,64,64,128]{3,1,0,2:T(8,128)S(1)} %slice_bitcast_fusion), kind=kLoop, calls=%fused_computation.4 | loop fusion | flops 11534336 | bytes 23068672 | tf_op jit(solution)/shard_map/reduce_sum | solution.py:68
  564.5 80.5 %all-gather = bf16[32,1,128]{2,1,0:T(2,128)(2,1)S(1)} all-gather(bf16[1,1,128]{2,1,0:T(2,128)(2,1)S(1)} %bitcast.135), channel_id=1, replica_groups=mesh['boot'=4,'slab'=32] {'slab'}, dimensions={0}, use_global_device_ids=true | all-gather | bytes 8448 | tf_op jit(solution)/shard_map/all_gather | solution.py:84
  645.1 2.8 fusion.8
  647.9 16.9 %gather_fusion = bf16[4096,200]{1,0:T(8,128)(2,1)} fusion(bf16[200,4096]{0,1:T(8,128)(2,1)S(1)} %fusion.8, s32[4096]{0:T(1024)S(1)} %copy-done.3), kind=kCustom, calls=%fused_computation | custom fusion | bytes 3293184 | tf_op jit(solution)/shard_map/jit(_take)/gather | solution.py:94
  664.9 5.4 convolution_bitcast_fusion
  670.3 7.8 %bitcast_add_fusion = f32[2,200,8192]{2,1,0:T(8,128)} fusion(f32[64,2,25,8,128]{4,3,2,1,0:T(8,128)S(1)} %convolution_bitcast_fusion, bf16[2,200,8192]{2,1,0:T(8,128)(2,1)} %param.7), kind=kLoop, calls=%fused_computation.5 | loop fusion | flops 6553600 | bytes 32768000 | tf_op jit(solution)/shard_map/add | solution.py:98
  (72 shorter events, 10.9 us)
Async XLA Ops:
  6.5 158.1 %all-gather.7.cloned.1.call-start = ((), (), s32[]{:S(2)}) async-start(), calls=%async_computation.1 | async-start | bytes 2162688 | tf_op jit(solution)/shard_map/all_gather | solution.py:82
  8.1 637.0 %all-gather.5.cloned.1.call-start = ((), (), s32[]{:S(2)}) async-start(), calls=%async_computation | async-start | bytes 2162688 | tf_op jit(solution)/shard_map/all_gather | solution.py:83
  9.7 655.2 %all-reduce.7.cloned.1.call-start = ((), (), s32[]{:S(2)}) async-start(), calls=%async_computation.2 | async-start | bytes 4194304 | tf_op jit(solution)/shard_map/psum | solution.py:92
  96.4 68.2 %copy-start.5 = (f32[32,1,128]{2,1,0:T(1,128)}, f32[32,1,128]{2,1,0:T(1,128)S(1)}, u32[]{:S(2)}) copy-start(f32[32,1,128]{2,1,0:T(1,128)S(1)} %convert_element_type.74) | copy-start | bytes 49156
  227.5 3.8 copy-start.4
  234.5 0.9 copy-start
  353.9 87.3 %copy-start.2 = (f32[72,200]{0,1:T(8,128)S(1)}, f32[72,200]{0,1:T(8,128)}, u32[]{:S(2)}) copy-start(f32[72,200]{0,1:T(8,128)} %copy.78) | copy-start | bytes 172804
  434.1 2.5 copy-start.1
  435.3 7.2 %copy-start.7 = (f32[4096]{0:T(1024)S(1)}, f32[4096]{0:T(1024)}, u32[]{:S(2)}) copy-start(f32[4096]{0:T(1024)} %multiply.21) | copy-start | bytes 49156
  460.0 19.8 %copy-start.3 = (s32[4096]{0:T(1024)S(1)}, s32[4096]{0:T(1024)}, u32[]{:S(2)}) copy-start(s32[4096]{0:T(1024)} %broadcast_clamp_fusion) | copy-start | bytes 49156
  555.3 9.2 %copy-start.8 = (bf16[128]{0:T(256)(128)(2,1)S(1)}, bf16[128]{0:T(256)(128)(2,1)}, u32[]{:S(2)}) copy-start(bf16[128]{0:T(256)(128)(2,1)} %param.10) | copy-start | bytes 772
  555.3 89.8 %copy-start.6 = (f32[32,1,128]{2,1,0:T(1,128)S(1)}, f32[32,1,128]{2,1,0:T(1,128)}, u32[]{:S(2)}) copy-start(f32[32,1,128]{2,1,0:T(1,128)} %copy-done.5) | copy-start | bytes 49156
Sparse Core Ops, SparseCore 0:
  9.0 155.5 all-gather.6
  166.3 154.2 all-gather.4
  564.6 58.9 all-reduce.6
where the time goes:
time: 695 us; the launch traced here: 685 us
  other arithmetic  272 us (39%)
  blocking collectives  163 us (23%)
  local copies, waits for them, and re-layouts  104 us (15%)
  matrix products  74.3 us (11%)
  waiting for transfers between devices  56.3 us (8%)
  between operations  15.3 us (2%)
    another operation x17, other arithmetic, member_map(): factor = jnp.linalg.cholesky(system)  146 us
    another operation x11, other arithmetic, member_map(): solved = jax.scipy.linalg.cho_solve((factor, True), proj_matrix.T)  102 us
    all_gather x1, blocking collectives, on_device(): lax.all_gather(obs_sd, 'slab', axis=0, tiled=True)  82.5 us
    all_gather x1, blocking collectives, on_device(): lax.all_gather(observed, 'slab', axis=0, tiled=True)  80.5 us
    all_gather x1, waiting for transfers between devices, on_device(): lax.all_gather(predicted, 'slab', axis=1, tiled=True)  56.2 us
    gather x2, local copies, waits for them, and re-layouts, gain_terms(): selected = jnp.take(columns, map_part, axis=2)  49.5 us
    dot_general x1, matrix products, gain_terms(): jnp.einsum('pmkc,bmkj->bpjkc', blocks, selected, preferred_element_type=j...  23.3 us
    convert_element_type x1, local copies, waits for them, and re-layouts, on_device(): jnp.einsum('bmn,nd->bmd', maps, weighted, precision=highest)  19.8 us
  transfers between devices with their start and end apart: 3, of which 1 were waited for; matrix products, arithmetic and copies ran while one was open for 63% of the time, Pallas kernels for 0%

commit v1 on v0

v1 whole, which is shorter than its diff:
```python
from functools import partial
import math

import jax
import jax.numpy as jnp
from jax import lax
from jax.experimental import pallas as pl
from jax.experimental.pallas import tpu as pltpu
from jax.sharding import PartitionSpec as P

M = 200
NB = 16
BLK = 128
NNZ = 64
MP = 256
HALF = 104
SHIFT = 96
ROWS = 112
PIV = 40
SYS = 9
MAPS = 17
GROUP = 8

screen_floor = 1e-05
f32 = jnp.float32
bf16 = jnp.bfloat16


def iota(shape, dim):
    return lax.broadcasted_iota(jnp.int32, shape, dim)


def split3(x):
    hi = x.astype(bf16).astype(f32)
    rest = x - hi
    mid = rest.astype(bf16).astype(f32)
    return hi, mid, rest - mid


def lhs6(c):
    hi, mid, lo = split3(c)
    left = hi + pltpu.roll(hi, PIV, 1) + pltpu.roll(hi, 2 * PIV, 1)
    right = mid + pltpu.roll(mid, PIV, 1) + pltpu.roll(lo, 2 * PIV, 1)
    return jnp.concatenate([left, right], axis=1).astype(bf16)


def rhs6(r):
    hi, mid, lo = split3(r)
    pad = jnp.zeros((BLK - 3 * PIV, MP), f32)
    return jnp.concatenate([hi, mid, lo, pad, hi, mid, hi, pad], axis=0).astype(bf16)


def dot(a, b):
    return jnp.dot(a, b, preferred_element_type=f32)


def member_rows(first, second):
    low = jnp.concatenate([first[:HALF], second[HALF - SHIFT:HALF - SHIFT + BLK - HALF]], axis=0)
    rest = second[BLK - SHIFT:HALF]
    return low, rest


def counts(members_ref, s):
    row = members_ref[pl.ds(s, 1), :]
    hit = jnp.where(iota((M, MP), 0) == row, 1.0, 0.0)
    down = jnp.sum(hit, axis=1, keepdims=True)
    across = jnp.sum(jnp.where(iota((M, MP), 0) == iota((M, MP), 1), down, 0.0), axis=0, keepdims=True)
    return jnp.sqrt(down), jnp.sqrt(across)


def map_kernel(core_ref, own_ref, other_ref, members_ref, full_ref, res_ref, gram_ref, sys_ref, piv_ref):
    core = core_ref[0]

    def chunk(i):
        own = own_ref[i].astype(f32)
        other = other_ref[i].astype(f32)
        first = jnp.where(core == 0, own, other)
        second = jnp.where(core == 0, other, own)
        low, rest = member_rows(first, second)
        sd = own[HALF:HALF + 1]
        ens = jnp.concatenate([low, rest, jnp.zeros((MP - M, BLK), f32)], axis=0)
        return ens, ens / (sd * sd)

    gram_ref[...] = jnp.zeros((MP, MP), f32)

    def add_gram(i, carry):
        a0, w0 = chunk(2 * i)
        a1, w1 = chunk(2 * i + 1)
        ens = jnp.concatenate([a0, a1], axis=1).astype(bf16)
        parts = split3(jnp.concatenate([w0, w1], axis=1))
        total = gram_ref[...]
        for part in parts:
            total = total + lax.dot_general(part.astype(bf16), ens, (((1,), (1,)), ((), ())), preferred_element_type=f32)
        gram_ref[...] = total
        return carry

    lax.fori_loop(0, own_ref.shape[0] // 2, add_gram, 0)

    row = iota((M, MP), 0)
    lane = iota((M, MP), 1)

    def build(s, carry):
        down, across = counts(members_ref, s)
        h = gram_ref[:M, :] * (down * (1.0 / (M - 1))) * across
        ud = down * (1.0 / math.sqrt(M))
        ua = across * (1.0 / math.sqrt(M))
        hu = jnp.sum(h * ua, axis=1, keepdims=True)
        uh = jnp.sum(h * ud, axis=0, keepdims=True)
        uhu = jnp.sum(hu * ud, axis=0, keepdims=True)
        h = h - ud * (uh - 0.5 * uhu * ua) - (hu - 0.5 * uhu * ud) * ua
        sys_ref[s] = h + jnp.where(row == lane, 1.0, 0.0)
        return carry

    lax.fori_loop(0, SYS, build, 0)

    prow = iota((PIV, MP), 0)
    plane = iota((PIV, MP), 1)
    drow = iota((PIV, BLK), 0)
    dlane = iota((PIV, BLK), 1)

    def panel_step(kp, carry):
        k0 = kp * PIV
        back = lax.rem(MP - k0, MP)
        ds = []
        for s in range(SYS):
            panel = sys_ref[s, pl.ds(pl.multiple_of(k0, 8), PIV), :]
            ds.append(jnp.where(dlane < PIV, pltpu.roll(panel, back, 1)[:, :BLK], 0.0))
        for t in range(PIV):
            at_lane = dlane == t
            at_row = drow == t
            for s in range(SYS):
                d = ds[s]
                col = d[:, t:t + 1]
                scale = 1.0 / d[t:t + 1, t:t + 1]
                line = jnp.where(dlane[:1] == t, 1.0, d[t:t + 1, :]) * scale
                new = jnp.where(at_lane, 0.0, d) - col * line
                ds[s] = jnp.where(at_row, line, new)
        for s in range(SYS):
            piv_ref[s] = ds[s]

        def update(s, inner):
            a = sys_ref[s]
            panel = sys_ref[s, pl.ds(pl.multiple_of(k0, 8), PIV), :]
            inside = (plane >= k0) & (plane < k0 + PIV)
            panel = jnp.where(plane == prow + k0, 1.0, jnp.where(inside, 0.0, panel))
            r = dot(lhs6(piv_ref[s]), rhs6(panel))
            c = jnp.where(iota((M, BLK), 1) < PIV, pltpu.roll(a, back, 1)[:, :BLK], 0.0)
            kept = jnp.where((lane >= k0) & (lane < k0 + PIV), 0.0, a)
            sys_ref[s] = kept - dot(lhs6(c), rhs6(r))
            sys_ref[s, pl.ds(pl.multiple_of(k0, 8), PIV), :] = r
            return inner

        lax.fori_loop(0, SYS, update, 0)
        return carry

    lax.fori_loop(0, M // PIV, panel_step, 0)

    def finish(s):
        down, across = counts(members_ref, s)
        ud = down * (1.0 / math.sqrt(M))
        ua = across * (1.0 / math.sqrt(M))
        return (sys_ref[s] - ud * ua) * (down * (1.0 / (M - 1))) * across

    full_ref[...] = finish(0)

    def finish_res(s, carry):
        res_ref[s] = finish(s + 1)
        return carry

    lax.fori_loop(0, SYS - 1, finish_res, 0)


def select_kernel(core_ref, map_ref, own_ref, other_ref, iown_ref, iother_ref, psel_ref, isel_ref, ptab_ref, itab_ref, line_ref):
    core = core_ref[0]
    blocks = map_ref.shape[0]

    def table(i, carry):
        for a_ref, b_ref, t_ref in ((own_ref, other_ref, ptab_ref), (iown_ref, iother_ref, itab_ref)):
            own = a_ref[i].astype(f32)
            other = b_ref[i].astype(f32)
            first = jnp.where(core == 0, own, other)
            second = jnp.where(core == 0, other, own)
            low, rest = member_rows(first, second)
            high = jnp.concatenate([rest, own[HALF:ROWS], jnp.zeros((2 * BLK - M - (ROWS - HALF), BLK), f32)], axis=0)
            base = pl.multiple_of(i * (2 * BLK), 8)
            t_ref[pl.ds(base, BLK, stride=2), :] = low.T
            t_ref[pl.ds(base + 1, BLK, stride=2), :] = high.T
        return carry

    lax.fori_loop(0, own_ref.shape[0], table, 0)

    def pick(t_ref, k, out_ref, at):
        for j in range(NNZ):
            line_ref[2 * j:2 * j + 2, :] = t_ref[pl.ds(2 * map_ref[k, j], 2), :]
        both = jnp.concatenate([line_ref[pl.ds(0, NNZ, stride=2), :], line_ref[pl.ds(1, NNZ, stride=2), :]], axis=1)
        out_ref[pl.ds(pl.multiple_of(at * NNZ, NNZ), NNZ), :] = both.astype(bf16)

    def pick_pred(k, carry):
        pick(ptab_ref, core * (blocks // 2) + k, psel_ref, k)
        return carry

    lax.fori_loop(0, blocks // 2, pick_pred, 0)

    def pick_innov(k, carry):
        pick(itab_ref, k, isel_ref, k)
        return carry

    lax.fori_loop(0, blocks, pick_innov, 0)


def gain_kernel(core_ref, psel_ref, full_ref, mine_ref, theirs_ref, params_ref, out_ref, maps_ref, cols_ref):
    @pl.when(pl.program_id(0) == 0)
    def _():
        def place(r, value):
            pad = jnp.zeros((MP - M, MP), f32)
            for n, part in enumerate(split3(value)):
                maps_ref[r, n * MP:(n + 1) * MP, :] = jnp.concatenate([part, pad], axis=0).astype(bf16)

        place(0, full_ref[...])

        def place_both(r, carry):
            place(1 + r, mine_ref[r])
            place(SYS + r, theirs_ref[r])
            return carry

        lax.fori_loop(0, SYS - 1, place_both, 0)

    x = psel_ref[...]
    sd = x[:, M:M + 1].astype(f32)
    weight = 1.0 / (sd * sd)

    def column(r, carry):
        total = dot(x, maps_ref[r, 0:MP, :]) + dot(x, maps_ref[r, MP:2 * MP, :]) + dot(x, maps_ref[r, 2 * MP:3 * MP, :])
        total = (total * weight).astype(bf16)
        for g in range(GROUP):
            cols_ref[g, pl.ds(pl.multiple_of(r * NNZ, NNZ), NNZ), :] = total[g * NNZ:(g + 1) * NNZ]
        return carry

    lax.fori_loop(0, MAPS, column, 0)

    def gains(g, carry):
        at = pl.ds(pl.multiple_of(g * BLK, BLK), BLK)
        cells = jnp.concatenate([params_ref[0, :, at], params_ref[1, :, at]], axis=1)
        every = dot(cols_ref[g][:, :M], cells)
        full = every[:NNZ]
        spread = jnp.zeros_like(full)
        for r in range(1, MAPS):
            off = every[r * NNZ:(r + 1) * NNZ] - full
            spread = spread + off * off
        squared = full * full
        out_ref[g] = (squared / (squared + spread * (1.0 / NB) + screen_floor) * full).astype(bf16)
        return carry

    lax.fori_loop(0, GROUP, gains, 0)


def change_kernel(half_ref, isel_ref, screened_ref, params_ref, *rest):
    out_ref = rest[-1]
    for g in range(GROUP):
        change = lax.dot_general(
            isel_ref[g * NNZ:(g + 1) * NNZ, :], screened_ref[g], (((0,), (0,)), ((), ())), preferred_element_type=f32
        )
        at = slice(g * BLK, (g + 1) * BLK)
        for p in range(2):
            out_ref[p, :, at] = params_ref[p, :, at].astype(f32) + change[:M, p * BLK:(p + 1) * BLK]


vmem = pl.BlockSpec(memory_space=pltpu.VMEM)
smem = pl.BlockSpec(memory_space=pltpu.SMEM)
limit = pltpu.CompilerParams(vmem_limit_bytes=56 * 1024 * 1024)


def make_maps(core, own, other, members):
    return pl.pallas_call(
        map_kernel,
        out_shape=(jax.ShapeDtypeStruct((M, MP), f32), jax.ShapeDtypeStruct((SYS - 1, M, MP), f32)),
        in_specs=[smem, vmem, vmem, vmem],
        out_specs=(vmem, vmem),
        scratch_shapes=[
            pltpu.VMEM((MP, MP), f32),
            pltpu.VMEM((SYS, M, MP), f32),
            pltpu.VMEM((SYS, PIV, BLK), f32),
        ],
        compiler_params=limit,
        cost_estimate=pl.CostEstimate(flops=20_000_000_000, bytes_accessed=8_000_000, transcendentals=0),
        name="maps",
    )(core, own, other, members)


def select(core, block_map, own, other, iown, iother):
    blocks = block_map.shape[0]
    data = own.shape[0] * BLK
    return pl.pallas_call(
        select_kernel,
        out_shape=(
            jax.ShapeDtypeStruct((blocks // 2 * NNZ, MP), bf16),
            jax.ShapeDtypeStruct((blocks * NNZ, MP), bf16),
        ),
        in_specs=[smem, smem, vmem, vmem, vmem, vmem],
        out_specs=(vmem, vmem),
        scratch_shapes=[
            pltpu.VMEM((2 * data, BLK), f32),
            pltpu.VMEM((2 * data, BLK), f32),
            pltpu.VMEM((2 * NNZ, BLK), f32),
        ],
        compiler_params=limit,
        cost_estimate=pl.CostEstimate(flops=10_000_000_000, bytes_accessed=8_000_000, transcendentals=0),
        name="select",
    )(core, block_map, own, other, iown, iother)


def make_screened(core, psel, full, mine, theirs, params):
    blocks = params.shape[2] // BLK // 2
    steps = blocks // GROUP
    return pl.pallas_call(
        gain_kernel,
        out_shape=jax.ShapeDtypeStruct((blocks, NNZ, 2 * BLK), bf16),
        grid_spec=pltpu.PrefetchScalarGridSpec(
            num_scalar_prefetch=1,
            grid=(steps,),
            in_specs=[
                pl.BlockSpec((GROUP * NNZ, MP), lambda i, c: (i, 0)),
                pl.BlockSpec((M, MP), lambda i, c: (0, 0)),
                pl.BlockSpec((SYS - 1, M, MP), lambda i, c: (0, 0, 0)),
                pl.BlockSpec((SYS - 1, M, MP), lambda i, c: (0, 0, 0)),
                pl.BlockSpec((2, M, GROUP * BLK), lambda i, c: (0, 0, c[0] * steps + i)),
            ],
            out_specs=pl.BlockSpec((GROUP, NNZ, 2 * BLK), lambda i, c: (i, 0, 0)),
            scratch_shapes=[
                pltpu.VMEM((MAPS, 3 * MP, MP), bf16),
                pltpu.VMEM((GROUP, MAPS * NNZ, MP), bf16),
            ],
        ),
        compiler_params=limit,
        cost_estimate=pl.CostEstimate(flops=20_000_000_000, bytes_accessed=8_000_000, transcendentals=0),
        name="gains",
    )(core, psel, full, mine, theirs, params)


def update(half, isel, screened, params, so_far=None):
    blocks = params.shape[2] // BLK // 2
    steps = blocks // GROUP
    cells = pl.BlockSpec((2, M, GROUP * BLK), lambda i, c: (0, 0, c[0] * steps + i))
    in_specs = [
        pl.BlockSpec((GROUP * NNZ, MP), lambda i, c: (c[0] * steps + i, 0)),
        pl.BlockSpec((GROUP, NNZ, 2 * BLK), lambda i, c: (i, 0, 0)),
        cells,
    ]
    operands = (half, isel, screened, params)
    if so_far is not None:
        in_specs.append(pl.BlockSpec(memory_space=pl.ANY))
        operands = operands + (so_far,)
    return pl.pallas_call(
        change_kernel,
        out_shape=jax.ShapeDtypeStruct(params.shape, f32),
        grid_spec=pltpu.PrefetchScalarGridSpec(
            num_scalar_prefetch=1, grid=(steps,), in_specs=in_specs, out_specs=cells
        ),
        input_output_aliases={} if so_far is None else {4: 0},
        compiler_params=limit,
        cost_estimate=pl.CostEstimate(flops=5_000_000_000, bytes_accessed=10_000_000, transcendentals=0),
        name="change",
    )(*operands)


def on_device(params, predicted, perturbation, observed, obs_sd, members, block_map):
    boot = lax.axis_index("boot")
    core = lax.rem(boot, 2)
    core_arg = core.reshape(1).astype(jnp.int32)
    slabs = lax.axis_size("slab")
    pair = [(i, i ^ 1) for i in range(4)]
    far = [(i, i ^ 2) for i in range(4)]

    def share(rows):
        part = lax.dynamic_slice_in_dim(rows, core * SHIFT, HALF, 0)
        tail = jnp.zeros((ROWS - HALF - 1, rows.shape[1]), bf16)
        return jnp.concatenate([part, obs_sd[None], tail], axis=0)

    def spread_out(part):
        whole = jnp.broadcast_to(part[None], (slabs,) + part.shape)
        own = lax.all_to_all(whole, "slab", 0, 0)
        return own, lax.ppermute(own, "boot", pair)

    noise = obs_sd.astype(f32)
    innovation = (observed.astype(f32) + noise * perturbation.astype(f32) - predicted.astype(f32)).astype(bf16)

    far_members = lax.ppermute(members, "boot", far)
    every = jnp.arange(M, dtype=jnp.int32)[None]
    lists = jnp.concatenate([every, members, far_members], axis=0)
    lists = jnp.pad(lists, ((0, 16 - SYS), (0, MP - M)), constant_values=-1)

    own, other = spread_out(share(predicted))
    innov_part, other = lax.optimization_barrier((share(innovation), other))
    iown, iother = spread_out(innov_part)

    full, mine = make_maps(core_arg, own, other, lists)
    block_map, mine = lax.optimization_barrier((block_map, mine))
    theirs = lax.ppermute(mine, "boot", pair)
    psel, isel = select(core_arg, block_map, own, other, iown, iother)
    screened = make_screened(core_arg, psel, full, mine, theirs, params)
    screened_other = lax.ppermute(screened, "boot", pair)
    partial_out = update(core_arg, isel, screened, params)
    return update(1 - core_arg, isel, screened_other, params, partial_out)


def solution(mesh):
    return jax.shard_map(
        on_device,
        mesh=mesh,
        in_specs=(
            P(None, None, "slab"),
            P(None, "slab"),
            P(None, "slab"),
            P("slab"),
            P("slab"),
            P("boot", None),
            P("slab", None),
        ),
        out_specs=P(None, None, "slab"),
        check_vma=False,
    )
```

time: 695 us -> 182 us (0.26); the launches traced: 685 us -> 180 us
  other arithmetic: 272 us -> 3.52 us
  blocking collectives: 163 us -> 24.1 us
  Pallas kernels: 0 us -> 125 us
  local copies, waits for them, and re-layouts: 104 us -> 5.81 us
  matrix products: 74.3 us -> 0 us
  waiting for transfers between devices: 56.3 us -> 13.7 us
  between operations: 15.3 us -> 0.06 us
  starting transfers between devices: 0.09 us -> 8.19 us
    another operation x29 -> x0, other arithmetic: 248 us -> none  [the longest x17 146 us: member_map(): factor = jnp.linalg.cholesky(system)]
    all_gather x2 -> x0, blocking collectives: 163 us -> none  [the longest x1 82.5 us: on_device(): lax.all_gather(obs_sd, 'slab', axis=0, tiled=True)]
    pallas_call x0 -> x5, Pallas kernels: none -> 125 us  [the longest x1 55.6 us: make_maps(): pl.pallas_call(map_kernel, out_shape=(jax.ShapeDtypeStruct((M, MP), f32),...]
    gather x3 -> x0, local copies, waits for them, and re-layouts: 66.4 us -> none  [the longest x2 49.5 us: gain_terms(): selected = jnp.take(columns, map_part, axis=2)]
    dot_general x11 -> x0, matrix products: 62.3 us -> none  [the longest x1 23.3 us: gain_terms(): jnp.einsum('pmkc,bmkj->bpjkc', blocks, selected, preferred_element_type=j...]
    all_gather x2 -> x0, waiting for transfers between devices: 56.2 us -> none  [the longest x1 56.2 us: on_device(): lax.all_gather(predicted, 'slab', axis=1, tiled=True)]
    all_to_all x0 -> x1, blocking collectives: none -> 24.1 us  [spread_out(): own = lax.all_to_all(whole, 'slab', 0, 0)]
    convert_element_type x1 -> x0, local copies, waits for them, and re-layouts: 19.8 us -> none  [on_device(): jnp.einsum('bmn,nd->bmd', maps, weighted, precision=highest)]
  transfers between devices with their start and end apart: 3 -> 6, of which waited for: 1 -> 3; matrix products, arithmetic and copies ran while one was open for 63% -> 1% of each run, Pallas kernels for 0% -> 42%
where the time goes in v1:
time: 182 us; the launch traced here: 180 us
  Pallas kernels  125 us (69%)
  blocking collectives  24.1 us (13%)
  waiting for transfers between devices  13.7 us (8%)
  starting transfers between devices  8.19 us (4%)
  local copies, waits for them, and re-layouts  5.81 us (3%)
  other arithmetic  3.52 us (2%)
    pallas_call x1, Pallas kernels, make_maps(): pl.pallas_call(map_kernel, out_shape=(jax.ShapeDtypeStruct((M, MP), f32),...  55.6 us
    pallas_call x1, Pallas kernels, make_screened(): pl.pallas_call(gain_kernel, out_shape=jax.ShapeDtypeStruct((blocks, NNZ,...  42.4 us
    all_to_all x1, blocking collectives, spread_out(): own = lax.all_to_all(whole, 'slab', 0, 0)  24.1 us
    pallas_call x1, Pallas kernels, select(): pl.pallas_call(select_kernel, out_shape=(jax.ShapeDtypeStruct((blocks //...  14.4 us
    pallas_call x2, Pallas kernels, update(): pl.pallas_call(change_kernel, out_shape=jax.ShapeDtypeStruct(params.shape...  12.6 us
    ppermute x1, waiting for transfers between devices, on_device(): far_members = lax.ppermute(members, 'boot', far)  10.5 us
    all_to_all x1, starting transfers between devices, spread_out(): own = lax.all_to_all(whole, 'slab', 0, 0)  4.87 us
  transfers between devices with their start and end apart: 6, of which 3 were waited for; matrix products, arithmetic and copies ran while one was open for 1% of the time, Pallas kernels for 42%

profile of v1, /device:TPU:0, one launch (start us, length us, event | category | flops | bytes accessed | tf_op | source)
XLA Modules:
  0.0 180.4 jit_solution(11521049557931933921)
XLA Ops:
  0.0 0.7 convert_element_type.15
  0.7 0.7 convert_element_type.16
  1.3 0.1 pad.13.clone
  1.4 0.7 constant_dynamic-slice_fusion
  2.1 0.8 subtract_convert_fusion
  2.9 0.7 fusion.1
  3.7 0.1 broadcast_in_dim.7
  3.8 24.1 %all_to_all.10.own_ref = bf16[32,112,128]{2,1,0:T(8,128)(2,1)S(1)} all-to-all(bf16[32,112,128]{2,1,0:T(8,128)(2,1)S(1)} %broadcast_in_dim.7), channel_id=1, replica_groups=mesh['boot'=4,'slab'=32] {'slab'}, dimensions={0} | all-to-all | bytes 1835008 | tf_op jit(solution)/shard_map/all_to_all | solution.py:381
  27.9 0.0 copy-start.1
  27.9 0.0 collective-permute-start
  27.9 2.5 %collective-permute-done.other_ref = bf16[32,112,128]{2,1,0:T(8,128)(2,1)S(1)} collective-permute-done((bf16[32,112,128]{2,1,0:T(8,128)(2,1)S(1)}, bf16[32,112,128]{2,1,0:T(8,128)(2,1)S(1)}, u32[]{:S(2)}, u32[]{:S(2)}) %collective-permute-start) | collective-permute-done | bytes 917536 | tf_op jit(solution)/shard_map/ppermute | solution.py:382
  30.3 0.0 copy-start.4
  30.3 1.1 broadcast_in_dim.8
  31.5 4.9 %all-to-all-start.1 = ((bf16[32,112,128]{2,1,0:T(8,128)(2,1)}), bf16[32,112,128]{2,1,0:T(8,128)(2,1)S(1)}, u32[]{:S(2)}, u32[]{:S(2)}) async-start(bf16[32,112,128]{2,1,0:T(8,128)(2,1)} %broadcast_in_dim.8), calls=%async_computation.1 | async-start | bytes 1835008 | tf_op jit(solution)/shard_map/all_to_all | solution.py:381
  36.4 2.8 %collective-permute-start.1 = (s32[4,200]{1,0:T(4,128)}, s32[4,200]{1,0:T(4,128)S(1)}, u32[]{:S(2)}, u32[]{:S(2)}) collective-permute-start(s32[4,200]{1,0:T(4,128)} %param.12), channel_id=1, source_target_pairs={{0,64},{32,96},{64,0},{96,32},{1,65},{33,97},{65,1},{97,33},{2,66}... | collective-permute-start | bytes 9608 | tf_op jit(solution)/shard_map/ppermute | solution.py:387
  39.2 10.5 %collective-permute-done.1 = s32[4,200]{1,0:T(4,128)S(1)} collective-permute-done((s32[4,200]{1,0:T(4,128)}, s32[4,200]{1,0:T(4,128)S(1)}, u32[]{:S(2)}, u32[]{:S(2)}) %collective-permute-start.1) | collective-permute-done | bytes 3232 | tf_op jit(solution)/shard_map/ppermute | solution.py:387
  49.7 0.7 pad_add_fusion
  50.4 0.6 pad.4.members_ref
  51.0 0.7 all-to-all-done.1.iown_ref
  51.7 0.0 copy-start.2
  51.7 0.0 collective-permute-start.2
  51.7 0.0 copy-done.1
  51.7 0.0 copy-done.4
  51.7 55.6 %maps.1 = (f32[200,256]{1,0:T(8,128)}, f32[8,200,256]{2,1,0:T(8,128)}) custom-call(s32[1]{0:T(128)} %bitcast.core_ref.half_ref, bf16[32,112,128]{2,1,0:T(8,128)(2,1)} %copy-done.1, bf16[32,112,128]{2,1,0:T(8,128)(2,1)} %copy-done.4, s32[16,256]{1,0:T(8,128)} %pad.4.members_ref), custom_call_target="tpu_custom_call" | custom-call | flops 20000000000 | bytes 8000000 | tf_op jit(solution)/shard_map/maps/pallas_call | solution.py:274
  107.3 0.0 copy-done.2
  107.3 0.2 collective-permute-start.3
  107.5 0.0 collective-permute-done.2.iother_ref
  107.5 0.0 copy-start.5
  107.5 0.9 copy-done.5
  108.5 14.4 %select.4 = (bf16[2048,256]{1,0:T(8,128)(2,1)}, bf16[4096,256]{1,0:T(8,128)(2,1)}) custom-call(s32[1]{0:T(128)} %bitcast.core_ref.half_ref, s32[64,64]{1,0:T(8,128)} %map_ref, bf16[32,112,128]{2,1,0:T(8,128)(2,1)} %copy-done.1, bf16[32,112,128]{2,1,0:T(8,128)(2,1)} %copy-done.4, bf16[32,112,128]{2,1,0:T(8,128)(2,1)} %copy-done.2, bf16[32,112,128]{2,1,0:T(8,128)(2,1)} %copy-done.5), custom_call_target="tpu_custom_call" | custom-call | flops 10000000000 | bytes 8000000 | tf_op jit(solution)/shard_map/select/pallas_call | solution.py:293
  122.9 0.0 collective-permute-done.3.theirs_ref
  122.9 0.0 copy-start.3
  122.9 1.2 copy-done.3
  124.0 42.4 %gains.1.screened_ref = bf16[32,64,256]{2,1,0:T(8,128)(2,1)} custom-call(s32[1]{0:T(128)} %bitcast.core_ref.half_ref, bf16[2048,256]{1,0:T(8,128)(2,1)} %get-tuple-element.18.psel_ref, f32[200,256]{1,0:T(8,128)} %get-tuple-element.19.full_ref, f32[8,200,256]{2,1,0:T(8,128)} %get-tuple-element.20.mine_ref, f32[8,200,256]{2,1,0:T(8,128)} %copy-done.3, ...), custom_call_target="tpu_custom_call" | custom-call | flops 20000000000 | bytes 8000000 | tf_op jit(solution)/shard_map/gains/pallas_call | solution.py:315
  166.4 0.3 collective-permute-start.4
  166.8 6.3 %change.2.rest_0_ = f32[2,200,8192]{2,1,0:T(8,128)} custom-call(s32[1]{0:T(128)} %bitcast.core_ref.half_ref, bf16[4096,256]{1,0:T(8,128)(2,1)} %get-tuple-element.17.isel_ref, bf16[32,64,256]{2,1,0:T(8,128)(2,1)} %gains.1.screened_ref, bf16[2,200,8192]{2,1,0:T(8,128)(2,1)} %params_ref.5), custom_call_target="tpu_custom_call" | custom-call | flops 5000000000 | bytes 10000000 | tf_op jit(solution)/shard_map/change/pallas_call | solution.py:353
  173.1 0.0 collective-permute-done.4.screened_ref
  173.1 0.0 copy-start
  173.1 1.0 copy-done
  174.0 6.3 %change.3 = f32[2,200,8192]{2,1,0:T(8,128)} custom-call(s32[1]{0:T(128)S(6)} %sub.6.half_ref, bf16[4096,256]{1,0:T(8,128)(2,1)} %get-tuple-element.17.isel_ref, bf16[32,64,256]{2,1,0:T(8,128)(2,1)} %copy-done, bf16[2,200,8192]{2,1,0:T(8,128)(2,1)} %params_ref.5, f32[2,200,8192]{2,1,0:T(8,128)} %change.2.rest_0_), custom_call_target="tpu_custom_call", output_to_operand_aliasing={{}: (4, {})} | custom-call | flops 5000000000 | bytes 10000000 | tf_op jit(solution)/shard_map/change/pallas_call | solution.py:353
  (2 shorter events, 0.0 us)
Async XLA Ops:
  27.9 23.8 %copy-start.1 = (bf16[32,112,128]{2,1,0:T(8,128)(2,1)}, bf16[32,112,128]{2,1,0:T(8,128)(2,1)S(1)}, u32[]{:S(2)}) copy-start(bf16[32,112,128]{2,1,0:T(8,128)(2,1)S(1)} %all_to_all.10.own_ref) | copy-start | bytes 2752516
  27.9 2.5 %collective-permute-start = (bf16[32,112,128]{2,1,0:T(8,128)(2,1)S(1)}, bf16[32,112,128]{2,1,0:T(8,128)(2,1)S(1)}, u32[]{:S(2)}, u32[]{:S(2)}) collective-permute-start(bf16[32,112,128]{2,1,0:T(8,128)(2,1)S(1)} %all_to_all.10.own_ref), channel_id=1, source_target_pairs={{0,32},{32,0},{64,96},{96,64},{1,33},{33,1},{65,97},{97,65},{2,34}... | collective-permute-start | bytes 2752520 | tf_op jit(solution)/shard_map/ppermute | solution.py:382
  30.3 21.3 %copy-start.4 = (bf16[32,112,128]{2,1,0:T(8,128)(2,1)}, bf16[32,112,128]{2,1,0:T(8,128)(2,1)S(1)}, u32[]{:S(2)}) copy-start(bf16[32,112,128]{2,1,0:T(8,128)(2,1)S(1)} %collective-permute-done.other_ref) | copy-start | bytes 2752516
  31.5 20.2 %all-to-all-start.1 = ((bf16[32,112,128]{2,1,0:T(8,128)(2,1)}), bf16[32,112,128]{2,1,0:T(8,128)(2,1)S(1)}, u32[]{:S(2)}, u32[]{:S(2)}) async-start(bf16[32,112,128]{2,1,0:T(8,128)(2,1)} %broadcast_in_dim.8), calls=%async_computation.1 | async-start | bytes 1835008 | tf_op jit(solution)/shard_map/all_to_all | solution.py:381
  36.4 13.3 %collective-permute-start.1 = (s32[4,200]{1,0:T(4,128)}, s32[4,200]{1,0:T(4,128)S(1)}, u32[]{:S(2)}, u32[]{:S(2)}) collective-permute-start(s32[4,200]{1,0:T(4,128)} %param.12), channel_id=1, source_target_pairs={{0,64},{32,96},{64,0},{96,32},{1,65},{33,97},{65,1},{97,33},{2,66}... | collective-permute-start | bytes 9608 | tf_op jit(solution)/shard_map/ppermute | solution.py:387
  51.7 55.7 %copy-start.2 = (bf16[32,112,128]{2,1,0:T(8,128)(2,1)}, bf16[32,112,128]{2,1,0:T(8,128)(2,1)S(1)}, u32[]{:S(2)}) copy-start(bf16[32,112,128]{2,1,0:T(8,128)(2,1)S(1)} %all-to-all-done.1.iown_ref) | copy-start | bytes 2752516
  51.7 55.8 %collective-permute-start.2 = (bf16[32,112,128]{2,1,0:T(8,128)(2,1)S(1)}, bf16[32,112,128]{2,1,0:T(8,128)(2,1)S(1)}, u32[]{:S(2)}, u32[]{:S(2)}) collective-permute-start(bf16[32,112,128]{2,1,0:T(8,128)(2,1)S(1)} %all-to-all-done.1.iown_ref), channel_id=1, source_target_pairs={{0,32},{32,0},{64,96},{96,64},{1,33},{33,1},{65,97},{97,65},{2,34}... | collective-permute-start | bytes 2752520 | tf_op jit(solution)/shard_map/ppermute | solution.py:382
  107.3 15.5 %collective-permute-start.3 = (f32[8,200,256]{2,1,0:T(8,128)}, f32[8,200,256]{2,1,0:T(8,128)S(1)}, u32[]{:S(2)}, u32[]{:S(2)}) collective-permute-start(f32[8,200,256]{2,1,0:T(8,128)} %get-tuple-element.20.mine_ref), channel_id=1, source_target_pairs={{0,32},{32,0},{64,96},{96,64},{1,33},{33,1},{65,97},{97,65},{2,34}... | collective-permute-start | bytes 4915208 | tf_op jit(solution)/shard_map/ppermute | solution.py:398
  107.5 0.9 copy-start.5
  122.9 1.2 copy-start.3
  166.4 6.7 %collective-permute-start.4 = (bf16[32,64,256]{2,1,0:T(8,128)(2,1)}, bf16[32,64,256]{2,1,0:T(8,128)(2,1)S(1)}, u32[]{:S(2)}, u32[]{:S(2)}) collective-permute-start(bf16[32,64,256]{2,1,0:T(8,128)(2,1)} %gains.1.screened_ref), channel_id=1, source_target_pairs={{0,32},{32,0},{64,96},{96,64},{1,33},{33,1},{65,97},{97,65},{2,34}... | collective-permute-start | bytes 3145736 | tf_op jit(solution)/shard_map/ppermute | solution.py:401
  173.1 1.0 copy-start

commit v2 on v1

v2 whole, which is shorter than its diff:
```python
from functools import partial
import math

import jax
import jax.numpy as jnp
from jax import lax
from jax.experimental import pallas as pl
from jax.experimental.pallas import tpu as pltpu
from jax.sharding import PartitionSpec as P

M = 200
NB = 16
BLK = 128
NNZ = 64
MP = 256
HALF = 104
SHIFT = 96
ROWS = 112
PIV = 40
SYS = 9
PACK = 3
ROWS_M = 208
MAPS = 17
GROUP = 8

screen_floor = 1e-05
f32 = jnp.float32
bf16 = jnp.bfloat16


def iota(shape, dim):
    return lax.broadcasted_iota(jnp.int32, shape, dim)


def split3(x):
    hi = x.astype(bf16).astype(f32)
    rest = x - hi
    mid = rest.astype(bf16).astype(f32)
    return hi, mid, rest - mid


def lhs6(c):
    hi, mid, lo = split3(c)
    left = hi + pltpu.roll(hi, PIV, 1) + pltpu.roll(hi, 2 * PIV, 1)
    right = mid + pltpu.roll(mid, PIV, 1) + pltpu.roll(lo, 2 * PIV, 1)
    return jnp.concatenate([left, right], axis=1).astype(bf16)


def rhs6(r):
    hi, mid, lo = split3(r)
    pad = jnp.zeros((BLK - 3 * PIV, MP), f32)
    return jnp.concatenate([hi, mid, lo, pad, hi, mid, hi, pad], axis=0).astype(bf16)


def dot(a, b):
    return jnp.dot(a, b, preferred_element_type=f32)


def counts(members_ref, s):
    row = members_ref[pl.ds(s, 1), :]
    hit = jnp.where(iota((M, MP), 0) == row, 1.0, 0.0)
    down = jnp.sum(hit, axis=1, keepdims=True)
    across = jnp.sum(jnp.where(iota((M, MP), 0) == iota((M, MP), 1), down, 0.0), axis=0, keepdims=True)
    return jnp.sqrt(down), jnp.sqrt(across)


def pack_kernel(core_ref, pred_ref, pert_ref, obs_ref, sd_ref, ens_ref, innov_ref):
    core = core_ref[0]
    sd = sd_ref[...].astype(f32)
    ens = pred_ref[...].astype(f32)
    innov = obs_ref[...].astype(f32) + sd * pert_ref[...].astype(f32) - ens
    tail = jnp.concatenate([sd, jnp.zeros((ROWS - HALF - 1, BLK), f32)], axis=0)
    for rows, out_ref in ((ens, ens_ref), (innov, innov_ref)):
        part = jnp.where(core == 0, rows[:HALF], rows[SHIFT:SHIFT + HALF])
        part = jnp.concatenate([part, tail], axis=0).astype(bf16)
        for i in range(out_ref.shape[0]):
            out_ref[i] = part


def members_first(core, own, other):
    first = jnp.where(core == 0, own, other)
    second = jnp.where(core == 0, other, own)
    low = jnp.concatenate([first[:HALF], second[HALF - SHIFT:BLK - SHIFT]], axis=0)
    high = jnp.concatenate([second[BLK - SHIFT:HALF], own[HALF:ROWS], jnp.zeros((MP - M - (ROWS - HALF), BLK), f32)], axis=0)
    return low, high


def fill_table(t_ref, i, low, high):
    base = pl.multiple_of(i * (2 * BLK), 8)
    t_ref[pl.ds(base, BLK, stride=2), :] = low
    t_ref[pl.ds(base + 1, BLK, stride=2), :] = high


def pick(t_ref, map_ref, k, line_ref):
    for j in range(NNZ):
        line_ref[2 * j:2 * j + 2, :] = t_ref[pl.ds(2 * map_ref[k, j], 2), :]
    both = [line_ref[pl.ds(n, NNZ, stride=2), :] for n in range(2)]
    return jnp.concatenate(both, axis=1).astype(bf16)


def map_kernel(core_ref, map_ref, own_ref, other_ref, members_ref, full_ref, res_ref, psel_ref, ens_ref, parts_ref, table_ref, line_ref, *sys_refs):
    core = core_ref[0]
    blocks = map_ref.shape[0]

    def chunk(i, carry):
        own = own_ref[i].astype(f32)
        low, high = members_first(core, own, other_ref[i].astype(f32))
        sd = own[HALF:HALF + 1]
        at = pl.ds(pl.multiple_of(i * BLK, BLK), BLK)
        rows = jnp.concatenate([low, high[:ROWS_M - BLK]], axis=0)
        for n, part in enumerate(split3(rows * (1.0 / (sd * sd)))):
            parts_ref[n, :, at] = part.astype(bf16)
        low, high = low.T, high.T
        ens_ref[at, :] = jnp.concatenate([low, high], axis=1).astype(bf16)
        fill_table(table_ref, i, low, high)
        return carry

    lax.fori_loop(0, own_ref.shape[0], chunk, 0, unroll=4)

    gram = 0.0
    for n in (2, 1, 0):
        gram = gram + dot(parts_ref[n], ens_ref[...])
    gram = gram[:M]

    def pick_own(k, carry):
        psel_ref[pl.ds(pl.multiple_of(k * NNZ, NNZ), NNZ), :] = pick(
            table_ref, map_ref, core * (blocks // 2) + k, line_ref
        )
        return carry

    lax.fori_loop(0, blocks // 2, pick_own, 0)

    row = iota((M, MP), 0)
    lane = iota((M, MP), 1)
    for s in range(SYS):
        down, across = counts(members_ref, s)
        h = gram * (down * (1.0 / (M - 1))) * across
        ud = down * (1.0 / math.sqrt(M))
        ua = across * (1.0 / math.sqrt(M))
        hu = jnp.sum(h * ua, axis=1, keepdims=True)
        uh = jnp.sum(h * ud, axis=0, keepdims=True)
        uhu = jnp.sum(hu * ud, axis=0, keepdims=True)
        h = h - ud * (uh - 0.5 * uhu * ua) - (hu - 0.5 * uhu * ud) * ua
        sys_refs[s][...] = h + jnp.where(row == lane, 1.0, 0.0)

    prow = iota((PIV, MP), 0)
    plane = iota((PIV, MP), 1)
    dlane = iota((PIV, BLK), 1)
    trow = iota((8, BLK), 0)
    tlane = iota((8, BLK), 1)
    first = jnp.minimum(tlane // PIV, PACK - 1) * PIV
    inner = tlane - first

    def panel_step(kp, carry):
        k0 = kp * PIV
        at = pl.ds(pl.multiple_of(k0, 8), PIV)
        packs = []
        for g in range(SYS // PACK):
            pack = jnp.zeros((PIV, BLK), f32)
            for q in range(PACK):
                moved = pltpu.roll(sys_refs[PACK * g + q][at, :], lax.rem(MP - k0 + q * PIV, MP), 1)[:, :BLK]
                pack = jnp.where((dlane >= q * PIV) & (dlane < (q + 1) * PIV), moved, pack)
            packs.append(pack)
        starts = packs
        tiles = [[pack[8 * i:8 * i + 8] for i in range(PIV // 8)] for pack in packs]
        for j in range(PIV // 8):
            cols = [
                [[jnp.take_along_axis(tile, first + 8 * j + u, axis=1) for u in range(8)] for tile in group]
                for group in tiles
            ]
            for u in range(8):
                at_lane = inner == 8 * j + u
                for group, col in zip(tiles, cols):
                    lead = col[j][u]
                    scale = 1.0 / lead[u:u + 1]
                    t = group[j]
                    line = jnp.where(at_lane[:1], 1.0, t[u:u + 1]) * scale
                    group[j] = jnp.where(trow == u, line, jnp.where(at_lane, 0.0, t) - lead * line)
                    for v in range(u + 1, 8):
                        c = col[j][v]
                        line = c[u:u + 1] * scale
                        col[j][v] = jnp.where(trow == u, line, c - lead * line)
            done = (inner >= 8 * j) & (inner < 8 * j + 8)
            for group, col in zip(tiles, cols):
                for i in range(PIV // 8):
                    if i != j:
                        tile = jnp.where(done, 0.0, group[i])
                        for u in range(8):
                            tile = tile - col[i][u] * group[j][u:u + 1]
                        group[i] = tile
        packs = [jnp.concatenate(group, axis=0) for group in tiles]
        inside = (lane >= k0) & (lane < k0 + PIV)
        pad = jnp.zeros((BLK - 3 * PIV, MP), f32)
        inverses, blocks_, panels, wanted, lines = [], [], [], [], []
        for s in range(SYS):
            back = (BLK - (s % PACK) * PIV) % BLK
            for kept, source in ((inverses, packs), (blocks_, starts)):
                moved = source[s // PACK]
                if back:
                    moved = pltpu.roll(moved, back, 1)
                kept.append(lhs6(jnp.where(dlane < PIV, moved, 0.0)))
            panels.append(sys_refs[s][at, :])
            wanted.append(jnp.where(plane == prow + k0, -1.0, jnp.where(inside[:PIV], 0.0, panels[s])))
        for s in range(SYS):
            lines.append(dot(inverses[s], rhs6(wanted[s])))
        for s in range(SYS):
            lines[s] = lines[s] + dot(inverses[s], rhs6(wanted[s] - dot(blocks_[s], rhs6(lines[s]))))
        for s in range(SYS):
            hi, mid, lo = split3(panels[s])
            left = jnp.concatenate([hi, hi, hi, pad, mid, mid, lo, pad], axis=0).astype(bf16)
            change = lax.dot_general(left, rhs6(lines[s]), (((0,), (0,)), ((), ())), preferred_element_type=f32)
            sys_refs[s][...] = jnp.where(inside, 0.0, sys_refs[s][...]) - change[:M]
            sys_refs[s][at, :] = lines[s]
        return carry

    lax.fori_loop(0, M // PIV, panel_step, 0)

    for s in range(SYS):
        down, across = counts(members_ref, s)
        both = down * across
        value = (-sys_refs[s][...] - both * (1.0 / M)) * (both * (1.0 / (M - 1)))
        if s == 0:
            full_ref[...] = value
        else:
            res_ref[s - 1] = value


def select_kernel(core_ref, map_ref, own_ref, other_ref, isel_ref, table_ref, line_ref):
    core = core_ref[0]

    def chunk(i, carry):
        low, high = members_first(core, own_ref[i].astype(f32), other_ref[i].astype(f32))
        fill_table(table_ref, i, low.T, high.T)
        return carry

    lax.fori_loop(0, own_ref.shape[0], chunk, 0, unroll=4)

    def pick_all(k, carry):
        isel_ref[pl.ds(pl.multiple_of(k * NNZ, NNZ), NNZ), :] = pick(table_ref, map_ref, k, line_ref)
        return carry

    lax.fori_loop(0, map_ref.shape[0], pick_all, 0)


def gain_kernel(core_ref, psel_ref, full_ref, mine_ref, theirs_ref, params_ref, out_ref, maps_ref, cols_ref):
    @pl.when(pl.program_id(0) == 0)
    def _():
        def place(r, value):
            pad = jnp.zeros((MP - M, MP), f32)
            for n, part in enumerate(split3(value)):
                maps_ref[r, n * MP:(n + 1) * MP, :] = jnp.concatenate([part, pad], axis=0).astype(bf16)

        place(0, full_ref[...])

        def place_both(r, carry):
            place(1 + r, mine_ref[r])
            place(SYS + r, theirs_ref[r])
            return carry

        lax.fori_loop(0, SYS - 1, place_both, 0)

    x = psel_ref[...]
    sd = x[:, M:M + 1].astype(f32)
    weight = 1.0 / (sd * sd)

    x3 = jnp.concatenate([x, x, x], axis=1)

    def column(r, carry):
        total = dot(x3, maps_ref[r])
        total = (total * weight).astype(bf16)
        for g in range(GROUP):
            cols_ref[g, pl.ds(pl.multiple_of(r * NNZ, NNZ), NNZ), :] = total[g * NNZ:(g + 1) * NNZ]
        return carry

    lax.fori_loop(0, MAPS, column, 0, unroll=True)

    def gains(g, carry):
        at = pl.ds(pl.multiple_of(g * BLK, BLK), BLK)
        cells = jnp.concatenate([params_ref[0, :, at], params_ref[1, :, at]], axis=1)
        every = dot(cols_ref[g][:, :M], cells)
        full = every[:NNZ]
        spread = jnp.zeros_like(full)
        for r in range(1, MAPS):
            off = every[r * NNZ:(r + 1) * NNZ] - full
            spread = spread + off * off
        squared = full * full
        out_ref[g] = (squared / (squared + spread * (1.0 / NB) + screen_floor) * full).astype(bf16)
        return carry

    lax.fori_loop(0, GROUP, gains, 0, unroll=4)


def change_kernel(half_ref, isel_ref, screened_ref, params_ref, *rest):
    out_ref = rest[-1]
    for g in range(GROUP):
        change = lax.dot_general(
            isel_ref[g * NNZ:(g + 1) * NNZ, :], screened_ref[g], (((0,), (0,)), ((), ())), preferred_element_type=f32
        )
        at = slice(g * BLK, (g + 1) * BLK)
        for p in range(2):
            out_ref[p, :, at] = params_ref[p, :, at].astype(f32) + change[:M, p * BLK:(p + 1) * BLK]


vmem = pl.BlockSpec(memory_space=pltpu.VMEM)
smem = pl.BlockSpec(memory_space=pltpu.SMEM)
limit = pltpu.CompilerParams(vmem_limit_bytes=56 * 1024 * 1024)


def pack(core, predicted, perturbation, observed, obs_sd, slabs):
    whole = jax.ShapeDtypeStruct((slabs, ROWS, BLK), bf16)
    return pl.pallas_call(
        pack_kernel,
        out_shape=(whole, whole),
        in_specs=[smem, vmem, vmem, vmem, vmem],
        out_specs=(vmem, vmem),
        compiler_params=limit,
        name="pack",
    )(core, predicted, perturbation, observed[None], obs_sd[None])


def make_maps(core, block_map, own, other, members):
    blocks = block_map.shape[0]
    data = own.shape[0] * BLK
    return pl.pallas_call(
        map_kernel,
        out_shape=(
            jax.ShapeDtypeStruct((M, MP), f32),
            jax.ShapeDtypeStruct((SYS - 1, M, MP), f32),
            jax.ShapeDtypeStruct((blocks // 2 * NNZ, MP), bf16),
        ),
        in_specs=[smem, smem, vmem, vmem, vmem],
        out_specs=(vmem, vmem, vmem),
        scratch_shapes=[
            pltpu.VMEM((data, MP), bf16),
            pltpu.VMEM((3, ROWS_M, data), bf16),
            pltpu.VMEM((2 * data, BLK), f32),
            pltpu.VMEM((2 * NNZ, BLK), f32),
        ] + [pltpu.VMEM((M, MP), f32)] * SYS,
        compiler_params=limit,
        cost_estimate=pl.CostEstimate(flops=20_000_000_000, bytes_accessed=8_000_000, transcendentals=0),
        name="maps",
    )(core, block_map, own, other, members)


def select(core, block_map, own, other):
    blocks = block_map.shape[0]
    data = own.shape[0] * BLK
    return pl.pallas_call(
        select_kernel,
        out_shape=jax.ShapeDtypeStruct((blocks * NNZ, MP), bf16),
        in_specs=[smem, smem, vmem, vmem],
        out_specs=vmem,
        scratch_shapes=[pltpu.VMEM((2 * data, BLK), f32), pltpu.VMEM((2 * NNZ, BLK), f32)],
        compiler_params=limit,
        cost_estimate=pl.CostEstimate(flops=10_000_000_000, bytes_accessed=8_000_000, transcendentals=0),
        name="select",
    )(core, block_map, own, other)


def make_screened(core, psel, full, mine, theirs, params):
    blocks = params.shape[2] // BLK // 2
    steps = blocks // GROUP
    return pl.pallas_call(
        gain_kernel,
        out_shape=jax.ShapeDtypeStruct((blocks, NNZ, 2 * BLK), bf16),
        grid_spec=pltpu.PrefetchScalarGridSpec(
            num_scalar_prefetch=1,
            grid=(steps,),
            in_specs=[
                pl.BlockSpec((GROUP * NNZ, MP), lambda i, c: (i, 0)),
                pl.BlockSpec((M, MP), lambda i, c: (0, 0)),
                pl.BlockSpec((SYS - 1, M, MP), lambda i, c: (0, 0, 0)),
                pl.BlockSpec((SYS - 1, M, MP), lambda i, c: (0, 0, 0)),
                pl.BlockSpec((2, M, GROUP * BLK), lambda i, c: (0, 0, c[0] * steps + i)),
            ],
            out_specs=pl.BlockSpec((GROUP, NNZ, 2 * BLK), lambda i, c: (i, 0, 0)),
            scratch_shapes=[
                pltpu.VMEM((MAPS, 3 * MP, MP), bf16),
                pltpu.VMEM((GROUP, MAPS * NNZ, MP), bf16),
            ],
        ),
        compiler_params=limit,
        cost_estimate=pl.CostEstimate(flops=20_000_000_000, bytes_accessed=8_000_000, transcendentals=0),
        name="gains",
    )(core, psel, full, mine, theirs, params)


def update(half, isel, screened, params, so_far=None):
    blocks = params.shape[2] // BLK // 2
    steps = blocks // GROUP
    cells = pl.BlockSpec((2, M, GROUP * BLK), lambda i, c: (0, 0, c[0] * steps + i))
    in_specs = [
        pl.BlockSpec((GROUP * NNZ, MP), lambda i, c: (c[0] * steps + i, 0)),
        pl.BlockSpec((GROUP, NNZ, 2 * BLK), lambda i, c: (i, 0, 0)),
        cells,
    ]
    operands = (half, isel, screened, params)
    if so_far is not None:
        in_specs.append(pl.BlockSpec(memory_space=pl.ANY))
        operands = operands + (so_far,)
    return pl.pallas_call(
        change_kernel,
        out_shape=jax.ShapeDtypeStruct(params.shape, f32),
        grid_spec=pltpu.PrefetchScalarGridSpec(
            num_scalar_prefetch=1, grid=(steps,), in_specs=in_specs, out_specs=cells
        ),
        input_output_aliases={} if so_far is None else {4: 0},
        compiler_params=limit,
        cost_estimate=pl.CostEstimate(flops=5_000_000_000, bytes_accessed=10_000_000, transcendentals=0),
        name="change",
    )(*operands)


def on_device(params, predicted, perturbation, observed, obs_sd, members, block_map):
    boot = lax.axis_index("boot")
    core = lax.rem(boot, 2)
    core_arg = core.reshape(1).astype(jnp.int32)
    slabs = lax.axis_size("slab")
    pair = [(i, i ^ 1) for i in range(4)]
    far = [(i, i ^ 2) for i in range(4)]

    def exchange(whole):
        own = lax.all_to_all(whole, "slab", 0, 0)
        return own, lax.ppermute(own, "boot", pair)

    far_members = lax.ppermute(members, "boot", far)
    whole, innov_whole = pack(core_arg, predicted, perturbation, observed, obs_sd, slabs)
    whole, far_members = lax.optimization_barrier((whole, far_members))
    every = jnp.arange(M, dtype=jnp.int32)[None]
    lists = jnp.concatenate([every, members, far_members], axis=0)
    lists = jnp.pad(lists, ((0, 16 - SYS), (0, MP - M)), constant_values=-1)

    own, other = exchange(whole)
    innov_whole, other = lax.optimization_barrier((innov_whole, other))
    iown, iother = exchange(innov_whole)

    full, mine, psel = make_maps(core_arg, block_map, own, other, lists)
    late_map, mine = lax.optimization_barrier((block_map, mine))
    theirs = lax.ppermute(mine, "boot", pair)
    isel = select(core_arg, late_map, iown, iother)
    screened = make_screened(core_arg, psel, full, mine, theirs, params)
    screened_other = lax.ppermute(screened, "boot", pair)
    partial_out = update(core_arg, isel, screened, params)
    return update(1 - core_arg, isel, screened_other, params, partial_out)


def solution(mesh):
    return jax.shard_map(
        on_device,
        mesh=mesh,
        in_specs=(
            P(None, None, "slab"),
            P(None, "slab"),
            P(None, "slab"),
            P("slab"),
            P("slab"),
            P("boot", None),
            P("slab", None),
        ),
        out_specs=P(None, None, "slab"),
        check_vma=False,
    )
```

time: 182 us -> 133 us (0.73)
  Pallas kernels: 125 us -> 77.1 us
  waiting for transfers between devices: 13.7 us -> 16.7 us
  other arithmetic: 3.52 us -> 0.72 us
    pallas_call x1, Pallas kernels: 55.6 us -> 28.4 us  [make_maps(): pl.pallas_call(map_kernel, out_shape=(jax.ShapeDtypeStruct((M, MP), f32),...]
    pallas_call x1, Pallas kernels: 42.4 us -> 25.2 us  [make_screened(): pl.pallas_call(gain_kernel, out_shape=jax.ShapeDtypeStruct((blocks, NNZ,...]
    all_to_all x1, waiting for transfers between devices: 0.68 us -> 15.4 us  [exchange(): own = lax.all_to_all(whole, 'slab', 0, 0)]
    ppermute x1, waiting for transfers between devices: 10.5 us -> 0.09 us  [on_device(): far_members = lax.ppermute(members, 'boot', far)]
    pallas_call x1 -> x2, Pallas kernels: 14.4 us -> 10.9 us  [the longest x1 8.82 us: select(): pl.pallas_call(select_kernel, out_shape=jax.ShapeDtypeStruct((blocks * NN...]
    convert_element_type x3 -> x0, other arithmetic: 2.09 us -> none  [the longest x1 0.77 us: on_device(): (observed.astype(f32) + noise * perturbation.astype(f32) - predicted.asty...]
  transfers between devices with their start and end apart: 6 -> 6, of which waited for: 3 -> 3; matrix products, arithmetic and copies ran while one was open for 1% -> 1% of each run, Pallas kernels for 42% -> 32%
where the time goes in v2:
time: 133 us; the launch traced here: 131 us
  Pallas kernels  77.1 us (58%)
  blocking collectives  23.6 us (18%)
  waiting for transfers between devices  16.7 us (13%)
  starting transfers between devices  8.16 us (6%)
  local copies, waits for them, and re-layouts  4.66 us (4%)
    pallas_call x1, Pallas kernels, make_maps(): pl.pallas_call(map_kernel, out_shape=(jax.ShapeDtypeStruct((M, MP), f32),...  28.4 us
    pallas_call x1, Pallas kernels, make_screened(): pl.pallas_call(gain_kernel, out_shape=jax.ShapeDtypeStruct((blocks, NNZ,...  25.2 us
    all_to_all x1, blocking collectives, exchange(): own = lax.all_to_all(whole, 'slab', 0, 0)  23.6 us
    all_to_all x1, waiting for transfers between devices, exchange(): own = lax.all_to_all(whole, 'slab', 0, 0)  15.4 us
    pallas_call x2, Pallas kernels, update(): pl.pallas_call(change_kernel, out_shape=jax.ShapeDtypeStruct(params.shape...  12.6 us
    pallas_call x1, Pallas kernels, select(): pl.pallas_call(select_kernel, out_shape=jax.ShapeDtypeStruct((blocks * NN...  8.82 us
    all_to_all x1, starting transfers between devices, exchange(): own = lax.all_to_all(whole, 'slab', 0, 0)  4.43 us
    unnamed x12, local copies, waits for them, and re-layouts  4.04 us
  transfers between devices with their start and end apart: 6, of which 3 were waited for; matrix products, arithmetic and copies ran while one was open for 1% of the time, Pallas kernels for 32%

profile of v2, /device:TPU:0, one launch (start us, length us, event | category | flops | bytes accessed | tf_op | source)
XLA Modules:
  0.0 131.0 jit_solution(1915106055442946597)
XLA Ops:
  0.0 3.1 %collective-permute-start = (s32[4,200]{1,0:T(4,128)}, s32[4,200]{1,0:T(4,128)S(1)}, u32[]{:S(2)}, u32[]{:S(2)}) collective-permute-start(s32[4,200]{1,0:T(4,128)} %param.12), channel_id=1, source_target_pairs={{0,64},{32,96},{64,0},{96,32},{1,65},{33,97},{65,1},{97,33},{2,66}... | collective-permute-start | bytes 9608 | tf_op jit(solution)/shard_map/ppermute | solution.py:426
  3.1 2.1 %pack.1 = (bf16[32,112,128]{2,1,0:T(8,128)(2,1)}, bf16[32,112,128]{2,1,0:T(8,128)(2,1)}) custom-call(s32[1]{0:T(128)} %bitcast.core_ref.half_ref, bf16[200,128]{1,0:T(8,128)(2,1)} %pred_ref.1, bf16[200,128]{1,0:T(8,128)(2,1)} %pert_ref.1, bf16[1,128]{1,0:T(2,128)(2,1)} %bitcast.3, bf16[1,128]{1,0:T(2,128)(2,1)} %bitcast.4), custom_call_target="tpu_custom_call" | custom-call | tf_op jit(solution)/shard_map/pack/pallas_call | solution.py:311
  5.2 0.1 collective-permute-done
  5.3 23.6 %all_to_all.10.own_ref = bf16[32,112,128]{2,1,0:T(8,128)(2,1)S(1)} all-to-all(bf16[32,112,128]{2,1,0:T(8,128)(2,1)} %get-tuple-element.17), channel_id=1, replica_groups=mesh['boot'=4,'slab'=32] {'slab'}, dimensions={0} | all-to-all | bytes 1835008 | tf_op jit(solution)/shard_map/all_to_all | solution.py:423
  28.9 0.0 copy-start.2
  28.9 0.0 collective-permute-start.1
  28.9 0.7 pad_add_fusion
  29.6 0.6 pad.4.members_ref
  30.2 1.1 collective-permute-done.1.other_ref
  31.4 0.0 copy-start.5
  31.4 0.0 copy-done.2
  31.4 0.9 copy-done.5
  32.3 28.4 %maps.1 = (f32[200,256]{1,0:T(8,128)}, f32[8,200,256]{2,1,0:T(8,128)}, bf16[2048,256]{1,0:T(8,128)(2,1)}) custom-call(s32[1]{0:T(128)} %bitcast.core_ref.half_ref, s32[64,64]{1,0:T(8,128)} %map_ref.2, bf16[32,112,128]{2,1,0:T(8,128)(2,1)} %copy-done.2, bf16[32,112,128]{2,1,0:T(8,128)(2,1)} %copy-done.5, s32[16,256]{1,0:T(8,128)} %pad.4.members_ref), custom_call_target="tpu_custom_call" | custom-call | flops 20000000000 | bytes 8000000 | tf_op jit(solution)/shard_map/maps/pallas_call | solution.py:324
  60.7 0.1 collective-permute-start.3
  60.8 4.4 %all-to-all-start.1 = ((bf16[32,112,128]{2,1,0:T(8,128)(2,1)}), bf16[32,112,128]{2,1,0:T(8,128)(2,1)S(1)}, u32[]{:S(2)}, u32[]{:S(2)}) async-start(bf16[32,112,128]{2,1,0:T(8,128)(2,1)} %get-tuple-element.23), calls=%async_computation.1 | async-start | bytes 1835008 | tf_op jit(solution)/shard_map/all_to_all | solution.py:423
  65.3 15.4 %all-to-all-done.1.own_ref = bf16[32,112,128]{2,1,0:T(8,128)(2,1)S(1)} async-done(((bf16[32,112,128]{2,1,0:T(8,128)(2,1)}), bf16[32,112,128]{2,1,0:T(8,128)(2,1)S(1)}, u32[]{:S(2)}, u32[]{:S(2)}) %all-to-all-start.1) | async-done | bytes 917536 | tf_op jit(solution)/shard_map/all_to_all | solution.py:423
  80.7 0.0 copy-start.1
  80.7 0.0 collective-permute-start.2
  80.7 0.0 collective-permute-done.3.theirs_ref
  80.7 0.0 copy-start.3
  80.7 1.2 copy-done.3
  81.9 25.2 %gains.1.screened_ref = bf16[32,64,256]{2,1,0:T(8,128)(2,1)} custom-call(s32[1]{0:T(128)} %bitcast.core_ref.half_ref, bf16[2048,256]{1,0:T(8,128)(2,1)} %get-tuple-element.24.psel_ref, f32[200,256]{1,0:T(8,128)} %get-tuple-element.25.full_ref, f32[8,200,256]{2,1,0:T(8,128)} %get-tuple-element.26.mine_ref, f32[8,200,256]{2,1,0:T(8,128)} %copy-done.3, ...), custom_call_target="tpu_custom_call" | custom-call | flops 20000000000 | bytes 8000000 | tf_op jit(solution)/shard_map/gains/pallas_call | solution.py:363
  107.1 0.0 copy-done.1
  107.1 0.5 collective-permute-start.4
  107.6 0.0 collective-permute-done.2.other_ref
  107.6 0.0 copy-start.4
  107.6 0.9 copy-done.4
  108.5 8.8 %select.4.isel_ref = bf16[4096,256]{1,0:T(8,128)(2,1)} custom-call(s32[1]{0:T(128)} %bitcast.core_ref.half_ref, s32[64,64]{1,0:T(8,128)} %map_ref.2, bf16[32,112,128]{2,1,0:T(8,128)(2,1)} %copy-done.1, bf16[32,112,128]{2,1,0:T(8,128)(2,1)} %copy-done.4), custom_call_target="tpu_custom_call" | custom-call | flops 10000000000 | bytes 8000000 | tf_op jit(solution)/shard_map/select/pallas_call | solution.py:348
  117.3 6.3 %change.2.rest_0_ = f32[2,200,8192]{2,1,0:T(8,128)} custom-call(s32[1]{0:T(128)} %bitcast.core_ref.half_ref, bf16[4096,256]{1,0:T(8,128)(2,1)} %select.4.isel_ref, bf16[32,64,256]{2,1,0:T(8,128)(2,1)} %gains.1.screened_ref, bf16[2,200,8192]{2,1,0:T(8,128)(2,1)} %params_ref.5), custom_call_target="tpu_custom_call" | custom-call | flops 5000000000 | bytes 10000000 | tf_op jit(solution)/shard_map/change/pallas_call | solution.py:401
  123.7 0.0 collective-permute-done.4.screened_ref
  123.7 0.0 copy-start
  123.7 1.0 copy-done
  124.6 6.3 %change.3 = f32[2,200,8192]{2,1,0:T(8,128)} custom-call(s32[1]{0:T(128)S(6)} %sub.3.half_ref, bf16[4096,256]{1,0:T(8,128)(2,1)} %select.4.isel_ref, bf16[32,64,256]{2,1,0:T(8,128)(2,1)} %copy-done, bf16[2,200,8192]{2,1,0:T(8,128)(2,1)} %params_ref.5, f32[2,200,8192]{2,1,0:T(8,128)} %change.2.rest_0_), custom_call_target="tpu_custom_call", output_to_operand_aliasing={{}: (4, {})} | custom-call | flops 5000000000 | bytes 10000000 | tf_op jit(solution)/shard_map/change/pallas_call | solution.py:401
  (1 shorter events, 0.0 us)
Async XLA Ops:
  0.0 5.3 %collective-permute-start = (s32[4,200]{1,0:T(4,128)}, s32[4,200]{1,0:T(4,128)S(1)}, u32[]{:S(2)}, u32[]{:S(2)}) collective-permute-start(s32[4,200]{1,0:T(4,128)} %param.12), channel_id=1, source_target_pairs={{0,64},{32,96},{64,0},{96,32},{1,65},{33,97},{65,1},{97,33},{2,66}... | collective-permute-start | bytes 9608 | tf_op jit(solution)/shard_map/ppermute | solution.py:426
  28.9 2.5 %copy-start.2 = (bf16[32,112,128]{2,1,0:T(8,128)(2,1)}, bf16[32,112,128]{2,1,0:T(8,128)(2,1)S(1)}, u32[]{:S(2)}) copy-start(bf16[32,112,128]{2,1,0:T(8,128)(2,1)S(1)} %all_to_all.10.own_ref) | copy-start | bytes 2752516
  28.9 2.5 %collective-permute-start.1 = (bf16[32,112,128]{2,1,0:T(8,128)(2,1)S(1)}, bf16[32,112,128]{2,1,0:T(8,128)(2,1)S(1)}, u32[]{:S(2)}, u32[]{:S(2)}) collective-permute-start(bf16[32,112,128]{2,1,0:T(8,128)(2,1)S(1)} %all_to_all.10.own_ref), channel_id=1, source_target_pairs={{0,32},{32,0},{64,96},{96,64},{1,33},{33,1},{65,97},{97,65},{2,34}... | collective-permute-start | bytes 2752520 | tf_op jit(solution)/shard_map/ppermute | solution.py:424
  31.4 0.9 copy-start.5
  60.7 20.0 %collective-permute-start.3 = (f32[8,200,256]{2,1,0:T(8,128)}, f32[8,200,256]{2,1,0:T(8,128)S(1)}, u32[]{:S(2)}, u32[]{:S(2)}) collective-permute-start(f32[8,200,256]{2,1,0:T(8,128)} %get-tuple-element.26.mine_ref), channel_id=1, source_target_pairs={{0,32},{32,0},{64,96},{96,64},{1,33},{33,1},{65,97},{97,65},{2,34}... | collective-permute-start | bytes 4915208 | tf_op jit(solution)/shard_map/ppermute | solution.py:439
  60.8 19.9 %all-to-all-start.1 = ((bf16[32,112,128]{2,1,0:T(8,128)(2,1)}), bf16[32,112,128]{2,1,0:T(8,128)(2,1)S(1)}, u32[]{:S(2)}, u32[]{:S(2)}) async-start(bf16[32,112,128]{2,1,0:T(8,128)(2,1)} %get-tuple-element.23), calls=%async_computation.1 | async-start | bytes 1835008 | tf_op jit(solution)/shard_map/all_to_all | solution.py:423
  80.7 26.4 %copy-start.1 = (bf16[32,112,128]{2,1,0:T(8,128)(2,1)}, bf16[32,112,128]{2,1,0:T(8,128)(2,1)S(1)}, u32[]{:S(2)}) copy-start(bf16[32,112,128]{2,1,0:T(8,128)(2,1)S(1)} %all-to-all-done.1.own_ref) | copy-start | bytes 2752516
  80.7 26.9 %collective-permute-start.2 = (bf16[32,112,128]{2,1,0:T(8,128)(2,1)S(1)}, bf16[32,112,128]{2,1,0:T(8,128)(2,1)S(1)}, u32[]{:S(2)}, u32[]{:S(2)}) collective-permute-start(bf16[32,112,128]{2,1,0:T(8,128)(2,1)S(1)} %all-to-all-done.1.own_ref), channel_id=1, source_target_pairs={{0,32},{32,0},{64,96},{96,64},{1,33},{33,1},{65,97},{97,65},{2,34}... | collective-permute-start | bytes 2752520 | tf_op jit(solution)/shard_map/ppermute | solution.py:424
  80.7 1.2 copy-start.3
  107.1 16.5 %collective-permute-start.4 = (bf16[32,64,256]{2,1,0:T(8,128)(2,1)}, bf16[32,64,256]{2,1,0:T(8,128)(2,1)S(1)}, u32[]{:S(2)}, u32[]{:S(2)}) collective-permute-start(bf16[32,64,256]{2,1,0:T(8,128)(2,1)} %gains.1.screened_ref), channel_id=1, source_target_pairs={{0,32},{32,0},{64,96},{96,64},{1,33},{33,1},{65,97},{97,65},{2,34}... | collective-permute-start | bytes 3145736 | tf_op jit(solution)/shard_map/ppermute | solution.py:442
  107.6 0.9 copy-start.4
  123.7 1.0 copy-start

commit v3 on v2

--- a/solution.py
+++ b/solution.py
@@ -13,13 +13,10 @@
 BLK = 128
 NNZ = 64
 MP = 256
-HALF = 104
-SHIFT = 96
-ROWS = 112
+ROWS = 208
 PIV = 40
 SYS = 9
 PACK = 3
-ROWS_M = 208
 MAPS = 17
 GROUP = 8
 
@@ -56,33 +53,33 @@
     return jnp.dot(a, b, preferred_element_type=f32)
 
 
-def counts(members_ref, s):
-    row = members_ref[pl.ds(s, 1), :]
-    hit = jnp.where(iota((M, MP), 0) == row, 1.0, 0.0)
-    down = jnp.sum(hit, axis=1, keepdims=True)
-    across = jnp.sum(jnp.where(iota((M, MP), 0) == iota((M, MP), 1), down, 0.0), axis=0, keepdims=True)
-    return jnp.sqrt(down), jnp.sqrt(across)
-
-
-def pack_kernel(core_ref, pred_ref, pert_ref, obs_ref, sd_ref, ens_ref, innov_ref):
-    core = core_ref[0]
+def scaling(listed):
+    lane = iota((M, MP), 1)
+    if listed is None:
+        down = jnp.ones((M, 1), f32)
+        across = jnp.where(lane[:1] < M, 1.0, 0.0)
+    else:
+        down = jnp.sqrt(jnp.sum(jnp.where(iota((M, M), 0) == listed, 1.0, 0.0), axis=1, keepdims=True))
+        across = jnp.sum(jnp.where(iota((M, MP), 0) == lane, down, 0.0), axis=0, keepdims=True)
+    root = 1.0 / math.sqrt(M)
+    return down * (1.0 / (M - 1)) * across, down * root, across * root
+
+
+def pack_kernel(core_ref, pred_ref, pert_ref, obs_ref, sd_ref, out_ref):
     sd = sd_ref[...].astype(f32)
     ens = pred_ref[...].astype(f32)
     innov = obs_ref[...].astype(f32) + sd * pert_ref[...].astype(f32) - ens
-    tail = jnp.concatenate([sd, jnp.zeros((ROWS - HALF - 1, BLK), f32)], axis=0)
-    for rows, out_ref in ((ens, ens_ref), (innov, innov_ref)):
-        part = jnp.where(core == 0, rows[:HALF], rows[SHIFT:SHIFT + HALF])
-        part = jnp.concatenate([part, tail], axis=0).astype(bf16)
-        for i in range(out_ref.shape[0]):
-            out_ref[i] = part
-
-
-def members_first(core, own, other):
-    first = jnp.where(core == 0, own, other)
-    second = jnp.where(core == 0, other, own)
-    low = jnp.concatenate([first[:HALF], second[HALF - SHIFT:BLK - SHIFT]], axis=0)
-    high = jnp.concatenate([second[BLK - SHIFT:HALF], own[HALF:ROWS], jnp.zeros((MP - M - (ROWS - HALF), BLK), f32)], axis=0)
-    return low, high
+    rows = jnp.where(core_ref[0] == 0, ens, innov)
+    tail = jnp.concatenate([sd, jnp.zeros((ROWS - M - 1, BLK), f32)], axis=0)
+    part = jnp.concatenate([rows, tail], axis=0).astype(bf16)
+    for i in range(out_ref.shape[0]):
+        out_ref[i] = part
+
+
+def chunk_rows(keep_own, own_ref, other_ref, i):
+    rows = jnp.where(keep_own, own_ref[i].astype(f32), other_ref[i].astype(f32))
+    high = jnp.concatenate([rows[BLK:], jnp.zeros((MP - ROWS, BLK), f32)], axis=0)
+    return rows, rows[:BLK], high
 
 
 def fill_table(t_ref, i, low, high):
@@ -98,16 +95,15 @@
     return jnp.concatenate(both, axis=1).astype(bf16)
 
 
-def map_kernel(core_ref, map_ref, own_ref, other_ref, members_ref, full_ref, res_ref, psel_ref, ens_ref, parts_ref, table_ref, line_ref, *sys_refs):
+def map_kernel(core_ref, map_ref, own_ref, other_ref, near_ref, far_ref, full_ref, res_ref, psel_ref, ens_ref, parts_ref, table_ref, line_ref, scale_ref, *sys_refs):
     core = core_ref[0]
+    near = near_ref.shape[0]
     blocks = map_ref.shape[0]
 
     def chunk(i, carry):
-        own = own_ref[i].astype(f32)
-        low, high = members_first(core, own, other_ref[i].astype(f32))
-        sd = own[HALF:HALF + 1]
+        rows, low, high = chunk_rows(core == 0, own_ref, other_ref, i)
+        sd = rows[M:M + 1]
         at = pl.ds(pl.multiple_of(i * BLK, BLK), BLK)
-        rows = jnp.concatenate([low, high[:ROWS_M - BLK]], axis=0)
         for n, part in enumerate(split3(rows * (1.0 / (sd * sd)))):
             parts_ref[n, :, at] = part.astype(bf16)
         low, high = low.T, high.T
@@ -133,10 +129,12 @@
     row = iota((M, MP), 0)
     lane = iota((M, MP), 1)
     for s in range(SYS):
-        down, across = counts(members_ref, s)
-        h = gram * (down * (1.0 / (M - 1))) * across
-        ud = down * (1.0 / math.sqrt(M))
-        ua = across * (1.0 / math.sqrt(M))
+        listed = None
+        if s:
+            listed = near_ref[s - 1:s, :] if s <= near else far_ref[s - 1 - near:s - near, :]
+        scale, ud, ua = scaling(listed)
+        scale_ref[s] = scale
+        h = gram * scale
         hu = jnp.sum(h * ua, axis=1, keepdims=True)
         uh = jnp.sum(h * ud, axis=0, keepdims=True)
         uhu = jnp.sum(hu * ud, axis=0, keepdims=True)
@@ -216,9 +214,8 @@
     lax.fori_loop(0, M // PIV, panel_step, 0)
 
     for s in range(SYS):
-        down, across = counts(members_ref, s)
-        both = down * across
-        value = (-sys_refs[s][...] - both * (1.0 / M)) * (both * (1.0 / (M - 1)))
+        scale = scale_ref[s]
+        value = (-sys_refs[s][...] - scale * ((M - 1) / M)) * scale
         if s == 0:
             full_ref[...] = value
         else:
@@ -229,7 +226,7 @@
     core = core_ref[0]
 
     def chunk(i, carry):
-        low, high = members_first(core, own_ref[i].astype(f32), other_ref[i].astype(f32))
+        _, low, high = chunk_rows(core == 1, own_ref, other_ref, i)
         fill_table(table_ref, i, low.T, high.T)
         return carry
 
@@ -310,15 +307,15 @@
     whole = jax.ShapeDtypeStruct((slabs, ROWS, BLK), bf16)
     return pl.pallas_call(
         pack_kernel,
-        out_shape=(whole, whole),
+        out_shape=whole,
         in_specs=[smem, vmem, vmem, vmem, vmem],
-        out_specs=(vmem, vmem),
+        out_specs=vmem,
         compiler_params=limit,
         name="pack",
     )(core, predicted, perturbation, observed[None], obs_sd[None])
 
 
-def make_maps(core, block_map, own, other, members):
+def make_maps(core, block_map, own, other, near, far):
     blocks = block_map.shape[0]
     data = own.shape[0] * BLK
     return pl.pallas_call(
@@ -328,18 +325,19 @@
             jax.ShapeDtypeStruct((SYS - 1, M, MP), f32),
             jax.ShapeDtypeStruct((blocks // 2 * NNZ, MP), bf16),
         ),
-        in_specs=[smem, smem, vmem, vmem, vmem],
+        in_specs=[smem, smem, vmem, vmem, vmem, vmem],
         out_specs=(vmem, vmem, vmem),
         scratch_shapes=[
             pltpu.VMEM((data, MP), bf16),
-            pltpu.VMEM((3, ROWS_M, data), bf16),
+            pltpu.VMEM((3, ROWS, data), bf16),
             pltpu.VMEM((2 * data, BLK), f32),
             pltpu.VMEM((2 * NNZ, BLK), f32),
+            pltpu.VMEM((SYS, M, MP), f32),
         ] + [pltpu.VMEM((M, MP), f32)] * SYS,
         compiler_params=limit,
         cost_estimate=pl.CostEstimate(flops=20_000_000_000, bytes_accessed=8_000_000, transcendentals=0),
         name="maps",
-    )(core, block_map, own, other, members)
+    )(core, block_map, own, other, near, far)
 
 
 def select(core, block_map, own, other):
@@ -419,25 +417,17 @@
     pair = [(i, i ^ 1) for i in range(4)]
     far = [(i, i ^ 2) for i in range(4)]
 
-    def exchange(whole):
-        own = lax.all_to_all(whole, "slab", 0, 0)
-        return own, lax.ppermute(own, "boot", pair)
-
     far_members = lax.ppermute(members, "boot", far)
-    whole, innov_whole = pack(core_arg, predicted, perturbation, observed, obs_sd, slabs)
+    whole = pack(core_arg, predicted, perturbation, observed, obs_sd, slabs)
     whole, far_members = lax.optimization_barrier((whole, far_members))
-    every = jnp.arange(M, dtype=jnp.int32)[None]
-    lists = jnp.concatenate([every, members, far_members], axis=0)
-    lists = jnp.pad(lists, ((0, 16 - SYS), (0, MP - M)), constant_values=-1)
-
-    own, other = exchange(whole)
-    innov_whole, other = lax.optimization_barrier((innov_whole, other))
-    iown, iother = exchange(innov_whole)
-
-    full, mine, psel = make_maps(core_arg, block_map, own, other, lists)
+    own = lax.all_to_all(whole, "slab", 0, 0)
+    other = lax.ppermute(own, "boot", pair)
+
+    full, mine, psel = make_maps(core_arg, block_map, own, other, members, far_members)
     late_map, mine = lax.optimization_barrier((block_map, mine))
     theirs = lax.ppermute(mine, "boot", pair)
-    isel = select(core_arg, late_map, iown, iother)
+    isel = select(core_arg, late_map, own, other)
+    isel, psel = lax.optimization_barrier((isel, psel))
     screened = make_screened(core_arg, psel, full, mine, theirs, params)
     screened_other = lax.ppermute(screened, "boot", pair)
     partial_out = update(core_arg, isel, screened, params)

time: 133 us -> 122 us (0.917)
  waiting for transfers between devices: 16.7 us -> 3.68 us
  blocking collectives: 23.6 us -> 32.2 us
  starting transfers between devices: 8.16 us -> 3.62 us
    all_to_all x1 -> x0, waiting for transfers between devices: 15.4 us -> none  [exchange(): own = lax.all_to_all(whole, 'slab', 0, 0)]
    all_to_all x1, blocking collectives: 23.6 us -> 32.2 us  [on_device(): own = lax.all_to_all(whole, 'slab', 0, 0)]
    all_to_all x1 -> x0, starting transfers between devices: 4.43 us -> none  [exchange(): own = lax.all_to_all(whole, 'slab', 0, 0)]
    ppermute x2 -> x1, waiting for transfers between devices: 1.13 us -> 3.59 us  [on_device(): other = lax.ppermute(own, 'boot', pair)]
    unnamed x12 -> x10, local copies, waits for them, and re-layouts: 4.04 us -> 3.34 us
  transfers between devices with their start and end apart: 6 -> 4, of which waited for: 3 -> 2; matrix products, arithmetic and copies ran while one was open for 1% -> 0% of each run, Pallas kernels for 32% -> 15%
where the time goes in v3:
time: 122 us; the launch traced here: 120 us
  Pallas kernels  77.5 us (64%)
  blocking collectives  32.2 us (26%)
  waiting for transfers between devices  3.68 us (3%)
  starting transfers between devices  3.62 us (3%)
  local copies, waits for them, and re-layouts  3.34 us (3%)
    all_to_all x1, blocking collectives, on_device(): own = lax.all_to_all(whole, 'slab', 0, 0)  32.2 us
    pallas_call x1, Pallas kernels, make_maps(): pl.pallas_call(map_kernel, out_shape=(jax.ShapeDtypeStruct((M, MP), f32),...  28.2 us
    pallas_call x1, Pallas kernels, make_screened(): pl.pallas_call(gain_kernel, out_shape=jax.ShapeDtypeStruct((blocks, NNZ,...  25.2 us
    pallas_call x2, Pallas kernels, update(): pl.pallas_call(change_kernel, out_shape=jax.ShapeDtypeStruct(params.shape...  12.6 us
    pallas_call x1, Pallas kernels, select(): pl.pallas_call(select_kernel, out_shape=jax.ShapeDtypeStruct((blocks * NN...  9.33 us
    ppermute x1, waiting for transfers between devices, on_device(): other = lax.ppermute(own, 'boot', pair)  3.59 us
    unnamed x10, local copies, waits for them, and re-layouts  3.34 us
    ppermute x1, starting transfers between devices, on_device(): far_members = lax.ppermute(members, 'boot', far)  3.11 us
  transfers between devices with their start and end apart: 4, of which 2 were waited for; matrix products, arithmetic and copies ran while one was open for 0% of the time, Pallas kernels for 15%

profile of v3, /device:TPU:0, one launch (start us, length us, event | category | flops | bytes accessed | tf_op | source)
XLA Modules:
  0.0 120.3 jit_solution(13406740426469236163)
XLA Ops:
  0.0 3.1 %collective-permute-start = (s32[4,200]{1,0:T(4,128)}, s32[4,200]{1,0:T(4,128)S(1)}, u32[]{:S(2)}, u32[]{:S(2)}) collective-permute-start(s32[4,200]{1,0:T(4,128)} %near_ref.1), channel_id=1, source_target_pairs={{0,64},{32,96},{64,0},{96,32},{1,65},{33,97},{65,1},{97,33},{2,66}... | collective-permute-start | bytes 9608 | tf_op jit(solution)/shard_map/ppermute | solution.py:420
  3.1 2.1 %pack.1 = bf16[32,208,128]{2,1,0:T(8,128)(2,1)} custom-call(s32[1]{0:T(128)} %bitcast.core_ref.half_ref, bf16[200,128]{1,0:T(8,128)(2,1)} %pred_ref.1, bf16[200,128]{1,0:T(8,128)(2,1)} %pert_ref.1, bf16[1,128]{1,0:T(2,128)(2,1)} %bitcast.3, bf16[1,128]{1,0:T(2,128)(2,1)} %bitcast.4), custom_call_target="tpu_custom_call" | custom-call | tf_op jit(solution)/shard_map/pack/pallas_call | solution.py:308
  5.2 0.1 collective-permute-done.far_ref
  5.3 0.0 copy-start.4
  5.3 32.2 %all_to_all.5.own_ref = bf16[32,208,128]{2,1,0:T(8,128)(2,1)S(1)} all-to-all(bf16[32,208,128]{2,1,0:T(8,128)(2,1)} %pack.1), channel_id=1, replica_groups=mesh['boot'=4,'slab'=32] {'slab'}, dimensions={0} | all-to-all | bytes 3407872 | tf_op jit(solution)/shard_map/all_to_all | solution.py:423
  37.5 0.0 copy-done.4
  37.5 0.0 copy-start
  37.5 0.0 collective-permute-start.1
  37.5 3.6 %collective-permute-done.1.other_ref = bf16[32,208,128]{2,1,0:T(8,128)(2,1)S(1)} collective-permute-done((bf16[32,208,128]{2,1,0:T(8,128)(2,1)S(1)}, bf16[32,208,128]{2,1,0:T(8,128)(2,1)S(1)}, u32[]{:S(2)}, u32[]{:S(2)}) %collective-permute-start.1) | collective-permute-done | bytes 1703968 | tf_op jit(solution)/shard_map/ppermute | solution.py:424
  41.1 0.0 copy-done
  41.1 0.0 copy-start.2
  41.1 1.2 copy-done.2
  42.3 28.2 %maps.1 = (f32[200,256]{1,0:T(8,128)}, f32[8,200,256]{2,1,0:T(8,128)}, bf16[2048,256]{1,0:T(8,128)(2,1)}) custom-call(s32[1]{0:T(128)} %bitcast.core_ref.half_ref, s32[64,64]{1,0:T(8,128)} %map_ref.2, bf16[32,208,128]{2,1,0:T(8,128)(2,1)} %copy-done, bf16[32,208,128]{2,1,0:T(8,128)(2,1)} %copy-done.2, s32[4,200]{1,0:T(4,128)} %near_ref.1, s32[4,200]{1,0:T(4,128)} %copy-done.4), custom_call_target="tpu_custom_call" | custom-call | flops 20000000000 | bytes 8000000 | tf_op jit(solution)/shard_map/maps/pallas_call | solution.py:321
  70.5 0.1 collective-permute-start.2
  70.6 9.3 %select.3.isel_ref = bf16[4096,256]{1,0:T(8,128)(2,1)} custom-call(s32[1]{0:T(128)} %bitcast.core_ref.half_ref, s32[64,64]{1,0:T(8,128)} %map_ref.2, bf16[32,208,128]{2,1,0:T(8,128)(2,1)} %copy-done, bf16[32,208,128]{2,1,0:T(8,128)(2,1)} %copy-done.2), custom_call_target="tpu_custom_call" | custom-call | flops 10000000000 | bytes 8000000 | tf_op jit(solution)/shard_map/select/pallas_call | solution.py:346
  79.9 0.0 collective-permute-done.2.theirs_ref
  79.9 0.0 copy-start.3
  79.9 1.2 copy-done.3
  81.1 25.2 %gains.1.screened_ref = bf16[32,64,256]{2,1,0:T(8,128)(2,1)} custom-call(s32[1]{0:T(128)} %bitcast.core_ref.half_ref, bf16[2048,256]{1,0:T(8,128)(2,1)} %get-tuple-element.20.psel_ref, f32[200,256]{1,0:T(8,128)} %get-tuple-element.21.full_ref, f32[8,200,256]{2,1,0:T(8,128)} %get-tuple-element.22.mine_ref, f32[8,200,256]{2,1,0:T(8,128)} %copy-done.3, ...), custom_call_target="tpu_custom_call" | custom-call | flops 20000000000 | bytes 8000000 | tf_op jit(solution)/shard_map/gains/pallas_call | solution.py:361
  106.3 0.4 collective-permute-start.3
  106.7 6.3 %change.2.rest_0_ = f32[2,200,8192]{2,1,0:T(8,128)} custom-call(s32[1]{0:T(128)} %bitcast.core_ref.half_ref, bf16[4096,256]{1,0:T(8,128)(2,1)} %select.3.isel_ref, bf16[32,64,256]{2,1,0:T(8,128)(2,1)} %gains.1.screened_ref, bf16[2,200,8192]{2,1,0:T(8,128)(2,1)} %params_ref.5), custom_call_target="tpu_custom_call" | custom-call | flops 5000000000 | bytes 10000000 | tf_op jit(solution)/shard_map/change/pallas_call | solution.py:399
  113.0 0.0 collective-permute-done.3.screened_ref
  113.0 0.0 copy-start.1
  113.0 1.0 copy-done.1
  114.0 6.3 %change.3 = f32[2,200,8192]{2,1,0:T(8,128)} custom-call(s32[1]{0:T(128)S(6)} %sub.3.half_ref, bf16[4096,256]{1,0:T(8,128)(2,1)} %select.3.isel_ref, bf16[32,64,256]{2,1,0:T(8,128)(2,1)} %copy-done.1, bf16[2,200,8192]{2,1,0:T(8,128)(2,1)} %params_ref.5, f32[2,200,8192]{2,1,0:T(8,128)} %change.2.rest_0_), custom_call_target="tpu_custom_call", output_to_operand_aliasing={{}: (4, {})} | custom-call | flops 5000000000 | bytes 10000000 | tf_op jit(solution)/shard_map/change/pallas_call | solution.py:399
Async XLA Ops:
  0.0 5.3 %collective-permute-start = (s32[4,200]{1,0:T(4,128)}, s32[4,200]{1,0:T(4,128)S(1)}, u32[]{:S(2)}, u32[]{:S(2)}) collective-permute-start(s32[4,200]{1,0:T(4,128)} %near_ref.1), channel_id=1, source_target_pairs={{0,64},{32,96},{64,0},{96,32},{1,65},{33,97},{65,1},{97,33},{2,66}... | collective-permute-start | bytes 9608 | tf_op jit(solution)/shard_map/ppermute | solution.py:420
  5.3 32.2 %copy-start.4 = (s32[4,200]{1,0:T(4,128)}, s32[4,200]{1,0:T(4,128)S(1)}, u32[]{:S(2)}) copy-start(s32[4,200]{1,0:T(4,128)S(1)} %collective-permute-done.far_ref) | copy-start | bytes 9604
  37.5 3.6 %copy-start = (bf16[32,208,128]{2,1,0:T(8,128)(2,1)}, bf16[32,208,128]{2,1,0:T(8,128)(2,1)S(1)}, u32[]{:S(2)}) copy-start(bf16[32,208,128]{2,1,0:T(8,128)(2,1)S(1)} %all_to_all.5.own_ref) | copy-start | bytes 5111812
  37.5 3.6 %collective-permute-start.1 = (bf16[32,208,128]{2,1,0:T(8,128)(2,1)S(1)}, bf16[32,208,128]{2,1,0:T(8,128)(2,1)S(1)}, u32[]{:S(2)}, u32[]{:S(2)}) collective-permute-start(bf16[32,208,128]{2,1,0:T(8,128)(2,1)S(1)} %all_to_all.5.own_ref), channel_id=1, source_target_pairs={{0,32},{32,0},{64,96},{96,64},{1,33},{33,1},{65,97},{97,65},{2,34}... | collective-permute-start | bytes 5111816 | tf_op jit(solution)/shard_map/ppermute | solution.py:424
  41.1 1.2 copy-start.2
  70.5 9.5 %collective-permute-start.2 = (f32[8,200,256]{2,1,0:T(8,128)}, f32[8,200,256]{2,1,0:T(8,128)S(1)}, u32[]{:S(2)}, u32[]{:S(2)}) collective-permute-start(f32[8,200,256]{2,1,0:T(8,128)} %get-tuple-element.22.mine_ref), channel_id=1, source_target_pairs={{0,32},{32,0},{64,96},{96,64},{1,33},{33,1},{65,97},{97,65},{2,34}... | collective-permute-start | bytes 4915208 | tf_op jit(solution)/shard_map/ppermute | solution.py:428
  79.9 1.2 copy-start.3
  106.3 6.7 %collective-permute-start.3 = (bf16[32,64,256]{2,1,0:T(8,128)(2,1)}, bf16[32,64,256]{2,1,0:T(8,128)(2,1)S(1)}, u32[]{:S(2)}, u32[]{:S(2)}) collective-permute-start(bf16[32,64,256]{2,1,0:T(8,128)(2,1)} %gains.1.screened_ref), channel_id=1, source_target_pairs={{0,32},{32,0},{64,96},{96,64},{1,33},{33,1},{65,97},{97,65},{2,34}... | collective-permute-start | bytes 3145736 | tf_op jit(solution)/shard_map/ppermute | solution.py:432
  113.0 1.0 copy-start.1

commit v4 on v3

--- a/solution.py
+++ b/solution.py
@@ -16,6 +16,7 @@
 ROWS = 208
 PIV = 40
 SYS = 9
+PARTS = 4
 PACK = 3
 MAPS = 17
 GROUP = 8
@@ -76,10 +77,39 @@
         out_ref[i] = part
 
 
-def chunk_rows(keep_own, own_ref, other_ref, i):
-    rows = jnp.where(keep_own, own_ref[i].astype(f32), other_ref[i].astype(f32))
+def gathered(first, own_ref, other_ref, rows_ref, map_ref, index_ref, sems):
+    index_copy = pltpu.make_async_copy(map_ref, index_ref, sems.at[PARTS])
+    step = rows_ref.shape[0] // PARTS
+
+    def copy(ref, n):
+        at = pl.ds(n * step, step)
+        return pltpu.make_async_copy(ref.at[at], rows_ref.at[at], sems.at[n])
+
+    @pl.when(first)
+    def _():
+        for n in range(PARTS):
+            copy(own_ref, n).start()
+
+    @pl.when(jnp.logical_not(first))
+    def _():
+        for n in range(PARTS):
+            copy(other_ref, n).start()
+
+    index_copy.start()
+    return lambda n: index_copy.wait() if n == PARTS else copy(own_ref, n).wait()
+
+
+def chunk_rows(rows_ref, i):
+    rows = rows_ref[i].astype(f32)
     high = jnp.concatenate([rows[BLK:], jnp.zeros((MP - ROWS, BLK), f32)], axis=0)
     return rows, rows[:BLK], high
+
+
+def by_parts(count, wait, chunk):
+    step = count // PARTS
+    for n in range(PARTS):
+        wait(n)
+        lax.fori_loop(n * step, (n + 1) * step, chunk, 0, unroll=4)
 
 
 def fill_table(t_ref, i, low, high):
@@ -95,13 +125,24 @@
     return jnp.concatenate(both, axis=1).astype(bf16)
 
 
-def map_kernel(core_ref, map_ref, own_ref, other_ref, near_ref, far_ref, full_ref, res_ref, psel_ref, ens_ref, parts_ref, table_ref, line_ref, scale_ref, *sys_refs):
+def along(tile, u):
+    return jnp.broadcast_to(tile[u:u + 1], tile.shape)
+
+
+def inverse_of(x):
+    guess = pl.reciprocal(x, approx=True)
+    guess = guess * (2.0 - x * guess)
+    return guess * (2.0 - x * guess)
+
+
+def map_kernel(core_ref, map_ref, own_ref, other_ref, near_ref, far_ref, full_ref, res_ref, psel_ref, ens_ref, parts_ref, table_ref, line_ref, scale_ref, rows_ref, index_ref, sems, picked_ref, maps_ref, out_sems, *sys_refs):
     core = core_ref[0]
     near = near_ref.shape[0]
+    wait = gathered(core == 0, own_ref, other_ref, rows_ref, map_ref, index_ref, sems)
     blocks = map_ref.shape[0]
 
     def chunk(i, carry):
-        rows, low, high = chunk_rows(core == 0, own_ref, other_ref, i)
+        rows, low, high = chunk_rows(rows_ref, i)
         sd = rows[M:M + 1]
         at = pl.ds(pl.multiple_of(i * BLK, BLK), BLK)
         for n, part in enumerate(split3(rows * (1.0 / (sd * sd)))):
@@ -111,7 +152,7 @@
         fill_table(table_ref, i, low, high)
         return carry
 
-    lax.fori_loop(0, own_ref.shape[0], chunk, 0, unroll=4)
+    by_parts(rows_ref.shape[0], wait, chunk)
 
     gram = 0.0
     for n in (2, 1, 0):
@@ -119,12 +160,15 @@
     gram = gram[:M]
 
     def pick_own(k, carry):
-        psel_ref[pl.ds(pl.multiple_of(k * NNZ, NNZ), NNZ), :] = pick(
-            table_ref, map_ref, core * (blocks // 2) + k, line_ref
+        picked_ref[pl.ds(pl.multiple_of(k * NNZ, NNZ), NNZ), :] = pick(
+            table_ref, index_ref, core * (blocks // 2) + k, line_ref
         )
         return carry
 
+    wait(PARTS)
     lax.fori_loop(0, blocks // 2, pick_own, 0)
+    outs = [pltpu.make_async_copy(picked_ref, psel_ref, out_sems.at[SYS])]
+    outs[0].start()
 
     row = iota((M, MP), 0)
     lane = iota((M, MP), 1)
@@ -170,13 +214,13 @@
                 at_lane = inner == 8 * j + u
                 for group, col in zip(tiles, cols):
                     lead = col[j][u]
-                    scale = 1.0 / lead[u:u + 1]
+                    scale = inverse_of(along(lead, u))
                     t = group[j]
-                    line = jnp.where(at_lane[:1], 1.0, t[u:u + 1]) * scale
+                    line = jnp.where(at_lane, 1.0, along(t, u)) * scale
                     group[j] = jnp.where(trow == u, line, jnp.where(at_lane, 0.0, t) - lead * line)
                     for v in range(u + 1, 8):
                         c = col[j][v]
-                        line = c[u:u + 1] * scale
+                        line = along(c, u) * scale
                         col[j][v] = jnp.where(trow == u, line, c - lead * line)
             done = (inner >= 8 * j) & (inner < 8 * j + 8)
             for group, col in zip(tiles, cols):
@@ -216,60 +260,76 @@
     for s in range(SYS):
         scale = scale_ref[s]
         value = (-sys_refs[s][...] - scale * ((M - 1) / M)) * scale
-        if s == 0:
-            full_ref[...] = value
-        else:
-            res_ref[s - 1] = value
-
-
-def select_kernel(core_ref, map_ref, own_ref, other_ref, isel_ref, table_ref, line_ref):
-    core = core_ref[0]
+        value = jnp.concatenate([value, jnp.zeros((MP - M, MP), f32)], axis=0)
+        hi = value.astype(bf16)
+        maps_ref[s] = jnp.concatenate([hi, (value - hi.astype(f32)).astype(bf16)], axis=0)
+        outs.append(pltpu.make_async_copy(maps_ref.at[s], res_ref.at[s - 1] if s else full_ref, out_sems.at[s]))
+        outs[-1].start()
+    for copy in outs:
+        copy.wait()
+
+
+def select_kernel(half_ref, core_ref, map_ref, own_ref, other_ref, isel_ref, table_ref, line_ref, rows_ref, index_ref, sems):
+    wait = gathered(core_ref[0] == 1, own_ref, other_ref, rows_ref, map_ref, index_ref, sems)
+    blocks = map_ref.shape[0] // 2
 
     def chunk(i, carry):
-        _, low, high = chunk_rows(core == 1, own_ref, other_ref, i)
+        _, low, high = chunk_rows(rows_ref, i)
         fill_table(table_ref, i, low.T, high.T)
         return carry
 
-    lax.fori_loop(0, own_ref.shape[0], chunk, 0, unroll=4)
-
-    def pick_all(k, carry):
-        isel_ref[pl.ds(pl.multiple_of(k * NNZ, NNZ), NNZ), :] = pick(table_ref, map_ref, k, line_ref)
+    by_parts(rows_ref.shape[0], wait, chunk)
+    wait(PARTS)
+
+    def pick_pair(k, carry):
+        for n in range(2):
+            for j in range(NNZ):
+                at = 2 * (n * NNZ + j)
+                line_ref[at:at + 2, :] = table_ref[pl.ds(2 * index_ref[half_ref[0] * blocks + 2 * k + n, j], 2), :]
+        at = pl.ds(pl.multiple_of(k * BLK, BLK), BLK)
+        for n in range(2):
+            isel_ref[n * BLK:(n + 1) * BLK, at] = line_ref[pl.ds(n, BLK, stride=2), :].T.astype(bf16)
         return carry
 
-    lax.fori_loop(0, map_ref.shape[0], pick_all, 0)
-
-
-def gain_kernel(core_ref, psel_ref, full_ref, mine_ref, theirs_ref, params_ref, out_ref, maps_ref, cols_ref):
+    lax.fori_loop(0, blocks // 2, pick_pair, 0, unroll=2)
+
+
+def change_block(isel_ref, screened_ref, cells_ref, new_ref, g):
+    picked = isel_ref[:ROWS, g // 2 * BLK:(g // 2 + 1) * BLK]
+    none = jnp.zeros((NNZ, 2 * BLK), bf16)
+    rows = [none, screened_ref[g]] if g % 2 else [screened_ref[g], none]
+    change = dot(picked, jnp.concatenate(rows, axis=0))
+    at = slice(g * BLK, (g + 1) * BLK)
+    for p in range(2):
+        new_ref[p, :, at] = cells_ref[p, :, at].astype(f32) + change[:M, p * BLK:(p + 1) * BLK]
+
+
+def gain_kernel(core_ref, psel_ref, isel_ref, full_ref, mine_ref, theirs_ref, params_ref, screened_ref, out_ref, cols_ref, maps_ref, sems):
+    def bring(r):
+        if r == 0:
+            ref = full_ref
+        elif r < SYS:
+            ref = mine_ref.at[r - 1]
+        else:
+            ref = theirs_ref.at[r - SYS]
+        return pltpu.make_async_copy(ref, maps_ref.at[r], sems.at[r])
+
     @pl.when(pl.program_id(0) == 0)
     def _():
-        def place(r, value):
-            pad = jnp.zeros((MP - M, MP), f32)
-            for n, part in enumerate(split3(value)):
-                maps_ref[r, n * MP:(n + 1) * MP, :] = jnp.concatenate([part, pad], axis=0).astype(bf16)
-
-        place(0, full_ref[...])
-
-        def place_both(r, carry):
-            place(1 + r, mine_ref[r])
-            place(SYS + r, theirs_ref[r])
-            return carry
-
-        lax.fori_loop(0, SYS - 1, place_both, 0)
+        for r in range(MAPS):
+            bring(r).start()
+        for r in range(MAPS):
+            bring(r).wait()
 
     x = psel_ref[...]
     sd = x[:, M:M + 1].astype(f32)
     weight = 1.0 / (sd * sd)
-
-    x3 = jnp.concatenate([x, x, x], axis=1)
-
-    def column(r, carry):
-        total = dot(x3, maps_ref[r])
-        total = (total * weight).astype(bf16)
+    x = jnp.concatenate([x, x], axis=1)
+
+    for r in range(MAPS):
+        total = (dot(x, maps_ref[r]) * weight).astype(bf16)
         for g in range(GROUP):
-            cols_ref[g, pl.ds(pl.multiple_of(r * NNZ, NNZ), NNZ), :] = total[g * NNZ:(g + 1) * NNZ]
-        return carry
-
-    lax.fori_loop(0, MAPS, column, 0, unroll=True)
+            cols_ref[g, r * NNZ:(r + 1) * NNZ, :] = total[g * NNZ:(g + 1) * NNZ]
 
     def gains(g, carry):
         at = pl.ds(pl.multiple_of(g * BLK, BLK), BLK)
@@ -281,25 +341,50 @@
             off = every[r * NNZ:(r + 1) * NNZ] - full
             spread = spread + off * off
         squared = full * full
-        out_ref[g] = (squared / (squared + spread * (1.0 / NB) + screen_floor) * full).astype(bf16)
+        screened_ref[g] = (squared / (squared + spread * (1.0 / NB) + screen_floor) * full).astype(bf16)
         return carry
 
-    lax.fori_loop(0, GROUP, gains, 0, unroll=4)
-
-
-def change_kernel(half_ref, isel_ref, screened_ref, params_ref, *rest):
-    out_ref = rest[-1]
+    lax.fori_loop(0, GROUP, gains, 0, unroll=GROUP)
     for g in range(GROUP):
-        change = lax.dot_general(
-            isel_ref[g * NNZ:(g + 1) * NNZ, :], screened_ref[g], (((0,), (0,)), ((), ())), preferred_element_type=f32
-        )
-        at = slice(g * BLK, (g + 1) * BLK)
+        change_block(isel_ref, screened_ref, params_ref, out_ref, g)
+
+
+def change_kernel(half_ref, isel_ref, screened_ref, params_ref, so_far_ref, out_ref, cells_ref, new_ref, in_sems, out_sems):
+    blocks = screened_ref.shape[0]
+    width = GROUP * BLK
+    steps = blocks // GROUP
+    start = pl.multiple_of(half_ref[0] * (blocks * BLK), BLK)
+
+    def here(n):
+        return pl.ds(n * width, width)
+
+    def there(n):
+        return pl.ds(pl.multiple_of(start + n * width, BLK), width)
+
+    def bring(n, p):
+        return pltpu.make_async_copy(params_ref.at[p, :, there(n)], cells_ref.at[p, :, here(n)], in_sems.at[n, p])
+
+    def send(n, p):
+        return pltpu.make_async_copy(new_ref.at[p, :, here(n)], out_ref.at[p, :, there(n)], out_sems.at[n, p])
+
+    for n in range(steps):
         for p in range(2):
-            out_ref[p, :, at] = params_ref[p, :, at].astype(f32) + change[:M, p * BLK:(p + 1) * BLK]
+            bring(n, p).start()
+    for n in range(steps):
+        for p in range(2):
+            bring(n, p).wait()
+        for g in range(n * GROUP, (n + 1) * GROUP):
+            change_block(isel_ref, screened_ref, cells_ref, new_ref, g)
+        for p in range(2):
+            send(n, p).start()
+    for n in range(steps):
+        for p in range(2):
+            send(n, p).wait()
 
 
 vmem = pl.BlockSpec(memory_space=pltpu.VMEM)
 smem = pl.BlockSpec(memory_space=pltpu.SMEM)
+hbm = pl.BlockSpec(memory_space=pl.ANY)
 limit = pltpu.CompilerParams(vmem_limit_bytes=56 * 1024 * 1024)
 
 
@@ -321,18 +406,24 @@
     return pl.pallas_call(
         map_kernel,
         out_shape=(
-            jax.ShapeDtypeStruct((M, MP), f32),
-            jax.ShapeDtypeStruct((SYS - 1, M, MP), f32),
+            jax.ShapeDtypeStruct((2 * MP, MP), bf16),
+            jax.ShapeDtypeStruct((SYS - 1, 2 * MP, MP), bf16),
             jax.ShapeDtypeStruct((blocks // 2 * NNZ, MP), bf16),
         ),
-        in_specs=[smem, smem, vmem, vmem, vmem, vmem],
-        out_specs=(vmem, vmem, vmem),
+        in_specs=[smem, hbm, hbm, hbm, vmem, vmem],
+        out_specs=(hbm, hbm, hbm),
         scratch_shapes=[
             pltpu.VMEM((data, MP), bf16),
             pltpu.VMEM((3, ROWS, data), bf16),
             pltpu.VMEM((2 * data, BLK), f32),
             pltpu.VMEM((2 * NNZ, BLK), f32),
             pltpu.VMEM((SYS, M, MP), f32),
+            pltpu.VMEM(own.shape, bf16),
+            pltpu.SMEM(block_map.shape, jnp.int32),
+            pltpu.SemaphoreType.DMA((PARTS + 1,)),
+            pltpu.VMEM((blocks // 2 * NNZ, MP), bf16),
+            pltpu.VMEM((SYS, 2 * MP, MP), bf16),
+            pltpu.SemaphoreType.DMA((SYS + 1,)),
         ] + [pltpu.VMEM((M, MP), f32)] * SYS,
         compiler_params=limit,
         cost_estimate=pl.CostEstimate(flops=20_000_000_000, bytes_accessed=8_000_000, transcendentals=0),
@@ -340,73 +431,74 @@
     )(core, block_map, own, other, near, far)
 
 
-def select(core, block_map, own, other):
-    blocks = block_map.shape[0]
+def select(half, core, block_map, own, other):
+    blocks = block_map.shape[0] // 2
     data = own.shape[0] * BLK
     return pl.pallas_call(
         select_kernel,
-        out_shape=jax.ShapeDtypeStruct((blocks * NNZ, MP), bf16),
-        in_specs=[smem, smem, vmem, vmem],
+        out_shape=jax.ShapeDtypeStruct((MP, blocks * NNZ), bf16),
+        in_specs=[smem, smem, hbm, hbm, hbm],
         out_specs=vmem,
-        scratch_shapes=[pltpu.VMEM((2 * data, BLK), f32), pltpu.VMEM((2 * NNZ, BLK), f32)],
+        scratch_shapes=[
+            pltpu.VMEM((2 * data, BLK), f32),
+            pltpu.VMEM((4 * NNZ, BLK), f32),
+            pltpu.VMEM(own.shape, bf16),
+            pltpu.SMEM(block_map.shape, jnp.int32),
+            pltpu.SemaphoreType.DMA((PARTS + 1,)),
+        ],
         compiler_params=limit,
-        cost_estimate=pl.CostEstimate(flops=10_000_000_000, bytes_accessed=8_000_000, transcendentals=0),
+        cost_estimate=pl.CostEstimate(flops=8_000_000_000, bytes_accessed=8_000_000, transcendentals=0),
         name="select",
-    )(core, block_map, own, other)
-
-
-def make_screened(core, psel, full, mine, theirs, params):
+    )(half, core, block_map, own, other)
+
+
+def screen(core, psel, isel, full, mine, theirs, params):
     blocks = params.shape[2] // BLK // 2
     steps = blocks // GROUP
+    cells = pl.BlockSpec((2, M, GROUP * BLK), lambda i, c: (0, 0, c[0] * steps + i))
+    rows = pl.BlockSpec((GROUP * NNZ, MP), lambda i, c: (i, 0))
     return pl.pallas_call(
         gain_kernel,
-        out_shape=jax.ShapeDtypeStruct((blocks, NNZ, 2 * BLK), bf16),
+        out_shape=(
+            jax.ShapeDtypeStruct((blocks, NNZ, 2 * BLK), bf16),
+            jax.ShapeDtypeStruct(params.shape, f32),
+        ),
         grid_spec=pltpu.PrefetchScalarGridSpec(
             num_scalar_prefetch=1,
             grid=(steps,),
-            in_specs=[
-                pl.BlockSpec((GROUP * NNZ, MP), lambda i, c: (i, 0)),
-                pl.BlockSpec((M, MP), lambda i, c: (0, 0)),
-                pl.BlockSpec((SYS - 1, M, MP), lambda i, c: (0, 0, 0)),
-                pl.BlockSpec((SYS - 1, M, MP), lambda i, c: (0, 0, 0)),
-                pl.BlockSpec((2, M, GROUP * BLK), lambda i, c: (0, 0, c[0] * steps + i)),
-            ],
-            out_specs=pl.BlockSpec((GROUP, NNZ, 2 * BLK), lambda i, c: (i, 0, 0)),
+            in_specs=[rows, pl.BlockSpec((MP, GROUP * NNZ), lambda i, c: (0, i)), hbm, hbm, hbm, cells],
+            out_specs=(pl.BlockSpec((GROUP, NNZ, 2 * BLK), lambda i, c: (i, 0, 0)), cells),
             scratch_shapes=[
-                pltpu.VMEM((MAPS, 3 * MP, MP), bf16),
                 pltpu.VMEM((GROUP, MAPS * NNZ, MP), bf16),
+                pltpu.VMEM((MAPS, 2 * MP, MP), bf16),
+                pltpu.SemaphoreType.DMA((MAPS,)),
             ],
         ),
         compiler_params=limit,
-        cost_estimate=pl.CostEstimate(flops=20_000_000_000, bytes_accessed=8_000_000, transcendentals=0),
+        cost_estimate=pl.CostEstimate(flops=20_000_000_000, bytes_accessed=16_000_000, transcendentals=0),
         name="gains",
-    )(core, psel, full, mine, theirs, params)
-
-
-def update(half, isel, screened, params, so_far=None):
-    blocks = params.shape[2] // BLK // 2
+    )(core, psel, isel, full, mine, theirs, params)
+
+
+def update(half, isel, screened, params, so_far):
+    blocks = screened.shape[0]
     steps = blocks // GROUP
-    cells = pl.BlockSpec((2, M, GROUP * BLK), lambda i, c: (0, 0, c[0] * steps + i))
-    in_specs = [
-        pl.BlockSpec((GROUP * NNZ, MP), lambda i, c: (c[0] * steps + i, 0)),
-        pl.BlockSpec((GROUP, NNZ, 2 * BLK), lambda i, c: (i, 0, 0)),
-        cells,
-    ]
-    operands = (half, isel, screened, params)
-    if so_far is not None:
-        in_specs.append(pl.BlockSpec(memory_space=pl.ANY))
-        operands = operands + (so_far,)
     return pl.pallas_call(
         change_kernel,
         out_shape=jax.ShapeDtypeStruct(params.shape, f32),
-        grid_spec=pltpu.PrefetchScalarGridSpec(
-            num_scalar_prefetch=1, grid=(steps,), in_specs=in_specs, out_specs=cells
-        ),
-        input_output_aliases={} if so_far is None else {4: 0},
+        in_specs=[smem, vmem, vmem, hbm, hbm],
+        out_specs=hbm,
+        scratch_shapes=[
+            pltpu.VMEM((2, M, blocks * BLK), bf16),
+            pltpu.VMEM((2, M, blocks * BLK), f32),
+            pltpu.SemaphoreType.DMA((steps, 2)),
+            pltpu.SemaphoreType.DMA((steps, 2)),
+        ],
+        input_output_aliases={4: 0},
         compiler_params=limit,
         cost_estimate=pl.CostEstimate(flops=5_000_000_000, bytes_accessed=10_000_000, transcendentals=0),
         name="change",
-    )(*operands)
+    )(half, isel, screened, params, so_far)
 
 
 def on_device(params, predicted, perturbation, observed, obs_sd, members, block_map):
@@ -426,12 +518,13 @@
     full, mine, psel = make_maps(core_arg, block_map, own, other, members, far_members)
     late_map, mine = lax.optimization_barrier((block_map, mine))
     theirs = lax.ppermute(mine, "boot", pair)
-    isel = select(core_arg, late_map, own, other)
+    isel = select(core_arg, core_arg, late_map, own, other)
     isel, psel = lax.optimization_barrier((isel, psel))
-    screened = make_screened(core_arg, psel, full, mine, theirs, params)
+    screened, so_far = screen(core_arg, psel, isel, full, mine, theirs, params)
+    last_map, screened = lax.optimization_barrier((block_map, screened))
     screened_other = lax.ppermute(screened, "boot", pair)
-    partial_out = update(core_arg, isel, screened, params)
-    return update(1 - core_arg, isel, screened_other, params, partial_out)
+    isel_other = select(1 - core_arg, core_arg, last_map, own, other)
+    return update(1 - core_arg, isel_other, screened_other, params, so_far)
 
 
 def solution(mesh):

time: 122 us -> 114 us (0.934)
  Pallas kernels: 77.5 us -> 69.3 us
    pallas_call x2 -> x1, Pallas kernels: 12.6 us -> 5.93 us  [update(): pl.pallas_call(change_kernel, out_shape=jax.ShapeDtypeStruct(params.shape...]
    pallas_call x3 -> x4, Pallas kernels: 62.7 us -> 61.2 us  [the longest x1 27.2 us: make_maps(): pl.pallas_call(map_kernel, out_shape=(jax.ShapeDtypeStruct((2 * MP, MP),...]
  transfers between devices with their start and end apart: 4 -> 4, of which waited for: 2 -> 2; matrix products, arithmetic and copies ran while one was open for 0% -> 0% of each run, Pallas kernels for 15% -> 13%
where the time goes in v4:
time: 114 us; the launch traced here: 113 us
  Pallas kernels  69.3 us (61%)
  blocking collectives  32.2 us (28%)
  starting transfers between devices  3.96 us (3%)
  waiting for transfers between devices  3.68 us (3%)
  local copies, waits for them, and re-layouts  3.55 us (3%)
    all_to_all x1, blocking collectives, on_device(): own = lax.all_to_all(whole, 'slab', 0, 0)  32.2 us
    pallas_call x1, Pallas kernels, make_maps(): pl.pallas_call(map_kernel, out_shape=(jax.ShapeDtypeStruct((2 * MP, MP),...  27.2 us
    pallas_call x1, Pallas kernels, screen(): pl.pallas_call(gain_kernel, out_shape=(jax.ShapeDtypeStruct((blocks, NNZ,...  21.4 us
    pallas_call x2, Pallas kernels, select(): pl.pallas_call(select_kernel, out_shape=jax.ShapeDtypeStruct((MP, blocks...  12.6 us
    pallas_call x1, Pallas kernels, update(): pl.pallas_call(change_kernel, out_shape=jax.ShapeDtypeStruct(params.shape...  5.93 us
    ppermute x1, waiting for transfers between devices, on_device(): other = lax.ppermute(own, 'boot', pair)  3.59 us
    unnamed x10, local copies, waits for them, and re-layouts  3.55 us
    ppermute x1, starting transfers between devices, on_device(): far_members = lax.ppermute(members, 'boot', far)  3.11 us
  transfers between devices with their start and end apart: 4, of which 2 were waited for; matrix products, arithmetic and copies ran while one was open for 0% of the time, Pallas kernels for 13%

profile of v4, /device:TPU:0, one launch (start us, length us, event | category | flops | bytes accessed | tf_op | source)
XLA Modules:
  0.0 112.9 jit_solution(3416507395181818704)
XLA Ops:
  0.0 3.1 %collective-permute-start = (s32[4,200]{1,0:T(4,128)}, s32[4,200]{1,0:T(4,128)S(1)}, u32[]{:S(2)}, u32[]{:S(2)}) collective-permute-start(s32[4,200]{1,0:T(4,128)} %near_ref.1), channel_id=1, source_target_pairs={{0,64},{32,96},{64,0},{96,32},{1,65},{33,97},{65,1},{97,33},{2,66}... | collective-permute-start | bytes 9608 | tf_op jit(solution)/shard_map/ppermute | solution.py:512
  3.1 2.1 %pack.1 = bf16[32,208,128]{2,1,0:T(8,128)(2,1)} custom-call(s32[1]{0:T(128)} %bitcast.core_ref.half_ref, bf16[200,128]{1,0:T(8,128)(2,1)} %pred_ref.1, bf16[200,128]{1,0:T(8,128)(2,1)} %pert_ref.1, bf16[1,128]{1,0:T(2,128)(2,1)} %bitcast.3, bf16[1,128]{1,0:T(2,128)(2,1)} %bitcast.4), custom_call_target="tpu_custom_call" | custom-call | tf_op jit(solution)/shard_map/pack/pallas_call | solution.py:393
  5.2 0.1 collective-permute-done.far_ref
  5.3 0.0 copy-start.4
  5.3 32.2 %all_to_all.5.own_ref = bf16[32,208,128]{2,1,0:T(8,128)(2,1)S(1)} all-to-all(bf16[32,208,128]{2,1,0:T(8,128)(2,1)} %pack.1), channel_id=1, replica_groups=mesh['boot'=4,'slab'=32] {'slab'}, dimensions={0} | all-to-all | bytes 3407872 | tf_op jit(solution)/shard_map/all_to_all | solution.py:515
  37.5 0.0 copy-start
  37.5 0.0 collective-permute-start.1
  37.5 3.6 %collective-permute-done.1.other_ref = bf16[32,208,128]{2,1,0:T(8,128)(2,1)S(1)} collective-permute-done((bf16[32,208,128]{2,1,0:T(8,128)(2,1)S(1)}, bf16[32,208,128]{2,1,0:T(8,128)(2,1)S(1)}, u32[]{:S(2)}, u32[]{:S(2)}) %collective-permute-start.1) | collective-permute-done | bytes 1703968 | tf_op jit(solution)/shard_map/ppermute | solution.py:516
  41.1 0.0 copy-done.4
  41.1 0.0 copy-done
  41.1 0.0 copy-start.3
  41.1 1.2 %copy-done.3 = bf16[32,208,128]{2,1,0:T(8,128)(2,1)} copy-done((bf16[32,208,128]{2,1,0:T(8,128)(2,1)}, bf16[32,208,128]{2,1,0:T(8,128)(2,1)S(1)}, u32[]{:S(2)}) %copy-start.3) | copy-done | bytes 1703960
  42.3 27.2 %maps.1 = (bf16[512,256]{1,0:T(8,128)(2,1)}, bf16[8,512,256]{2,1,0:T(8,128)(2,1)}, bf16[2048,256]{1,0:T(8,128)(2,1)}) custom-call(s32[1]{0:T(128)} %bitcast.core_ref.half_ref, s32[64,64]{1,0:T(8,128)} %map_ref.3, bf16[32,208,128]{2,1,0:T(8,128)(2,1)} %copy-done, bf16[32,208,128]{2,1,0:T(8,128)(2,1)} %copy-done.3, s32[4,200]{1,0:T(4,128)} %near_ref.1, ...), custom_call_target="tpu_custom_call" | custom-call | flops 20000000000 | bytes 8000000 | tf_op jit(solution)/shard_map/maps/pallas_call | solution.py:406
  69.5 0.4 collective-permute-start.2
  69.9 6.3 %select.4.isel_ref = bf16[256,2048]{1,0:T(8,128)(2,1)} custom-call(s32[1]{0:T(128)} %bitcast.core_ref.half_ref, s32[1]{0:T(128)} %bitcast.core_ref.half_ref, s32[64,64]{1,0:T(8,128)} %map_ref.3, bf16[32,208,128]{2,1,0:T(8,128)(2,1)} %copy-done, bf16[32,208,128]{2,1,0:T(8,128)(2,1)} %copy-done.3), custom_call_target="tpu_custom_call" | custom-call | flops 8000000000 | bytes 8000000 | tf_op jit(solution)/shard_map/select/pallas_call | solution.py:437
  76.2 0.0 collective-permute-done.2.theirs_ref
  76.3 0.0 copy-start.2
  76.3 1.3 %copy-done.2 = bf16[8,512,256]{2,1,0:T(8,128)(2,1)} copy-done((bf16[8,512,256]{2,1,0:T(8,128)(2,1)}, bf16[8,512,256]{2,1,0:T(8,128)(2,1)S(1)}, u32[]{:S(2)}) %copy-start.2) | copy-done | bytes 2097176
  77.6 21.4 %gains.1 = (bf16[32,64,256]{2,1,0:T(8,128)(2,1)}, f32[2,200,8192]{2,1,0:T(8,128)}) custom-call(s32[1]{0:T(128)} %bitcast.core_ref.half_ref, bf16[2048,256]{1,0:T(8,128)(2,1)} %get-tuple-element.23.psel_ref, bf16[256,2048]{1,0:T(8,128)(2,1)} %select.4.isel_ref, bf16[512,256]{1,0:T(8,128)(2,1)} %get-tuple-element.25.full_ref, ...), custom_call_target="tpu_custom_call" | custom-call | flops 20000000000 | bytes 16000000 | tf_op jit(solution)/shard_map/gains/pallas_call | solution.py:460
  99.0 0.5 collective-permute-start.3
  99.4 6.3 %select.5.isel_ref = bf16[256,2048]{1,0:T(8,128)(2,1)} custom-call(s32[1]{0:T(128)S(6)} %sub.4.half_ref, s32[1]{0:T(128)} %bitcast.core_ref.half_ref, s32[64,64]{1,0:T(8,128)} %map_ref.3, bf16[32,208,128]{2,1,0:T(8,128)(2,1)} %copy-done, bf16[32,208,128]{2,1,0:T(8,128)(2,1)} %copy-done.3), custom_call_target="tpu_custom_call" | custom-call | flops 8000000000 | bytes 8000000 | tf_op jit(solution)/shard_map/select/pallas_call | solution.py:437
  105.7 0.0 collective-permute-done.3.screened_ref
  105.8 0.0 copy-start.1
  105.8 1.0 copy-done.1
  106.8 5.9 %change.1 = f32[2,200,8192]{2,1,0:T(8,128)} custom-call(s32[1]{0:T(128)S(6)} %sub.4.half_ref, bf16[256,2048]{1,0:T(8,128)(2,1)} %select.5.isel_ref, bf16[32,64,256]{2,1,0:T(8,128)(2,1)} %copy-done.1, bf16[2,200,8192]{2,1,0:T(8,128)(2,1)} %params_ref.3, f32[2,200,8192]{2,1,0:T(8,128)} %get-tuple-element.30.so_far_ref), custom_call_target="tpu_custom_call", output_to_operand_aliasing={{}: (4, {})} | custom-call | flops 5000000000 | bytes 10000000 | tf_op jit(solution)/shard_map/change/pallas_call | solution.py:486
Async XLA Ops:
  0.0 5.3 %collective-permute-start = (s32[4,200]{1,0:T(4,128)}, s32[4,200]{1,0:T(4,128)S(1)}, u32[]{:S(2)}, u32[]{:S(2)}) collective-permute-start(s32[4,200]{1,0:T(4,128)} %near_ref.1), channel_id=1, source_target_pairs={{0,64},{32,96},{64,0},{96,32},{1,65},{33,97},{65,1},{97,33},{2,66}... | collective-permute-start | bytes 9608 | tf_op jit(solution)/shard_map/ppermute | solution.py:512
  5.3 35.8 %copy-start.4 = (s32[4,200]{1,0:T(4,128)}, s32[4,200]{1,0:T(4,128)S(1)}, u32[]{:S(2)}) copy-start(s32[4,200]{1,0:T(4,128)S(1)} %collective-permute-done.far_ref) | copy-start | bytes 9604
  37.5 3.6 %copy-start = (bf16[32,208,128]{2,1,0:T(8,128)(2,1)}, bf16[32,208,128]{2,1,0:T(8,128)(2,1)S(1)}, u32[]{:S(2)}) copy-start(bf16[32,208,128]{2,1,0:T(8,128)(2,1)S(1)} %all_to_all.5.own_ref) | copy-start | bytes 5111812
  37.5 3.6 %collective-permute-start.1 = (bf16[32,208,128]{2,1,0:T(8,128)(2,1)S(1)}, bf16[32,208,128]{2,1,0:T(8,128)(2,1)S(1)}, u32[]{:S(2)}, u32[]{:S(2)}) collective-permute-start(bf16[32,208,128]{2,1,0:T(8,128)(2,1)S(1)} %all_to_all.5.own_ref), channel_id=1, source_target_pairs={{0,32},{32,0},{64,96},{96,64},{1,33},{33,1},{65,97},{97,65},{2,34}... | collective-permute-start | bytes 5111816 | tf_op jit(solution)/shard_map/ppermute | solution.py:516
  41.1 1.2 %copy-start.3 = (bf16[32,208,128]{2,1,0:T(8,128)(2,1)}, bf16[32,208,128]{2,1,0:T(8,128)(2,1)S(1)}, u32[]{:S(2)}) copy-start(bf16[32,208,128]{2,1,0:T(8,128)(2,1)S(1)} %collective-permute-done.1.other_ref) | copy-start | bytes 5111812
  69.5 6.7 %collective-permute-start.2 = (bf16[8,512,256]{2,1,0:T(8,128)(2,1)}, bf16[8,512,256]{2,1,0:T(8,128)(2,1)S(1)}, u32[]{:S(2)}, u32[]{:S(2)}) collective-permute-start(bf16[8,512,256]{2,1,0:T(8,128)(2,1)} %get-tuple-element.26.mine_ref), channel_id=1, source_target_pairs={{0,32},{32,0},{64,96},{96,64},{1,33},{33,1},{65,97},{97,65},{2,34}... | collective-permute-start | bytes 6291464 | tf_op jit(solution)/shard_map/ppermute | solution.py:520
  76.3 1.3 %copy-start.2 = (bf16[8,512,256]{2,1,0:T(8,128)(2,1)}, bf16[8,512,256]{2,1,0:T(8,128)(2,1)S(1)}, u32[]{:S(2)}) copy-start(bf16[8,512,256]{2,1,0:T(8,128)(2,1)S(1)} %collective-permute-done.2.theirs_ref) | copy-start | bytes 6291460
  99.0 6.8 %collective-permute-start.3 = (bf16[32,64,256]{2,1,0:T(8,128)(2,1)}, bf16[32,64,256]{2,1,0:T(8,128)(2,1)S(1)}, u32[]{:S(2)}, u32[]{:S(2)}) collective-permute-start(bf16[32,64,256]{2,1,0:T(8,128)(2,1)} %get-tuple-element.29), channel_id=1, source_target_pairs={{0,32},{32,0},{64,96},{96,64},{1,33},{33,1},{65,97},{97,65},{2,34}... | collective-permute-start | bytes 3145736 | tf_op jit(solution)/shard_map/ppermute | solution.py:525
  105.8 1.0 copy-start.1

commit v5 on v4

--- a/solution.py
+++ b/solution.py
@@ -77,26 +77,37 @@
         out_ref[i] = part
 
 
-def gathered(first, own_ref, other_ref, rows_ref, map_ref, index_ref, sems):
-    index_copy = pltpu.make_async_copy(map_ref, index_ref, sems.at[PARTS])
-    step = rows_ref.shape[0] // PARTS
-
-    def copy(ref, n):
-        at = pl.ds(n * step, step)
-        return pltpu.make_async_copy(ref.at[at], rows_ref.at[at], sems.at[n])
-
-    @pl.when(first)
+def gathered(own_first, own_ref, other_ref, ens_ref, innov_ref, map_ref, index_ref, sems):
+    step = ens_ref.shape[0] // PARTS
+
+    def copy(source, target, n):
+        at = pl.ds(n % PARTS * step, step)
+        return pltpu.make_async_copy(source.at[at], target.at[at], sems.at[n])
+
+    def start(first_ref, second_ref):
+        for n in range(PARTS):
+            copy(first_ref, ens_ref, n).start()
+        index_copy.start()
+        for n in range(PARTS):
+            copy(second_ref, innov_ref, PARTS + n).start()
+
+    index_copy = pltpu.make_async_copy(map_ref, index_ref, sems.at[2 * PARTS])
+
+    @pl.when(own_first)
     def _():
-        for n in range(PARTS):
-            copy(own_ref, n).start()
-
-    @pl.when(jnp.logical_not(first))
+        start(own_ref, other_ref)
+
+    @pl.when(jnp.logical_not(own_first))
     def _():
-        for n in range(PARTS):
-            copy(other_ref, n).start()
-
-    index_copy.start()
-    return lambda n: index_copy.wait() if n == PARTS else copy(own_ref, n).wait()
+        start(other_ref, own_ref)
+
+    def wait(n):
+        if n == 2 * PARTS:
+            index_copy.wait()
+        else:
+            copy(own_ref, ens_ref if n < PARTS else innov_ref, n).wait()
+
+    return wait
 
 
 def chunk_rows(rows_ref, i):
@@ -105,10 +116,10 @@
     return rows, rows[:BLK], high
 
 
-def by_parts(count, wait, chunk):
+def by_parts(count, first, wait, chunk):
     step = count // PARTS
     for n in range(PARTS):
-        wait(n)
+        wait(first + n)
         lax.fori_loop(n * step, (n + 1) * step, chunk, 0, unroll=4)
 
 
@@ -118,13 +129,6 @@
     t_ref[pl.ds(base + 1, BLK, stride=2), :] = high
 
 
-def pick(t_ref, map_ref, k, line_ref):
-    for j in range(NNZ):
-        line_ref[2 * j:2 * j + 2, :] = t_ref[pl.ds(2 * map_ref[k, j], 2), :]
-    both = [line_ref[pl.ds(n, NNZ, stride=2), :] for n in range(2)]
-    return jnp.concatenate(both, axis=1).astype(bf16)
-
-
 def along(tile, u):
     return jnp.broadcast_to(tile[u:u + 1], tile.shape)
 
@@ -135,11 +139,15 @@
     return guess * (2.0 - x * guess)
 
 
-def map_kernel(core_ref, map_ref, own_ref, other_ref, near_ref, far_ref, full_ref, res_ref, psel_ref, ens_ref, parts_ref, table_ref, line_ref, scale_ref, rows_ref, index_ref, sems, picked_ref, maps_ref, out_sems, *sys_refs):
+def map_kernel(
+    core_ref, map_ref, own_ref, other_ref, near_ref, far_ref, full_ref, res_ref, psel_ref, isel_ref,
+    ens_ref, parts_ref, ptab_ref, itab_ref, pline_ref, iline_ref, scale_ref, rows_ref, late_ref, index_ref,
+    sems, maps_ref, out_sems, *sys_refs
+):
     core = core_ref[0]
+    blocks = map_ref.shape[0]
+    wait = gathered(core == 0, own_ref, other_ref, rows_ref, late_ref, map_ref, index_ref, sems)
     near = near_ref.shape[0]
-    wait = gathered(core == 0, own_ref, other_ref, rows_ref, map_ref, index_ref, sems)
-    blocks = map_ref.shape[0]
 
     def chunk(i, carry):
         rows, low, high = chunk_rows(rows_ref, i)
@@ -149,26 +157,39 @@
             parts_ref[n, :, at] = part.astype(bf16)
         low, high = low.T, high.T
         ens_ref[at, :] = jnp.concatenate([low, high], axis=1).astype(bf16)
-        fill_table(table_ref, i, low, high)
+        fill_table(ptab_ref, i, low, high)
         return carry
 
-    by_parts(rows_ref.shape[0], wait, chunk)
+    by_parts(rows_ref.shape[0], 0, wait, chunk)
+
+    def late_chunk(i, carry):
+        _, low, high = chunk_rows(late_ref, i)
+        fill_table(itab_ref, i, low.T, high.T)
+        return carry
+
+    by_parts(late_ref.shape[0], PARTS, wait, late_chunk)
+    wait(2 * PARTS)
 
     gram = 0.0
     for n in (2, 1, 0):
         gram = gram + dot(parts_ref[n], ens_ref[...])
     gram = gram[:M]
 
-    def pick_own(k, carry):
-        picked_ref[pl.ds(pl.multiple_of(k * NNZ, NNZ), NNZ), :] = pick(
-            table_ref, index_ref, core * (blocks // 2) + k, line_ref
-        )
-        return carry
-
-    wait(PARTS)
-    lax.fori_loop(0, blocks // 2, pick_own, 0)
-    outs = [pltpu.make_async_copy(picked_ref, psel_ref, out_sems.at[SYS])]
-    outs[0].start()
+    ipanel = -(-blocks // (M // PIV))
+    ppanel = -(-(blocks // 2) // (M // PIV))
+    share = -(-(ipanel + ppanel) * NNZ // PIV)
+
+    def pick(kp, t):
+        for n in range(t * share, min((t + 1) * share, (ipanel + ppanel) * NNZ)):
+            b, j = n // NNZ, n % NNZ
+            if b < ipanel:
+                k = jnp.minimum(kp * ipanel + b, blocks - 1)
+                at = index_ref[k, j]
+                iline_ref[pl.ds(k * (2 * NNZ) + 2 * j, 2), :] = itab_ref[pl.ds(2 * at, 2), :]
+            else:
+                k = jnp.minimum(kp * ppanel + b - ipanel, blocks // 2 - 1)
+                at = index_ref[core * (blocks // 2) + k, j]
+                pline_ref[pl.ds(k * (2 * NNZ) + 2 * j, 2), :] = ptab_ref[pl.ds(2 * at, 2), :]
 
     row = iota((M, MP), 0)
     lane = iota((M, MP), 1)
@@ -222,6 +243,7 @@
                         c = col[j][v]
                         line = along(c, u) * scale
                         col[j][v] = jnp.where(trow == u, line, c - lead * line)
+                pick(kp, 8 * j + u)
             done = (inner >= 8 * j) & (inner < 8 * j + 8)
             for group, col in zip(tiles, cols):
                 for i in range(PIV // 8):
@@ -257,6 +279,12 @@
 
     lax.fori_loop(0, M // PIV, panel_step, 0)
 
+    outs = [
+        pltpu.make_async_copy(pline_ref, psel_ref, out_sems.at[SYS]),
+        pltpu.make_async_copy(iline_ref, isel_ref, out_sems.at[SYS + 1]),
+    ]
+    for copy in outs:
+        copy.start()
     for s in range(SYS):
         scale = scale_ref[s]
         value = (-sys_refs[s][...] - scale * ((M - 1) / M)) * scale
@@ -269,29 +297,13 @@
         copy.wait()
 
 
-def select_kernel(half_ref, core_ref, map_ref, own_ref, other_ref, isel_ref, table_ref, line_ref, rows_ref, index_ref, sems):
-    wait = gathered(core_ref[0] == 1, own_ref, other_ref, rows_ref, map_ref, index_ref, sems)
-    blocks = map_ref.shape[0] // 2
-
-    def chunk(i, carry):
-        _, low, high = chunk_rows(rows_ref, i)
-        fill_table(table_ref, i, low.T, high.T)
-        return carry
-
-    by_parts(rows_ref.shape[0], wait, chunk)
-    wait(PARTS)
-
-    def pick_pair(k, carry):
-        for n in range(2):
-            for j in range(NNZ):
-                at = 2 * (n * NNZ + j)
-                line_ref[at:at + 2, :] = table_ref[pl.ds(2 * index_ref[half_ref[0] * blocks + 2 * k + n, j], 2), :]
-        at = pl.ds(pl.multiple_of(k * BLK, BLK), BLK)
-        for n in range(2):
-            isel_ref[n * BLK:(n + 1) * BLK, at] = line_ref[pl.ds(n, BLK, stride=2), :].T.astype(bf16)
-        return carry
-
-    lax.fori_loop(0, blocks // 2, pick_pair, 0, unroll=2)
+def arrange_kernel(pline_ref, iline_ref, psel_ref, isel_ref):
+    for n in range(2):
+        lanes = slice(n * BLK, (n + 1) * BLK)
+        psel_ref[:, lanes] = pline_ref[pl.ds(n, psel_ref.shape[0], stride=2), :].astype(bf16)
+        for k in range(isel_ref.shape[1] // BLK):
+            at = slice(k * BLK, (k + 1) * BLK)
+            isel_ref[lanes, at] = iline_ref[pl.ds(2 * k * BLK + n, BLK, stride=2), :].T.astype(bf16)
 
 
 def change_block(isel_ref, screened_ref, cells_ref, new_ref, g):
@@ -305,31 +317,30 @@
 
 
 def gain_kernel(core_ref, psel_ref, isel_ref, full_ref, mine_ref, theirs_ref, params_ref, screened_ref, out_ref, cols_ref, maps_ref, sems):
-    def bring(r):
-        if r == 0:
-            ref = full_ref
-        elif r < SYS:
-            ref = mine_ref.at[r - 1]
-        else:
-            ref = theirs_ref.at[r - SYS]
-        return pltpu.make_async_copy(ref, maps_ref.at[r], sems.at[r])
-
-    @pl.when(pl.program_id(0) == 0)
+    refs = [full_ref] + [mine_ref.at[r] for r in range(SYS - 1)] + [theirs_ref.at[r] for r in range(SYS - 1)]
+    copies = [pltpu.make_async_copy(ref, maps_ref.at[r], sems.at[r]) for r, ref in enumerate(refs)]
+    opening = pl.program_id(0) == 0
+
+    @pl.when(opening)
     def _():
-        for r in range(MAPS):
-            bring(r).start()
-        for r in range(MAPS):
-            bring(r).wait()
+        for copy in copies:
+            copy.start()
 
     x = psel_ref[...]
     sd = x[:, M:M + 1].astype(f32)
     weight = 1.0 / (sd * sd)
     x = jnp.concatenate([x, x], axis=1)
 
-    for r in range(MAPS):
-        total = (dot(x, maps_ref[r]) * weight).astype(bf16)
-        for g in range(GROUP):
-            cols_ref[g, r * NNZ:(r + 1) * NNZ, :] = total[g * NNZ:(g + 1) * NNZ]
+    for some in (range(4), range(4, 10), range(10, MAPS)):
+        @pl.when(opening)
+        def _():
+            for r in some:
+                copies[r].wait()
+
+        for r in some:
+            total = (dot(x, maps_ref[r]) * weight).astype(bf16)
+            for g in range(GROUP):
+                cols_ref[g, r * NNZ:(r + 1) * NNZ, :] = total[g * NNZ:(g + 1) * NNZ]
 
     def gains(g, carry):
         at = pl.ds(pl.multiple_of(g * BLK, BLK), BLK)
@@ -349,7 +360,7 @@
         change_block(isel_ref, screened_ref, params_ref, out_ref, g)
 
 
-def change_kernel(half_ref, isel_ref, screened_ref, params_ref, so_far_ref, out_ref, cells_ref, new_ref, in_sems, out_sems):
+def change_kernel(half_ref, all_ref, theirs_ref, params_ref, so_far_ref, out_ref, isel_ref, screened_ref, cells_ref, new_ref, sems, in_sems, out_sems):
     blocks = screened_ref.shape[0]
     width = GROUP * BLK
     steps = blocks // GROUP
@@ -367,9 +378,18 @@
     def send(n, p):
         return pltpu.make_async_copy(new_ref.at[p, :, here(n)], out_ref.at[p, :, there(n)], out_sems.at[n, p])
 
+    at = pl.ds(pl.multiple_of(half_ref[0] * (blocks * NNZ), BLK), blocks * NNZ)
+    both = [
+        pltpu.make_async_copy(all_ref.at[:, at], isel_ref, sems.at[0]),
+        pltpu.make_async_copy(theirs_ref, screened_ref, sems.at[1]),
+    ]
+    for copy in both:
+        copy.start()
     for n in range(steps):
         for p in range(2):
             bring(n, p).start()
+    for copy in both:
+        copy.wait()
     for n in range(steps):
         for p in range(2):
             bring(n, p).wait()
@@ -385,7 +405,7 @@
 vmem = pl.BlockSpec(memory_space=pltpu.VMEM)
 smem = pl.BlockSpec(memory_space=pltpu.SMEM)
 hbm = pl.BlockSpec(memory_space=pl.ANY)
-limit = pltpu.CompilerParams(vmem_limit_bytes=56 * 1024 * 1024)
+limit = pltpu.CompilerParams(vmem_limit_bytes=62 * 1024 * 1024)
 
 
 def pack(core, predicted, perturbation, observed, obs_sd, slabs):
@@ -408,22 +428,25 @@
         out_shape=(
             jax.ShapeDtypeStruct((2 * MP, MP), bf16),
             jax.ShapeDtypeStruct((SYS - 1, 2 * MP, MP), bf16),
-            jax.ShapeDtypeStruct((blocks // 2 * NNZ, MP), bf16),
+            jax.ShapeDtypeStruct((blocks * NNZ, BLK), f32),
+            jax.ShapeDtypeStruct((2 * blocks * NNZ, BLK), f32),
         ),
         in_specs=[smem, hbm, hbm, hbm, vmem, vmem],
-        out_specs=(hbm, hbm, hbm),
+        out_specs=(hbm, hbm, hbm, hbm),
         scratch_shapes=[
             pltpu.VMEM((data, MP), bf16),
             pltpu.VMEM((3, ROWS, data), bf16),
             pltpu.VMEM((2 * data, BLK), f32),
-            pltpu.VMEM((2 * NNZ, BLK), f32),
+            pltpu.VMEM((2 * data, BLK), f32),
+            pltpu.VMEM((blocks * NNZ, BLK), f32),
+            pltpu.VMEM((2 * blocks * NNZ, BLK), f32),
             pltpu.VMEM((SYS, M, MP), f32),
             pltpu.VMEM(own.shape, bf16),
+            pltpu.VMEM(own.shape, bf16),
             pltpu.SMEM(block_map.shape, jnp.int32),
-            pltpu.SemaphoreType.DMA((PARTS + 1,)),
-            pltpu.VMEM((blocks // 2 * NNZ, MP), bf16),
+            pltpu.SemaphoreType.DMA((2 * PARTS + 1,)),
             pltpu.VMEM((SYS, 2 * MP, MP), bf16),
-            pltpu.SemaphoreType.DMA((SYS + 1,)),
+            pltpu.SemaphoreType.DMA((SYS + 2,)),
         ] + [pltpu.VMEM((M, MP), f32)] * SYS,
         compiler_params=limit,
         cost_estimate=pl.CostEstimate(flops=20_000_000_000, bytes_accessed=8_000_000, transcendentals=0),
@@ -431,25 +454,25 @@
     )(core, block_map, own, other, near, far)
 
 
-def select(half, core, block_map, own, other):
-    blocks = block_map.shape[0] // 2
-    data = own.shape[0] * BLK
+def arrange(pline, iline):
+    steps = 4
+    prows, irows = pline.shape[0] // steps, iline.shape[0] // steps
     return pl.pallas_call(
-        select_kernel,
-        out_shape=jax.ShapeDtypeStruct((MP, blocks * NNZ), bf16),
-        in_specs=[smem, smem, hbm, hbm, hbm],
-        out_specs=vmem,
-        scratch_shapes=[
-            pltpu.VMEM((2 * data, BLK), f32),
-            pltpu.VMEM((4 * NNZ, BLK), f32),
-            pltpu.VMEM(own.shape, bf16),
-            pltpu.SMEM(block_map.shape, jnp.int32),
-            pltpu.SemaphoreType.DMA((PARTS + 1,)),
-        ],
+        arrange_kernel,
+        out_shape=(
+            jax.ShapeDtypeStruct((pline.shape[0] // 2, MP), bf16),
+            jax.ShapeDtypeStruct((MP, iline.shape[0] // 2), bf16),
+        ),
+        grid=(steps,),
+        in_specs=[pl.BlockSpec((prows, BLK), lambda i: (i, 0)), pl.BlockSpec((irows, BLK), lambda i: (i, 0))],
+        out_specs=(
+            pl.BlockSpec((prows // 2, MP), lambda i: (i, 0)),
+            pl.BlockSpec((MP, irows // 2), lambda i: (0, i)),
+        ),
         compiler_params=limit,
-        cost_estimate=pl.CostEstimate(flops=8_000_000_000, bytes_accessed=8_000_000, transcendentals=0),
-        name="select",
-    )(half, core, block_map, own, other)
+        cost_estimate=pl.CostEstimate(flops=6_000_000_000, bytes_accessed=9_000_000, transcendentals=0),
+        name="arrange",
+    )(pline, iline)
 
 
 def screen(core, psel, isel, full, mine, theirs, params):
@@ -466,7 +489,7 @@
         grid_spec=pltpu.PrefetchScalarGridSpec(
             num_scalar_prefetch=1,
             grid=(steps,),
-            in_specs=[rows, pl.BlockSpec((MP, GROUP * NNZ), lambda i, c: (0, i)), hbm, hbm, hbm, cells],
+            in_specs=[rows, pl.BlockSpec((MP, GROUP * NNZ), lambda i, c: (0, c[0] * steps + i)), hbm, hbm, hbm, cells],
             out_specs=(pl.BlockSpec((GROUP, NNZ, 2 * BLK), lambda i, c: (i, 0, 0)), cells),
             scratch_shapes=[
                 pltpu.VMEM((GROUP, MAPS * NNZ, MP), bf16),
@@ -486,11 +509,14 @@
     return pl.pallas_call(
         change_kernel,
         out_shape=jax.ShapeDtypeStruct(params.shape, f32),
-        in_specs=[smem, vmem, vmem, hbm, hbm],
+        in_specs=[smem, hbm, hbm, hbm, hbm],
         out_specs=hbm,
         scratch_shapes=[
+            pltpu.VMEM((MP, blocks * NNZ), bf16),
+            pltpu.VMEM(screened.shape, bf16),
             pltpu.VMEM((2, M, blocks * BLK), bf16),
             pltpu.VMEM((2, M, blocks * BLK), f32),
+            pltpu.SemaphoreType.DMA((2,)),
             pltpu.SemaphoreType.DMA((steps, 2)),
             pltpu.SemaphoreType.DMA((steps, 2)),
         ],
@@ -515,16 +541,12 @@
     own = lax.all_to_all(whole, "slab", 0, 0)
     other = lax.ppermute(own, "boot", pair)
 
-    full, mine, psel = make_maps(core_arg, block_map, own, other, members, far_members)
-    late_map, mine = lax.optimization_barrier((block_map, mine))
+    full, mine, pline, iline = make_maps(core_arg, block_map, own, other, members, far_members)
     theirs = lax.ppermute(mine, "boot", pair)
-    isel = select(core_arg, core_arg, late_map, own, other)
-    isel, psel = lax.optimization_barrier((isel, psel))
+    psel, isel = arrange(pline, iline)
     screened, so_far = screen(core_arg, psel, isel, full, mine, theirs, params)
-    last_map, screened = lax.optimization_barrier((block_map, screened))
     screened_other = lax.ppermute(screened, "boot", pair)
-    isel_other = select(1 - core_arg, core_arg, last_map, own, other)
-    return update(1 - core_arg, isel_other, screened_other, params, so_far)
+    return update(1 - core_arg, isel, screened_other, params, so_far)
 
 
 def solution(mesh):

time: 114 us -> 109 us (0.956)
  Pallas kernels: 69.3 us -> 63.5 us
  waiting for transfers between devices: 3.68 us -> 6.31 us
  local copies, waits for them, and re-layouts: 3.55 us -> 0.97 us
    pallas_call x2 -> x1, Pallas kernels: 12.6 us -> 5.26 us  [arrange(): pl.pallas_call(arrange_kernel, out_shape=(jax.ShapeDtypeStruct((pline.sha...]
    unnamed x10 -> x6, local copies, waits for them, and re-layouts: 3.55 us -> 0.97 us
    ppermute x1, waiting for transfers between devices: 0.01 us -> 2.5 us  [on_device(): screened_other = lax.ppermute(screened, 'boot', pair)]
    pallas_call x1, Pallas kernels: 27.2 us -> 28.5 us  [make_maps(): pl.pallas_call(map_kernel, out_shape=(jax.ShapeDtypeStruct((2 * MP, MP),...]
  transfers between devices with their start and end apart: 4 -> 4, of which waited for: 2 -> 3; matrix products, arithmetic and copies ran while one was open for 0% -> 0% of each run, Pallas kernels for 13% -> 7%
where the time goes in v5:
time: 109 us; the launch traced here: 107 us
  Pallas kernels  63.5 us (58%)
  blocking collectives  32.2 us (30%)
  waiting for transfers between devices  6.31 us (6%)
  starting transfers between devices  3.96 us (4%)
    all_to_all x1, blocking collectives, on_device(): own = lax.all_to_all(whole, 'slab', 0, 0)  32.2 us
    pallas_call x1, Pallas kernels, make_maps(): pl.pallas_call(map_kernel, out_shape=(jax.ShapeDtypeStruct((2 * MP, MP),...  28.5 us
    pallas_call x1, Pallas kernels, screen(): pl.pallas_call(gain_kernel, out_shape=(jax.ShapeDtypeStruct((blocks, NNZ,...  21.9 us
    pallas_call x1, Pallas kernels, update(): pl.pallas_call(change_kernel, out_shape=jax.ShapeDtypeStruct(params.shape...  5.7 us
    pallas_call x1, Pallas kernels, arrange(): pl.pallas_call(arrange_kernel, out_shape=(jax.ShapeDtypeStruct((pline.sha...  5.26 us
    ppermute x1, waiting for transfers between devices, on_device(): other = lax.ppermute(own, 'boot', pair)  3.73 us
    ppermute x1, starting transfers between devices, on_device(): far_members = lax.ppermute(members, 'boot', far)  3.11 us
    ppermute x1, waiting for transfers between devices, on_device(): screened_other = lax.ppermute(screened, 'boot', pair)  2.5 us
  transfers between devices with their start and end apart: 4, of which 3 were waited for; matrix products, arithmetic and copies ran while one was open for 0% of the time, Pallas kernels for 7%

profile of v5, /device:TPU:0, one launch (start us, length us, event | category | flops | bytes accessed | tf_op | source)
XLA Modules:
  0.0 107.1 jit_solution(16003580126400225055)
XLA Ops:
  0.0 3.1 %collective-permute-start = (s32[4,200]{1,0:T(4,128)}, s32[4,200]{1,0:T(4,128)S(1)}, u32[]{:S(2)}, u32[]{:S(2)}) collective-permute-start(s32[4,200]{1,0:T(4,128)} %near_ref.1), channel_id=1, source_target_pairs={{0,64},{32,96},{64,0},{96,32},{1,65},{33,97},{65,1},{97,33},{2,66}... | collective-permute-start | bytes 9608 | tf_op jit(solution)/shard_map/ppermute | solution.py:538
  3.1 2.1 %pack.1 = bf16[32,208,128]{2,1,0:T(8,128)(2,1)} custom-call(s32[1]{0:T(128)} %bitcast.core_ref, bf16[200,128]{1,0:T(8,128)(2,1)} %pred_ref.1, bf16[200,128]{1,0:T(8,128)(2,1)} %pert_ref.1, bf16[1,128]{1,0:T(2,128)(2,1)} %bitcast.3, bf16[1,128]{1,0:T(2,128)(2,1)} %bitcast.4), custom_call_target="tpu_custom_call" | custom-call | tf_op jit(solution)/shard_map/pack/pallas_call | solution.py:413
  5.2 0.1 collective-permute-done.far_ref
  5.3 0.0 copy-start.2
  5.3 32.2 %all_to_all.5.own_ref = bf16[32,208,128]{2,1,0:T(8,128)(2,1)S(1)} all-to-all(bf16[32,208,128]{2,1,0:T(8,128)(2,1)} %pack.1), channel_id=1, replica_groups=mesh['boot'=4,'slab'=32] {'slab'}, dimensions={0} | all-to-all | bytes 3407872 | tf_op jit(solution)/shard_map/all_to_all | solution.py:541
  37.5 0.0 copy-start
  37.5 0.0 collective-permute-start.1
  37.5 3.7 %collective-permute-done.1.other_ref = bf16[32,208,128]{2,1,0:T(8,128)(2,1)} collective-permute-done((bf16[32,208,128]{2,1,0:T(8,128)(2,1)S(1)}, bf16[32,208,128]{2,1,0:T(8,128)(2,1)}, u32[]{:S(2)}, u32[]{:S(2)}) %collective-permute-start.1) | collective-permute-done | bytes 1703968 | tf_op jit(solution)/shard_map/ppermute | solution.py:542
  41.2 0.0 copy-done.2
  41.2 0.0 copy-done
  41.2 28.5 %maps.1 = (bf16[512,256]{1,0:T(8,128)(2,1)}, bf16[8,512,256]{2,1,0:T(8,128)(2,1)}, f32[4096,128]{1,0:T(8,128)}, f32[8192,128]{1,0:T(8,128)}) custom-call(s32[1]{0:T(128)} %bitcast.core_ref, s32[64,64]{1,0:T(8,128)} %map_ref.1, bf16[32,208,128]{2,1,0:T(8,128)(2,1)} %copy-done, bf16[32,208,128]{2,1,0:T(8,128)(2,1)} %collective-permute-done.1.other_ref, ...), custom_call_target="tpu_custom_call" | custom-call | flops 20000000000 | bytes 8000000 | tf_op jit(solution)/shard_map/maps/pallas_call | solution.py:426
  69.7 0.4 collective-permute-start.2
  70.1 5.3 %arrange.1 = (bf16[2048,256]{1,0:T(8,128)(2,1)}, bf16[256,4096]{1,0:T(8,128)(2,1)}) custom-call(f32[4096,128]{1,0:T(8,128)} %get-tuple-element.17.pline_ref, f32[8192,128]{1,0:T(8,128)} %get-tuple-element.18.iline_ref), custom_call_target="tpu_custom_call" | custom-call | flops 6000000000 | bytes 9000000 | tf_op jit(solution)/shard_map/arrange/pallas_call | solution.py:460
  75.4 0.0 collective-permute-done.2.theirs_ref
  75.4 21.9 %gains.1 = (bf16[32,64,256]{2,1,0:T(8,128)(2,1)}, f32[2,200,8192]{2,1,0:T(8,128)}) custom-call(s32[1]{0:T(128)} %bitcast.core_ref, bf16[2048,256]{1,0:T(8,128)(2,1)} %get-tuple-element.20.psel_ref, bf16[256,4096]{1,0:T(8,128)(2,1)} %get-tuple-element.19.isel_ref.all_ref, bf16[512,256]{1,0:T(8,128)(2,1)} %get-tuple-element.21.full_ref, ...), custom_call_target="tpu_custom_call" | custom-call | flops 20000000000 | bytes 16000000 | tf_op jit(solution)/shard_map/gains/pallas_call | solution.py:483
  97.3 0.4 collective-permute-start.3
  97.7 2.5 %collective-permute-done.3.theirs_ref = bf16[32,64,256]{2,1,0:T(8,128)(2,1)S(1)} collective-permute-done((bf16[32,64,256]{2,1,0:T(8,128)(2,1)}, bf16[32,64,256]{2,1,0:T(8,128)(2,1)S(1)}, u32[]{:S(2)}, u32[]{:S(2)}) %collective-permute-start.3) | collective-permute-done | bytes 1048608 | tf_op jit(solution)/shard_map/ppermute | solution.py:548
  100.2 0.0 copy-start.1
  100.2 1.0 copy-done.1
  101.2 5.7 %change.1 = f32[2,200,8192]{2,1,0:T(8,128)} custom-call(s32[1]{0:T(128)S(6)} %sub.3.half_ref, bf16[256,4096]{1,0:T(8,128)(2,1)} %get-tuple-element.19.isel_ref.all_ref, bf16[32,64,256]{2,1,0:T(8,128)(2,1)} %copy-done.1, bf16[2,200,8192]{2,1,0:T(8,128)(2,1)} %params_ref.3, f32[2,200,8192]{2,1,0:T(8,128)} %get-tuple-element.24.so_far_ref), custom_call_target="tpu_custom_call", output_to_operand_aliasing={{}: (4, {})} | custom-call | flops 5000000000 | bytes 10000000 | tf_op jit(solution)/shard_map/change/pallas_call | solution.py:509
Async XLA Ops:
  0.0 5.3 %collective-permute-start = (s32[4,200]{1,0:T(4,128)}, s32[4,200]{1,0:T(4,128)S(1)}, u32[]{:S(2)}, u32[]{:S(2)}) collective-permute-start(s32[4,200]{1,0:T(4,128)} %near_ref.1), channel_id=1, source_target_pairs={{0,64},{32,96},{64,0},{96,32},{1,65},{33,97},{65,1},{97,33},{2,66}... | collective-permute-start | bytes 9608 | tf_op jit(solution)/shard_map/ppermute | solution.py:538
  5.3 35.9 %copy-start.2 = (s32[4,200]{1,0:T(4,128)}, s32[4,200]{1,0:T(4,128)S(1)}, u32[]{:S(2)}) copy-start(s32[4,200]{1,0:T(4,128)S(1)} %collective-permute-done.far_ref) | copy-start | bytes 9604
  37.5 3.7 %copy-start = (bf16[32,208,128]{2,1,0:T(8,128)(2,1)}, bf16[32,208,128]{2,1,0:T(8,128)(2,1)S(1)}, u32[]{:S(2)}) copy-start(bf16[32,208,128]{2,1,0:T(8,128)(2,1)S(1)} %all_to_all.5.own_ref) | copy-start | bytes 5111812
  37.5 3.7 %collective-permute-start.1 = (bf16[32,208,128]{2,1,0:T(8,128)(2,1)S(1)}, bf16[32,208,128]{2,1,0:T(8,128)(2,1)}, u32[]{:S(2)}, u32[]{:S(2)}) collective-permute-start(bf16[32,208,128]{2,1,0:T(8,128)(2,1)S(1)} %all_to_all.5.own_ref), channel_id=1, source_target_pairs={{0,32},{32,0},{64,96},{96,64},{1,33},{33,1},{65,97},{97,65},{2,34}... | collective-permute-start | bytes 5111816 | tf_op jit(solution)/shard_map/ppermute | solution.py:542
  69.7 5.7 %collective-permute-start.2 = (bf16[8,512,256]{2,1,0:T(8,128)(2,1)}, bf16[8,512,256]{2,1,0:T(8,128)(2,1)}, u32[]{:S(2)}, u32[]{:S(2)}) collective-permute-start(bf16[8,512,256]{2,1,0:T(8,128)(2,1)} %get-tuple-element.22.mine_ref), channel_id=1, source_target_pairs={{0,32},{32,0},{64,96},{96,64},{1,33},{33,1},{65,97},{97,65},{2,34}... | collective-permute-start | bytes 6291464 | tf_op jit(solution)/shard_map/ppermute | solution.py:545
  97.3 3.0 %collective-permute-start.3 = (bf16[32,64,256]{2,1,0:T(8,128)(2,1)}, bf16[32,64,256]{2,1,0:T(8,128)(2,1)S(1)}, u32[]{:S(2)}, u32[]{:S(2)}) collective-permute-start(bf16[32,64,256]{2,1,0:T(8,128)(2,1)} %get-tuple-element.23), channel_id=1, source_target_pairs={{0,32},{32,0},{64,96},{96,64},{1,33},{33,1},{65,97},{97,65},{2,34}... | collective-permute-start | bytes 3145736 | tf_op jit(solution)/shard_map/ppermute | solution.py:548
  100.2 1.0 copy-start.1

commit v6 on v5

--- a/solution.py
+++ b/solution.py
@@ -153,7 +153,7 @@
         rows, low, high = chunk_rows(rows_ref, i)
         sd = rows[M:M + 1]
         at = pl.ds(pl.multiple_of(i * BLK, BLK), BLK)
-        for n, part in enumerate(split3(rows * (1.0 / (sd * sd)))):
+        for n, part in enumerate(split3(rows * (1.0 / (sd * sd)))[:2]):
             parts_ref[n, :, at] = part.astype(bf16)
         low, high = low.T, high.T
         ens_ref[at, :] = jnp.concatenate([low, high], axis=1).astype(bf16)
@@ -171,7 +171,7 @@
     wait(2 * PARTS)
 
     gram = 0.0
-    for n in (2, 1, 0):
+    for n in (1, 0):
         gram = gram + dot(parts_ref[n], ens_ref[...])
     gram = gram[:M]
 
@@ -405,7 +405,7 @@
 vmem = pl.BlockSpec(memory_space=pltpu.VMEM)
 smem = pl.BlockSpec(memory_space=pltpu.SMEM)
 hbm = pl.BlockSpec(memory_space=pl.ANY)
-limit = pltpu.CompilerParams(vmem_limit_bytes=62 * 1024 * 1024)
+limit = pltpu.CompilerParams(vmem_limit_bytes=64 * 1024 * 1024)
 
 
 def pack(core, predicted, perturbation, observed, obs_sd, slabs):
@@ -435,7 +435,7 @@
         out_specs=(hbm, hbm, hbm, hbm),
         scratch_shapes=[
             pltpu.VMEM((data, MP), bf16),
-            pltpu.VMEM((3, ROWS, data), bf16),
+            pltpu.VMEM((2, ROWS, data), bf16),
             pltpu.VMEM((2 * data, BLK), f32),
             pltpu.VMEM((2 * data, BLK), f32),
             pltpu.VMEM((blocks * NNZ, BLK), f32),
@@ -535,10 +535,10 @@
     pair = [(i, i ^ 1) for i in range(4)]
     far = [(i, i ^ 2) for i in range(4)]
 
-    far_members = lax.ppermute(members, "boot", far)
     whole = pack(core_arg, predicted, perturbation, observed, obs_sd, slabs)
-    whole, far_members = lax.optimization_barrier((whole, far_members))
     own = lax.all_to_all(whole, "slab", 0, 0)
+    own, late_members = lax.optimization_barrier((own, members))
+    far_members = lax.ppermute(late_members, "boot", far)
     other = lax.ppermute(own, "boot", pair)
 
     full, mine, pline, iline = make_maps(core_arg, block_map, own, other, members, far_members)

time: 109 us -> 108 us (level)
  waiting for transfers between devices: 6.31 us -> 5.02 us
  blocking collectives: 32.2 us -> 33.4 us
    ppermute x1, waiting for transfers between devices: 3.73 us -> 0.01 us  [on_device(): other = lax.ppermute(own, 'boot', pair)]
    ppermute x1, waiting for transfers between devices: 0.08 us -> 2.38 us  [on_device(): far_members = lax.ppermute(late_members, 'boot', far)]
    all_to_all x1, blocking collectives: 32.2 us -> 33.4 us  [on_device(): own = lax.all_to_all(whole, 'slab', 0, 0)]
  transfers between devices with their start and end apart: 4 -> 4, of which waited for: 3 -> 2; matrix products, arithmetic and copies ran while one was open for 0% -> 0% of each run, Pallas kernels for 7% -> 5%
where the time goes in v6:
time: 108 us; the launch traced here: 107 us
  Pallas kernels  62.5 us (58%)
  blocking collectives  33.4 us (31%)
  waiting for transfers between devices  5.02 us (5%)
  starting transfers between devices  3.56 us (3%)
  local copies, waits for them, and re-layouts  1.79 us (2%)
    all_to_all x1, blocking collectives, on_device(): own = lax.all_to_all(whole, 'slab', 0, 0)  33.4 us
    pallas_call x1, Pallas kernels, make_maps(): pl.pallas_call(map_kernel, out_shape=(jax.ShapeDtypeStruct((2 * MP, MP),...  27.5 us
    pallas_call x1, Pallas kernels, screen(): pl.pallas_call(gain_kernel, out_shape=(jax.ShapeDtypeStruct((blocks, NNZ,...  21.9 us
    pallas_call x1, Pallas kernels, update(): pl.pallas_call(change_kernel, out_shape=jax.ShapeDtypeStruct(params.shape...  5.7 us
    pallas_call x1, Pallas kernels, arrange(): pl.pallas_call(arrange_kernel, out_shape=(jax.ShapeDtypeStruct((pline.sha...  5.27 us
    ppermute x1, starting transfers between devices, on_device(): far_members = lax.ppermute(late_members, 'boot', far)  2.73 us
    ppermute x1, waiting for transfers between devices, on_device(): screened_other = lax.ppermute(screened, 'boot', pair)  2.63 us
    ppermute x1, waiting for transfers between devices, on_device(): far_members = lax.ppermute(late_members, 'boot', far)  2.38 us
  transfers between devices with their start and end apart: 4, of which 2 were waited for; matrix products, arithmetic and copies ran while one was open for 0% of the time, Pallas kernels for 5%

profile of v6, /device:TPU:0, one launch (start us, length us, event | category | flops | bytes accessed | tf_op | source)
XLA Modules:
  0.0 106.5 jit_solution(11595245643892771092)
XLA Ops:
  0.0 2.1 %pack.1 = bf16[32,208,128]{2,1,0:T(8,128)(2,1)} custom-call(s32[1]{0:T(128)} %bitcast.core_ref, bf16[200,128]{1,0:T(8,128)(2,1)} %pred_ref.1, bf16[200,128]{1,0:T(8,128)(2,1)} %pert_ref.1, bf16[1,128]{1,0:T(2,128)(2,1)} %bitcast.3, bf16[1,128]{1,0:T(2,128)(2,1)} %bitcast.4), custom_call_target="tpu_custom_call" | custom-call | tf_op jit(solution)/shard_map/pack/pallas_call | solution.py:413
  2.1 0.0 copy-start.1
  2.1 33.4 %all_to_all.5.own_ref = bf16[32,208,128]{2,1,0:T(8,128)(2,1)S(1)} all-to-all(bf16[32,208,128]{2,1,0:T(8,128)(2,1)} %pack.1), channel_id=1, replica_groups=mesh['boot'=4,'slab'=32] {'slab'}, dimensions={0} | all-to-all | bytes 3407872 | tf_op jit(solution)/shard_map/all_to_all | solution.py:539
  35.6 0.0 copy-start
  35.6 1.2 %copy-done = bf16[32,208,128]{2,1,0:T(8,128)(2,1)} copy-done((bf16[32,208,128]{2,1,0:T(8,128)(2,1)}, bf16[32,208,128]{2,1,0:T(8,128)(2,1)S(1)}, u32[]{:S(2)}) %copy-start) | copy-done | bytes 1703960
  36.8 0.0 collective-permute-start
  36.8 0.0 copy-done.1
  36.8 2.7 %collective-permute-start.1 = (s32[4,200]{1,0:T(4,128)S(1)}, s32[4,200]{1,0:T(4,128)S(1)}, u32[]{:S(2)}, u32[]{:S(2)}) collective-permute-start(s32[4,200]{1,0:T(4,128)S(1)} %copy-done.1), channel_id=1, source_target_pairs={{0,64},{32,96},{64,0},{96,32},{1,65},{33,97},{65,1},{97,33},{2,66}... | collective-permute-start | bytes 9608 | tf_op jit(solution)/shard_map/ppermute | solution.py:541
  39.5 2.4 %collective-permute-done.1.far_ref = s32[4,200]{1,0:T(4,128)S(1)} collective-permute-done((s32[4,200]{1,0:T(4,128)S(1)}, s32[4,200]{1,0:T(4,128)S(1)}, u32[]{:S(2)}, u32[]{:S(2)}) %collective-permute-start.1) | collective-permute-done | bytes 3232 | tf_op jit(solution)/shard_map/ppermute | solution.py:541
  41.9 0.0 copy-start.2
  41.9 0.6 copy-done.2
  42.5 0.0 collective-permute-done.other_ref
  42.5 27.5 %maps.1 = (bf16[512,256]{1,0:T(8,128)(2,1)}, bf16[8,512,256]{2,1,0:T(8,128)(2,1)}, f32[4096,128]{1,0:T(8,128)}, f32[8192,128]{1,0:T(8,128)}) custom-call(s32[1]{0:T(128)} %bitcast.core_ref, s32[64,64]{1,0:T(8,128)} %map_ref.1, bf16[32,208,128]{2,1,0:T(8,128)(2,1)} %copy-done, bf16[32,208,128]{2,1,0:T(8,128)(2,1)} %collective-permute-done.other_ref, ...), custom_call_target="tpu_custom_call" | custom-call | flops 20000000000 | bytes 8000000 | tf_op jit(solution)/shard_map/maps/pallas_call | solution.py:426
  70.0 0.3 collective-permute-start.2
  70.3 5.3 %arrange.1 = (bf16[2048,256]{1,0:T(8,128)(2,1)}, bf16[256,4096]{1,0:T(8,128)(2,1)}) custom-call(f32[4096,128]{1,0:T(8,128)} %get-tuple-element.17.pline_ref, f32[8192,128]{1,0:T(8,128)} %get-tuple-element.18.iline_ref), custom_call_target="tpu_custom_call" | custom-call | flops 6000000000 | bytes 9000000 | tf_op jit(solution)/shard_map/arrange/pallas_call | solution.py:460
  75.6 0.0 collective-permute-done.2.theirs_ref
  75.6 21.9 %gains.1 = (bf16[32,64,256]{2,1,0:T(8,128)(2,1)}, f32[2,200,8192]{2,1,0:T(8,128)}) custom-call(s32[1]{0:T(128)} %bitcast.core_ref, bf16[2048,256]{1,0:T(8,128)(2,1)} %get-tuple-element.20.psel_ref, bf16[256,4096]{1,0:T(8,128)(2,1)} %get-tuple-element.19.isel_ref.all_ref, bf16[512,256]{1,0:T(8,128)(2,1)} %get-tuple-element.21.full_ref, ...), custom_call_target="tpu_custom_call" | custom-call | flops 20000000000 | bytes 16000000 | tf_op jit(solution)/shard_map/gains/pallas_call | solution.py:483
  97.4 0.6 collective-permute-start.3
  98.0 2.6 %collective-permute-done.3.theirs_ref = bf16[32,64,256]{2,1,0:T(8,128)(2,1)} collective-permute-done((bf16[32,64,256]{2,1,0:T(8,128)(2,1)}, bf16[32,64,256]{2,1,0:T(8,128)(2,1)}, u32[]{:S(2)}, u32[]{:S(2)}) %collective-permute-start.3) | collective-permute-done | bytes 1048608 | tf_op jit(solution)/shard_map/ppermute | solution.py:548
  100.6 5.7 %change.1 = f32[2,200,8192]{2,1,0:T(8,128)} custom-call(s32[1]{0:T(128)S(6)} %sub.3.half_ref, bf16[256,4096]{1,0:T(8,128)(2,1)} %get-tuple-element.19.isel_ref.all_ref, bf16[32,64,256]{2,1,0:T(8,128)(2,1)} %collective-permute-done.3.theirs_ref, bf16[2,200,8192]{2,1,0:T(8,128)(2,1)} %params_ref.3, ...), custom_call_target="tpu_custom_call", output_to_operand_aliasing={{}: (4, {})} | custom-call | flops 5000000000 | bytes 10000000 | tf_op jit(solution)/shard_map/change/pallas_call | solution.py:509
Async XLA Ops:
  2.1 34.6 %copy-start.1 = (s32[4,200]{1,0:T(4,128)S(1)}, s32[4,200]{1,0:T(4,128)}, u32[]{:S(2)}) copy-start(s32[4,200]{1,0:T(4,128)} %near_ref.1) | copy-start | bytes 9604
  35.6 1.2 %copy-start = (bf16[32,208,128]{2,1,0:T(8,128)(2,1)}, bf16[32,208,128]{2,1,0:T(8,128)(2,1)S(1)}, u32[]{:S(2)}) copy-start(bf16[32,208,128]{2,1,0:T(8,128)(2,1)S(1)} %all_to_all.5.own_ref) | copy-start | bytes 5111812
  36.8 5.7 %collective-permute-start = (bf16[32,208,128]{2,1,0:T(8,128)(2,1)S(1)}, bf16[32,208,128]{2,1,0:T(8,128)(2,1)}, u32[]{:S(2)}, u32[]{:S(2)}) collective-permute-start(bf16[32,208,128]{2,1,0:T(8,128)(2,1)S(1)} %all_to_all.5.own_ref), channel_id=1, source_target_pairs={{0,32},{32,0},{64,96},{96,64},{1,33},{33,1},{65,97},{97,65},{2,34}... | collective-permute-start | bytes 5111816 | tf_op jit(solution)/shard_map/ppermute | solution.py:542
  36.8 5.1 %collective-permute-start.1 = (s32[4,200]{1,0:T(4,128)S(1)}, s32[4,200]{1,0:T(4,128)S(1)}, u32[]{:S(2)}, u32[]{:S(2)}) collective-permute-start(s32[4,200]{1,0:T(4,128)S(1)} %copy-done.1), channel_id=1, source_target_pairs={{0,64},{32,96},{64,0},{96,32},{1,65},{33,97},{65,1},{97,33},{2,66}... | collective-permute-start | bytes 9608 | tf_op jit(solution)/shard_map/ppermute | solution.py:541
  41.9 0.6 copy-start.2
  70.0 5.6 %collective-permute-start.2 = (bf16[8,512,256]{2,1,0:T(8,128)(2,1)}, bf16[8,512,256]{2,1,0:T(8,128)(2,1)}, u32[]{:S(2)}, u32[]{:S(2)}) collective-permute-start(bf16[8,512,256]{2,1,0:T(8,128)(2,1)} %get-tuple-element.22.mine_ref), channel_id=1, source_target_pairs={{0,32},{32,0},{64,96},{96,64},{1,33},{33,1},{65,97},{97,65},{2,34}... | collective-permute-start | bytes 6291464 | tf_op jit(solution)/shard_map/ppermute | solution.py:545
  97.4 3.2 %collective-permute-start.3 = (bf16[32,64,256]{2,1,0:T(8,128)(2,1)}, bf16[32,64,256]{2,1,0:T(8,128)(2,1)}, u32[]{:S(2)}, u32[]{:S(2)}) collective-permute-start(bf16[32,64,256]{2,1,0:T(8,128)(2,1)} %get-tuple-element.23), channel_id=1, source_target_pairs={{0,32},{32,0},{64,96},{96,64},{1,33},{33,1},{65,97},{97,65},{2,34}... | collective-permute-start | bytes 3145736 | tf_op jit(solution)/shard_map/ppermute | solution.py:548

commit v7 on v6

--- a/solution.py
+++ b/solution.py
@@ -405,7 +405,8 @@
 vmem = pl.BlockSpec(memory_space=pltpu.VMEM)
 smem = pl.BlockSpec(memory_space=pltpu.SMEM)
 hbm = pl.BlockSpec(memory_space=pl.ANY)
-limit = pltpu.CompilerParams(vmem_limit_bytes=64 * 1024 * 1024)
+limit = pltpu.CompilerParams(vmem_limit_bytes=62 * 1024 * 1024)
+whole_limit = pltpu.CompilerParams(vmem_limit_bytes=64 * 1024 * 1024)
 
 
 def pack(core, predicted, perturbation, observed, obs_sd, slabs):
@@ -521,7 +522,7 @@
             pltpu.SemaphoreType.DMA((steps, 2)),
         ],
         input_output_aliases={4: 0},
-        compiler_params=limit,
+        compiler_params=whole_limit,
         cost_estimate=pl.CostEstimate(flops=5_000_000_000, bytes_accessed=10_000_000, transcendentals=0),
         name="change",
     )(half, isel, screened, params, so_far)

time: 108 us -> 107 us (level)
  local copies, waits for them, and re-layouts: 1.79 us -> 0.59 us
    unnamed x6, local copies, waits for them, and re-layouts: 1.79 us -> 0.59 us
where the time goes in v7:
time: 107 us; the launch traced here: 105 us
  Pallas kernels  62.5 us (58%)
  blocking collectives  33.4 us (31%)
  waiting for transfers between devices  5.02 us (5%)
  starting transfers between devices  3.64 us (3%)
    all_to_all x1, blocking collectives, on_device(): own = lax.all_to_all(whole, 'slab', 0, 0)  33.4 us
    pallas_call x1, Pallas kernels, make_maps(): pl.pallas_call(map_kernel, out_shape=(jax.ShapeDtypeStruct((2 * MP, MP),...  27.5 us
    pallas_call x1, Pallas kernels, screen(): pl.pallas_call(gain_kernel, out_shape=(jax.ShapeDtypeStruct((blocks, NNZ,...  21.9 us
    pallas_call x1, Pallas kernels, update(): pl.pallas_call(change_kernel, out_shape=jax.ShapeDtypeStruct(params.shape...  5.7 us
    pallas_call x1, Pallas kernels, arrange(): pl.pallas_call(arrange_kernel, out_shape=(jax.ShapeDtypeStruct((pline.sha...  5.27 us
    ppermute x1, starting transfers between devices, on_device(): far_members = lax.ppermute(late_members, 'boot', far)  2.81 us
    ppermute x1, waiting for transfers between devices, on_device(): screened_other = lax.ppermute(screened, 'boot', pair)  2.63 us
    ppermute x1, waiting for transfers between devices, on_device(): far_members = lax.ppermute(late_members, 'boot', far)  2.38 us
  transfers between devices with their start and end apart: 4, of which 2 were waited for; matrix products, arithmetic and copies ran while one was open for 0% of the time, Pallas kernels for 5%

profile of v7, /device:TPU:0, one launch (start us, length us, event | category | flops | bytes accessed | tf_op | source)
XLA Modules:
  0.0 105.4 jit_solution(12166660302511489641)
XLA Ops:
  0.0 2.1 %pack.1 = bf16[32,208,128]{2,1,0:T(8,128)(2,1)} custom-call(s32[1]{0:T(128)} %bitcast.core_ref, bf16[200,128]{1,0:T(8,128)(2,1)} %pred_ref.1, bf16[200,128]{1,0:T(8,128)(2,1)} %pert_ref.1, bf16[1,128]{1,0:T(2,128)(2,1)} %bitcast.3, bf16[1,128]{1,0:T(2,128)(2,1)} %bitcast.4), custom_call_target="tpu_custom_call" | custom-call | tf_op jit(solution)/shard_map/pack/pallas_call | solution.py:414
  2.1 0.0 copy-start.1
  2.1 33.4 %all_to_all.5.own_ref = bf16[32,208,128]{2,1,0:T(8,128)(2,1)S(1)} all-to-all(bf16[32,208,128]{2,1,0:T(8,128)(2,1)} %pack.1), channel_id=1, replica_groups=mesh['boot'=4,'slab'=32] {'slab'}, dimensions={0} | all-to-all | bytes 3407872 | tf_op jit(solution)/shard_map/all_to_all | solution.py:540
  35.6 0.0 copy-start
  35.6 0.0 collective-permute-start
  35.6 0.0 copy-done.1
  35.6 2.8 %collective-permute-start.1 = (s32[4,200]{1,0:T(4,128)S(1)}, s32[4,200]{1,0:T(4,128)S(1)}, u32[]{:S(2)}, u32[]{:S(2)}) collective-permute-start(s32[4,200]{1,0:T(4,128)S(1)} %copy-done.1), channel_id=1, source_target_pairs={{0,64},{32,96},{64,0},{96,32},{1,65},{33,97},{65,1},{97,33},{2,66}... | collective-permute-start | bytes 9608 | tf_op jit(solution)/shard_map/ppermute | solution.py:542
  38.4 2.4 %collective-permute-done.1.far_ref = s32[4,200]{1,0:T(4,128)S(1)} collective-permute-done((s32[4,200]{1,0:T(4,128)S(1)}, s32[4,200]{1,0:T(4,128)S(1)}, u32[]{:S(2)}, u32[]{:S(2)}) %collective-permute-start.1) | collective-permute-done | bytes 3232 | tf_op jit(solution)/shard_map/ppermute | solution.py:542
  40.8 0.0 copy-start.2
  40.8 0.0 collective-permute-done.other_ref
  40.8 0.0 copy-done
  40.8 0.6 copy-done.2
  41.4 27.5 %maps.1 = (bf16[512,256]{1,0:T(8,128)(2,1)}, bf16[8,512,256]{2,1,0:T(8,128)(2,1)}, f32[4096,128]{1,0:T(8,128)}, f32[8192,128]{1,0:T(8,128)}) custom-call(s32[1]{0:T(128)} %bitcast.core_ref, s32[64,64]{1,0:T(8,128)} %map_ref.1, bf16[32,208,128]{2,1,0:T(8,128)(2,1)} %copy-done, bf16[32,208,128]{2,1,0:T(8,128)(2,1)} %collective-permute-done.other_ref, ...), custom_call_target="tpu_custom_call" | custom-call | flops 20000000000 | bytes 8000000 | tf_op jit(solution)/shard_map/maps/pallas_call | solution.py:427
  68.9 0.3 collective-permute-start.2
  69.2 5.3 %arrange.1 = (bf16[2048,256]{1,0:T(8,128)(2,1)}, bf16[256,4096]{1,0:T(8,128)(2,1)}) custom-call(f32[4096,128]{1,0:T(8,128)} %get-tuple-element.17.pline_ref, f32[8192,128]{1,0:T(8,128)} %get-tuple-element.18.iline_ref), custom_call_target="tpu_custom_call" | custom-call | flops 6000000000 | bytes 9000000 | tf_op jit(solution)/shard_map/arrange/pallas_call | solution.py:461
  74.5 0.0 collective-permute-done.2.theirs_ref
  74.5 21.9 %gains.1 = (bf16[32,64,256]{2,1,0:T(8,128)(2,1)}, f32[2,200,8192]{2,1,0:T(8,128)}) custom-call(s32[1]{0:T(128)} %bitcast.core_ref, bf16[2048,256]{1,0:T(8,128)(2,1)} %get-tuple-element.20.psel_ref, bf16[256,4096]{1,0:T(8,128)(2,1)} %get-tuple-element.19.isel_ref.all_ref, bf16[512,256]{1,0:T(8,128)(2,1)} %get-tuple-element.21.full_ref, ...), custom_call_target="tpu_custom_call" | custom-call | flops 20000000000 | bytes 16000000 | tf_op jit(solution)/shard_map/gains/pallas_call | solution.py:484
  96.3 0.6 collective-permute-start.3
  96.9 2.6 %collective-permute-done.3.theirs_ref = bf16[32,64,256]{2,1,0:T(8,128)(2,1)} collective-permute-done((bf16[32,64,256]{2,1,0:T(8,128)(2,1)}, bf16[32,64,256]{2,1,0:T(8,128)(2,1)}, u32[]{:S(2)}, u32[]{:S(2)}) %collective-permute-start.3) | collective-permute-done | bytes 1048608 | tf_op jit(solution)/shard_map/ppermute | solution.py:549
  99.5 5.7 %change.1 = f32[2,200,8192]{2,1,0:T(8,128)} custom-call(s32[1]{0:T(128)S(6)} %sub.3.half_ref, bf16[256,4096]{1,0:T(8,128)(2,1)} %get-tuple-element.19.isel_ref.all_ref, bf16[32,64,256]{2,1,0:T(8,128)(2,1)} %collective-permute-done.3.theirs_ref, bf16[2,200,8192]{2,1,0:T(8,128)(2,1)} %params_ref.3, ...), custom_call_target="tpu_custom_call", output_to_operand_aliasing={{}: (4, {})} | custom-call | flops 5000000000 | bytes 10000000 | tf_op jit(solution)/shard_map/change/pallas_call | solution.py:510
Async XLA Ops:
  2.1 33.4 %copy-start.1 = (s32[4,200]{1,0:T(4,128)S(1)}, s32[4,200]{1,0:T(4,128)}, u32[]{:S(2)}) copy-start(s32[4,200]{1,0:T(4,128)} %near_ref.1) | copy-start | bytes 9604
  35.6 5.2 %copy-start = (bf16[32,208,128]{2,1,0:T(8,128)(2,1)}, bf16[32,208,128]{2,1,0:T(8,128)(2,1)S(1)}, u32[]{:S(2)}) copy-start(bf16[32,208,128]{2,1,0:T(8,128)(2,1)S(1)} %all_to_all.5.own_ref) | copy-start | bytes 5111812
  35.6 5.2 %collective-permute-start = (bf16[32,208,128]{2,1,0:T(8,128)(2,1)S(1)}, bf16[32,208,128]{2,1,0:T(8,128)(2,1)}, u32[]{:S(2)}, u32[]{:S(2)}) collective-permute-start(bf16[32,208,128]{2,1,0:T(8,128)(2,1)S(1)} %all_to_all.5.own_ref), channel_id=1, source_target_pairs={{0,32},{32,0},{64,96},{96,64},{1,33},{33,1},{65,97},{97,65},{2,34}... | collective-permute-start | bytes 5111816 | tf_op jit(solution)/shard_map/ppermute | solution.py:543
  35.6 5.2 %collective-permute-start.1 = (s32[4,200]{1,0:T(4,128)S(1)}, s32[4,200]{1,0:T(4,128)S(1)}, u32[]{:S(2)}, u32[]{:S(2)}) collective-permute-start(s32[4,200]{1,0:T(4,128)S(1)} %copy-done.1), channel_id=1, source_target_pairs={{0,64},{32,96},{64,0},{96,32},{1,65},{33,97},{65,1},{97,33},{2,66}... | collective-permute-start | bytes 9608 | tf_op jit(solution)/shard_map/ppermute | solution.py:542
  40.8 0.6 copy-start.2
  68.9 5.6 %collective-permute-start.2 = (bf16[8,512,256]{2,1,0:T(8,128)(2,1)}, bf16[8,512,256]{2,1,0:T(8,128)(2,1)}, u32[]{:S(2)}, u32[]{:S(2)}) collective-permute-start(bf16[8,512,256]{2,1,0:T(8,128)(2,1)} %get-tuple-element.22.mine_ref), channel_id=1, source_target_pairs={{0,32},{32,0},{64,96},{96,64},{1,33},{33,1},{65,97},{97,65},{2,34}... | collective-permute-start | bytes 6291464 | tf_op jit(solution)/shard_map/ppermute | solution.py:546
  96.3 3.2 %collective-permute-start.3 = (bf16[32,64,256]{2,1,0:T(8,128)(2,1)}, bf16[32,64,256]{2,1,0:T(8,128)(2,1)}, u32[]{:S(2)}, u32[]{:S(2)}) collective-permute-start(bf16[32,64,256]{2,1,0:T(8,128)(2,1)} %get-tuple-element.23), channel_id=1, source_target_pairs={{0,32},{32,0},{64,96},{96,64},{1,33},{33,1},{65,97},{97,65},{2,34}... | collective-permute-start | bytes 3145736 | tf_op jit(solution)/shard_map/ppermute | solution.py:549

commit v8 on v7

--- a/solution.py
+++ b/solution.py
@@ -120,7 +120,7 @@
     step = count // PARTS
     for n in range(PARTS):
         wait(first + n)
-        lax.fori_loop(n * step, (n + 1) * step, chunk, 0, unroll=4)
+        lax.fori_loop(n * step, (n + 1) * step, chunk, 0, unroll=8)
 
 
 def fill_table(t_ref, i, low, high):
@@ -267,8 +267,9 @@
             wanted.append(jnp.where(plane == prow + k0, -1.0, jnp.where(inside[:PIV], 0.0, panels[s])))
         for s in range(SYS):
             lines.append(dot(inverses[s], rhs6(wanted[s])))
+        offs = [wanted[s] - dot(blocks_[s], rhs6(lines[s])) for s in range(SYS)]
         for s in range(SYS):
-            lines[s] = lines[s] + dot(inverses[s], rhs6(wanted[s] - dot(blocks_[s], rhs6(lines[s]))))
+            lines[s] = lines[s] + dot(inverses[s], rhs6(offs[s]))
         for s in range(SYS):
             hi, mid, lo = split3(panels[s])
             left = jnp.concatenate([hi, hi, hi, pad, mid, mid, lo, pad], axis=0).astype(bf16)

time: 107 us -> 106 us (level)
  Pallas kernels: 62.5 us -> 61.4 us
    pallas_call x1, Pallas kernels: 27.5 us -> 26.4 us  [make_maps(): pl.pallas_call(map_kernel, out_shape=(jax.ShapeDtypeStruct((2 * MP, MP),...]
where the time goes in v8:
time: 106 us; the launch traced here: 104 us
  Pallas kernels  61.4 us (58%)
  blocking collectives  33.4 us (32%)
  waiting for transfers between devices  5.02 us (5%)
  starting transfers between devices  3.64 us (3%)
    all_to_all x1, blocking collectives, on_device(): own = lax.all_to_all(whole, 'slab', 0, 0)  33.4 us
    pallas_call x1, Pallas kernels, make_maps(): pl.pallas_call(map_kernel, out_shape=(jax.ShapeDtypeStruct((2 * MP, MP),...  26.4 us
    pallas_call x1, Pallas kernels, screen(): pl.pallas_call(gain_kernel, out_shape=(jax.ShapeDtypeStruct((blocks, NNZ,...  21.9 us
    pallas_call x1, Pallas kernels, update(): pl.pallas_call(change_kernel, out_shape=jax.ShapeDtypeStruct(params.shape...  5.7 us
    pallas_call x1, Pallas kernels, arrange(): pl.pallas_call(arrange_kernel, out_shape=(jax.ShapeDtypeStruct((pline.sha...  5.27 us
    ppermute x1, starting transfers between devices, on_device(): far_members = lax.ppermute(late_members, 'boot', far)  2.81 us
    ppermute x1, waiting for transfers between devices, on_device(): screened_other = lax.ppermute(screened, 'boot', pair)  2.63 us
    ppermute x1, waiting for transfers between devices, on_device(): far_members = lax.ppermute(late_members, 'boot', far)  2.38 us
  transfers between devices with their start and end apart: 4, of which 2 were waited for; matrix products, arithmetic and copies ran while one was open for 0% of the time, Pallas kernels for 5%

profile of v8, /device:TPU:0, one launch (start us, length us, event | category | flops | bytes accessed | tf_op | source)
XLA Modules:
  0.0 104.2 jit_solution(18360254677036483624)
XLA Ops:
  0.0 2.1 %pack.1 = bf16[32,208,128]{2,1,0:T(8,128)(2,1)} custom-call(s32[1]{0:T(128)} %bitcast.core_ref, bf16[200,128]{1,0:T(8,128)(2,1)} %pred_ref.1, bf16[200,128]{1,0:T(8,128)(2,1)} %pert_ref.1, bf16[1,128]{1,0:T(2,128)(2,1)} %bitcast.3, bf16[1,128]{1,0:T(2,128)(2,1)} %bitcast.4), custom_call_target="tpu_custom_call" | custom-call | tf_op jit(solution)/shard_map/pack/pallas_call | solution.py:415
  2.1 0.0 copy-start.1
  2.1 33.4 %all_to_all.5.own_ref = bf16[32,208,128]{2,1,0:T(8,128)(2,1)S(1)} all-to-all(bf16[32,208,128]{2,1,0:T(8,128)(2,1)} %pack.1), channel_id=1, replica_groups=mesh['boot'=4,'slab'=32] {'slab'}, dimensions={0} | all-to-all | bytes 3407872 | tf_op jit(solution)/shard_map/all_to_all | solution.py:541
  35.6 0.0 copy-start
  35.6 0.0 collective-permute-start
  35.6 0.0 copy-done.1
  35.6 2.8 %collective-permute-start.1 = (s32[4,200]{1,0:T(4,128)S(1)}, s32[4,200]{1,0:T(4,128)S(1)}, u32[]{:S(2)}, u32[]{:S(2)}) collective-permute-start(s32[4,200]{1,0:T(4,128)S(1)} %copy-done.1), channel_id=1, source_target_pairs={{0,64},{32,96},{64,0},{96,32},{1,65},{33,97},{65,1},{97,33},{2,66}... | collective-permute-start | bytes 9608 | tf_op jit(solution)/shard_map/ppermute | solution.py:543
  38.4 2.4 %collective-permute-done.1.far_ref = s32[4,200]{1,0:T(4,128)S(1)} collective-permute-done((s32[4,200]{1,0:T(4,128)S(1)}, s32[4,200]{1,0:T(4,128)S(1)}, u32[]{:S(2)}, u32[]{:S(2)}) %collective-permute-start.1) | collective-permute-done | bytes 3232 | tf_op jit(solution)/shard_map/ppermute | solution.py:543
  40.8 0.0 copy-start.2
  40.8 0.0 collective-permute-done.other_ref
  40.8 0.0 copy-done
  40.8 0.6 copy-done.2
  41.4 26.4 %maps.1 = (bf16[512,256]{1,0:T(8,128)(2,1)}, bf16[8,512,256]{2,1,0:T(8,128)(2,1)}, f32[4096,128]{1,0:T(8,128)}, f32[8192,128]{1,0:T(8,128)}) custom-call(s32[1]{0:T(128)} %bitcast.core_ref, s32[64,64]{1,0:T(8,128)} %map_ref.1, bf16[32,208,128]{2,1,0:T(8,128)(2,1)} %copy-done, bf16[32,208,128]{2,1,0:T(8,128)(2,1)} %collective-permute-done.other_ref, ...), custom_call_target="tpu_custom_call" | custom-call | flops 20000000000 | bytes 8000000 | tf_op jit(solution)/shard_map/maps/pallas_call | solution.py:428
  67.8 0.3 collective-permute-start.2
  68.0 5.3 %arrange.1 = (bf16[2048,256]{1,0:T(8,128)(2,1)}, bf16[256,4096]{1,0:T(8,128)(2,1)}) custom-call(f32[4096,128]{1,0:T(8,128)} %get-tuple-element.17.pline_ref, f32[8192,128]{1,0:T(8,128)} %get-tuple-element.18.iline_ref), custom_call_target="tpu_custom_call" | custom-call | flops 6000000000 | bytes 9000000 | tf_op jit(solution)/shard_map/arrange/pallas_call | solution.py:462
  73.3 0.0 collective-permute-done.2.theirs_ref
  73.3 21.9 %gains.1 = (bf16[32,64,256]{2,1,0:T(8,128)(2,1)}, f32[2,200,8192]{2,1,0:T(8,128)}) custom-call(s32[1]{0:T(128)} %bitcast.core_ref, bf16[2048,256]{1,0:T(8,128)(2,1)} %get-tuple-element.20.psel_ref, bf16[256,4096]{1,0:T(8,128)(2,1)} %get-tuple-element.19.isel_ref.all_ref, bf16[512,256]{1,0:T(8,128)(2,1)} %get-tuple-element.21.full_ref, ...), custom_call_target="tpu_custom_call" | custom-call | flops 20000000000 | bytes 16000000 | tf_op jit(solution)/shard_map/gains/pallas_call | solution.py:485
  95.2 0.6 collective-permute-start.3
  95.8 2.6 %collective-permute-done.3.theirs_ref = bf16[32,64,256]{2,1,0:T(8,128)(2,1)} collective-permute-done((bf16[32,64,256]{2,1,0:T(8,128)(2,1)}, bf16[32,64,256]{2,1,0:T(8,128)(2,1)}, u32[]{:S(2)}, u32[]{:S(2)}) %collective-permute-start.3) | collective-permute-done | bytes 1048608 | tf_op jit(solution)/shard_map/ppermute | solution.py:550
  98.4 5.7 %change.1 = f32[2,200,8192]{2,1,0:T(8,128)} custom-call(s32[1]{0:T(128)S(6)} %sub.3.half_ref, bf16[256,4096]{1,0:T(8,128)(2,1)} %get-tuple-element.19.isel_ref.all_ref, bf16[32,64,256]{2,1,0:T(8,128)(2,1)} %collective-permute-done.3.theirs_ref, bf16[2,200,8192]{2,1,0:T(8,128)(2,1)} %params_ref.3, ...), custom_call_target="tpu_custom_call", output_to_operand_aliasing={{}: (4, {})} | custom-call | flops 5000000000 | bytes 10000000 | tf_op jit(solution)/shard_map/change/pallas_call | solution.py:511
Async XLA Ops:
  2.1 33.4 %copy-start.1 = (s32[4,200]{1,0:T(4,128)S(1)}, s32[4,200]{1,0:T(4,128)}, u32[]{:S(2)}) copy-start(s32[4,200]{1,0:T(4,128)} %near_ref.1) | copy-start | bytes 9604
  35.6 5.2 %copy-start = (bf16[32,208,128]{2,1,0:T(8,128)(2,1)}, bf16[32,208,128]{2,1,0:T(8,128)(2,1)S(1)}, u32[]{:S(2)}) copy-start(bf16[32,208,128]{2,1,0:T(8,128)(2,1)S(1)} %all_to_all.5.own_ref) | copy-start | bytes 5111812
  35.6 5.2 %collective-permute-start = (bf16[32,208,128]{2,1,0:T(8,128)(2,1)S(1)}, bf16[32,208,128]{2,1,0:T(8,128)(2,1)}, u32[]{:S(2)}, u32[]{:S(2)}) collective-permute-start(bf16[32,208,128]{2,1,0:T(8,128)(2,1)S(1)} %all_to_all.5.own_ref), channel_id=1, source_target_pairs={{0,32},{32,0},{64,96},{96,64},{1,33},{33,1},{65,97},{97,65},{2,34}... | collective-permute-start | bytes 5111816 | tf_op jit(solution)/shard_map/ppermute | solution.py:544
  35.6 5.2 %collective-permute-start.1 = (s32[4,200]{1,0:T(4,128)S(1)}, s32[4,200]{1,0:T(4,128)S(1)}, u32[]{:S(2)}, u32[]{:S(2)}) collective-permute-start(s32[4,200]{1,0:T(4,128)S(1)} %copy-done.1), channel_id=1, source_target_pairs={{0,64},{32,96},{64,0},{96,32},{1,65},{33,97},{65,1},{97,33},{2,66}... | collective-permute-start | bytes 9608 | tf_op jit(solution)/shard_map/ppermute | solution.py:543
  40.8 0.6 copy-start.2
  67.8 5.6 %collective-permute-start.2 = (bf16[8,512,256]{2,1,0:T(8,128)(2,1)}, bf16[8,512,256]{2,1,0:T(8,128)(2,1)}, u32[]{:S(2)}, u32[]{:S(2)}) collective-permute-start(bf16[8,512,256]{2,1,0:T(8,128)(2,1)} %get-tuple-element.22.mine_ref), channel_id=1, source_target_pairs={{0,32},{32,0},{64,96},{96,64},{1,33},{33,1},{65,97},{97,65},{2,34}... | collective-permute-start | bytes 6291464 | tf_op jit(solution)/shard_map/ppermute | solution.py:547
  95.2 3.2 %collective-permute-start.3 = (bf16[32,64,256]{2,1,0:T(8,128)(2,1)}, bf16[32,64,256]{2,1,0:T(8,128)(2,1)}, u32[]{:S(2)}, u32[]{:S(2)}) collective-permute-start(bf16[32,64,256]{2,1,0:T(8,128)(2,1)} %get-tuple-element.23), channel_id=1, source_target_pairs={{0,32},{32,0},{64,96},{96,64},{1,33},{33,1},{65,97},{97,65},{2,34}... | collective-permute-start | bytes 3145736 | tf_op jit(solution)/shard_map/ppermute | solution.py:550

commit v9 on v8

--- a/solution.py
+++ b/solution.py
@@ -281,8 +281,8 @@
     lax.fori_loop(0, M // PIV, panel_step, 0)
 
     outs = [
-        pltpu.make_async_copy(pline_ref, psel_ref, out_sems.at[SYS]),
-        pltpu.make_async_copy(iline_ref, isel_ref, out_sems.at[SYS + 1]),
+        pltpu.make_async_copy(pline_ref.at[pl.ds(0, psel_ref.shape[0])], psel_ref, out_sems.at[SYS]),
+        pltpu.make_async_copy(iline_ref.at[pl.ds(0, isel_ref.shape[0])], isel_ref, out_sems.at[SYS + 1]),
     ]
     for copy in outs:
         copy.start()
@@ -438,10 +438,10 @@
         scratch_shapes=[
             pltpu.VMEM((data, MP), bf16),
             pltpu.VMEM((2, ROWS, data), bf16),
-            pltpu.VMEM((2 * data, BLK), f32),
-            pltpu.VMEM((2 * data, BLK), f32),
-            pltpu.VMEM((blocks * NNZ, BLK), f32),
-            pltpu.VMEM((2 * blocks * NNZ, BLK), f32),
+            pltpu.VMEM((2 * data + 8, BLK), f32),
+            pltpu.VMEM((2 * data + 8, BLK), f32),
+            pltpu.VMEM((blocks * NNZ + 8, BLK), f32),
+            pltpu.VMEM((2 * blocks * NNZ + 8, BLK), f32),
             pltpu.VMEM((SYS, M, MP), f32),
             pltpu.VMEM(own.shape, bf16),
             pltpu.VMEM(own.shape, bf16),

time: 106 us -> 106 us (level)
  no operation moved by 1% of the time
where the time goes in v9:
time: 106 us; the launch traced here: 104 us
  Pallas kernels  61.4 us (58%)
  blocking collectives  33.4 us (32%)
  waiting for transfers between devices  5.02 us (5%)
  starting transfers between devices  3.64 us (3%)
    all_to_all x1, blocking collectives, on_device(): own = lax.all_to_all(whole, 'slab', 0, 0)  33.4 us
    pallas_call x1, Pallas kernels, make_maps(): pl.pallas_call(map_kernel, out_shape=(jax.ShapeDtypeStruct((2 * MP, MP),...  26.4 us
    pallas_call x1, Pallas kernels, screen(): pl.pallas_call(gain_kernel, out_shape=(jax.ShapeDtypeStruct((blocks, NNZ,...  21.9 us
    pallas_call x1, Pallas kernels, update(): pl.pallas_call(change_kernel, out_shape=jax.ShapeDtypeStruct(params.shape...  5.7 us
    pallas_call x1, Pallas kernels, arrange(): pl.pallas_call(arrange_kernel, out_shape=(jax.ShapeDtypeStruct((pline.sha...  5.27 us
    ppermute x1, starting transfers between devices, on_device(): far_members = lax.ppermute(late_members, 'boot', far)  2.81 us
    ppermute x1, waiting for transfers between devices, on_device(): screened_other = lax.ppermute(screened, 'boot', pair)  2.63 us
    ppermute x1, waiting for transfers between devices, on_device(): far_members = lax.ppermute(late_members, 'boot', far)  2.38 us
  transfers between devices with their start and end apart: 4, of which 2 were waited for; matrix products, arithmetic and copies ran while one was open for 0% of the time, Pallas kernels for 5%

profile of v9, /device:TPU:0, one launch (start us, length us, event | category | flops | bytes accessed | tf_op | source)
XLA Modules:
  0.0 104.3 jit_solution(10285431594178921449)
XLA Ops:
  0.0 2.1 %pack.1 = bf16[32,208,128]{2,1,0:T(8,128)(2,1)} custom-call(s32[1]{0:T(128)} %bitcast.core_ref, bf16[200,128]{1,0:T(8,128)(2,1)} %pred_ref.1, bf16[200,128]{1,0:T(8,128)(2,1)} %pert_ref.1, bf16[1,128]{1,0:T(2,128)(2,1)} %bitcast.3, bf16[1,128]{1,0:T(2,128)(2,1)} %bitcast.4), custom_call_target="tpu_custom_call" | custom-call | tf_op jit(solution)/shard_map/pack/pallas_call | solution.py:415
  2.1 0.0 copy-start.1
  2.1 33.4 %all_to_all.5.own_ref = bf16[32,208,128]{2,1,0:T(8,128)(2,1)S(1)} all-to-all(bf16[32,208,128]{2,1,0:T(8,128)(2,1)} %pack.1), channel_id=1, replica_groups=mesh['boot'=4,'slab'=32] {'slab'}, dimensions={0} | all-to-all | bytes 3407872 | tf_op jit(solution)/shard_map/all_to_all | solution.py:541
  35.6 0.0 copy-start
  35.6 0.0 collective-permute-start
  35.6 0.0 copy-done.1
  35.6 2.8 %collective-permute-start.1 = (s32[4,200]{1,0:T(4,128)S(1)}, s32[4,200]{1,0:T(4,128)S(1)}, u32[]{:S(2)}, u32[]{:S(2)}) collective-permute-start(s32[4,200]{1,0:T(4,128)S(1)} %copy-done.1), channel_id=1, source_target_pairs={{0,64},{32,96},{64,0},{96,32},{1,65},{33,97},{65,1},{97,33},{2,66}... | collective-permute-start | bytes 9608 | tf_op jit(solution)/shard_map/ppermute | solution.py:543
  38.4 2.4 %collective-permute-done.1.far_ref = s32[4,200]{1,0:T(4,128)S(1)} collective-permute-done((s32[4,200]{1,0:T(4,128)S(1)}, s32[4,200]{1,0:T(4,128)S(1)}, u32[]{:S(2)}, u32[]{:S(2)}) %collective-permute-start.1) | collective-permute-done | bytes 3232 | tf_op jit(solution)/shard_map/ppermute | solution.py:543
  40.8 0.0 copy-start.2
  40.8 0.0 collective-permute-done.other_ref
  40.8 0.0 copy-done
  40.8 0.6 copy-done.2
  41.4 26.4 %maps.1 = (bf16[512,256]{1,0:T(8,128)(2,1)}, bf16[8,512,256]{2,1,0:T(8,128)(2,1)}, f32[4096,128]{1,0:T(8,128)}, f32[8192,128]{1,0:T(8,128)}) custom-call(s32[1]{0:T(128)} %bitcast.core_ref, s32[64,64]{1,0:T(8,128)} %map_ref.1, bf16[32,208,128]{2,1,0:T(8,128)(2,1)} %copy-done, bf16[32,208,128]{2,1,0:T(8,128)(2,1)} %collective-permute-done.other_ref, ...), custom_call_target="tpu_custom_call" | custom-call | flops 20000000000 | bytes 8000000 | tf_op jit(solution)/shard_map/maps/pallas_call | solution.py:428
  67.8 0.3 collective-permute-start.2
  68.0 5.3 %arrange.1 = (bf16[2048,256]{1,0:T(8,128)(2,1)}, bf16[256,4096]{1,0:T(8,128)(2,1)}) custom-call(f32[4096,128]{1,0:T(8,128)} %get-tuple-element.17.pline_ref, f32[8192,128]{1,0:T(8,128)} %get-tuple-element.18.iline_ref), custom_call_target="tpu_custom_call" | custom-call | flops 6000000000 | bytes 9000000 | tf_op jit(solution)/shard_map/arrange/pallas_call | solution.py:462
  73.3 0.0 collective-permute-done.2.theirs_ref
  73.3 21.9 %gains.1 = (bf16[32,64,256]{2,1,0:T(8,128)(2,1)}, f32[2,200,8192]{2,1,0:T(8,128)}) custom-call(s32[1]{0:T(128)} %bitcast.core_ref, bf16[2048,256]{1,0:T(8,128)(2,1)} %get-tuple-element.20.psel_ref, bf16[256,4096]{1,0:T(8,128)(2,1)} %get-tuple-element.19.isel_ref.all_ref, bf16[512,256]{1,0:T(8,128)(2,1)} %get-tuple-element.21.full_ref, ...), custom_call_target="tpu_custom_call" | custom-call | flops 20000000000 | bytes 16000000 | tf_op jit(solution)/shard_map/gains/pallas_call | solution.py:485
  95.2 0.6 collective-permute-start.3
  95.8 2.6 %collective-permute-done.3.theirs_ref = bf16[32,64,256]{2,1,0:T(8,128)(2,1)} collective-permute-done((bf16[32,64,256]{2,1,0:T(8,128)(2,1)}, bf16[32,64,256]{2,1,0:T(8,128)(2,1)}, u32[]{:S(2)}, u32[]{:S(2)}) %collective-permute-start.3) | collective-permute-done | bytes 1048608 | tf_op jit(solution)/shard_map/ppermute | solution.py:550
  98.4 5.7 %change.1 = f32[2,200,8192]{2,1,0:T(8,128)} custom-call(s32[1]{0:T(128)S(6)} %sub.3.half_ref, bf16[256,4096]{1,0:T(8,128)(2,1)} %get-tuple-element.19.isel_ref.all_ref, bf16[32,64,256]{2,1,0:T(8,128)(2,1)} %collective-permute-done.3.theirs_ref, bf16[2,200,8192]{2,1,0:T(8,128)(2,1)} %params_ref.3, ...), custom_call_target="tpu_custom_call", output_to_operand_aliasing={{}: (4, {})} | custom-call | flops 5000000000 | bytes 10000000 | tf_op jit(solution)/shard_map/change/pallas_call | solution.py:511
Async XLA Ops:
  2.1 33.4 %copy-start.1 = (s32[4,200]{1,0:T(4,128)S(1)}, s32[4,200]{1,0:T(4,128)}, u32[]{:S(2)}) copy-start(s32[4,200]{1,0:T(4,128)} %near_ref.1) | copy-start | bytes 9604
  35.6 5.2 %copy-start = (bf16[32,208,128]{2,1,0:T(8,128)(2,1)}, bf16[32,208,128]{2,1,0:T(8,128)(2,1)S(1)}, u32[]{:S(2)}) copy-start(bf16[32,208,128]{2,1,0:T(8,128)(2,1)S(1)} %all_to_all.5.own_ref) | copy-start | bytes 5111812
  35.6 5.2 %collective-permute-start = (bf16[32,208,128]{2,1,0:T(8,128)(2,1)S(1)}, bf16[32,208,128]{2,1,0:T(8,128)(2,1)}, u32[]{:S(2)}, u32[]{:S(2)}) collective-permute-start(bf16[32,208,128]{2,1,0:T(8,128)(2,1)S(1)} %all_to_all.5.own_ref), channel_id=1, source_target_pairs={{0,32},{32,0},{64,96},{96,64},{1,33},{33,1},{65,97},{97,65},{2,34}... | collective-permute-start | bytes 5111816 | tf_op jit(solution)/shard_map/ppermute | solution.py:544
  35.6 5.2 %collective-permute-start.1 = (s32[4,200]{1,0:T(4,128)S(1)}, s32[4,200]{1,0:T(4,128)S(1)}, u32[]{:S(2)}, u32[]{:S(2)}) collective-permute-start(s32[4,200]{1,0:T(4,128)S(1)} %copy-done.1), channel_id=1, source_target_pairs={{0,64},{32,96},{64,0},{96,32},{1,65},{33,97},{65,1},{97,33},{2,66}... | collective-permute-start | bytes 9608 | tf_op jit(solution)/shard_map/ppermute | solution.py:543
  40.8 0.6 copy-start.2
  67.8 5.6 %collective-permute-start.2 = (bf16[8,512,256]{2,1,0:T(8,128)(2,1)}, bf16[8,512,256]{2,1,0:T(8,128)(2,1)}, u32[]{:S(2)}, u32[]{:S(2)}) collective-permute-start(bf16[8,512,256]{2,1,0:T(8,128)(2,1)} %get-tuple-element.22.mine_ref), channel_id=1, source_target_pairs={{0,32},{32,0},{64,96},{96,64},{1,33},{33,1},{65,97},{97,65},{2,34}... | collective-permute-start | bytes 6291464 | tf_op jit(solution)/shard_map/ppermute | solution.py:547
  95.2 3.2 %collective-permute-start.3 = (bf16[32,64,256]{2,1,0:T(8,128)(2,1)}, bf16[32,64,256]{2,1,0:T(8,128)(2,1)}, u32[]{:S(2)}, u32[]{:S(2)}) collective-permute-start(bf16[32,64,256]{2,1,0:T(8,128)(2,1)} %get-tuple-element.23), channel_id=1, source_target_pairs={{0,32},{32,0},{64,96},{96,64},{1,33},{33,1},{65,97},{97,65},{2,34}... | collective-permute-start | bytes 3145736 | tf_op jit(solution)/shard_map/ppermute | solution.py:550
